TPU v7x, 32 devices: a whole 2x2x4 slice. The times are simulated.
32 devices in a mesh: dp: 16 (over z, y, core), head: 2 (over x).
Axes of the slice: x: 2, y: 2, z: 4, core: 2. Of those that a mesh axis runs over, the one named last changes fastest.
Arguments:
- tokens: bfloat16 [16384, 768], P(('dp', 'head')), may hold values from -6 to 6
- w_heads: bfloat16 [768, 2304], replicated, may hold values from -0.21875 to 0.21875
- b_heads: bfloat16 [2304], replicated, may hold values from -3 to 3
- w_merge: bfloat16 [768, 768], replicated, may hold values from -3 to 3
- b_merge: bfloat16 [768], replicated, may hold values from -3 to 3
- gain_first: bfloat16 [768], replicated, may hold values from 0.25 to 1.75
- bias_first: bfloat16 [768], replicated, may hold values from -3 to 3
- w_expand: bfloat16 [768, 3072], replicated, may hold values from -0.21875 to 0.21875
- b_expand: bfloat16 [3072], replicated, may hold values from -3 to 3
- w_reduce: bfloat16 [3072, 768], replicated, may hold values from -0.109375 to 0.109375
- b_reduce: bfloat16 [768], replicated, may hold values from -3 to 3
- gain_second: bfloat16 [768], replicated, may hold values from 0.25 to 1.75
- bias_second: bfloat16 [768], replicated, may hold values from -3 to 3
- seq_lengths: int32 [16, 4], P('dp'), may hold values from 1 to 640, 896 in all within a row
- cotangent: bfloat16 [16384, 768], P(('dp', 'head')), may hold values from -6 to 6
Outputs:
- block_output: bfloat16 [16384, 768], P(('dp', 'head'))
- input_grad: float32 [16384, 768], P(('dp', 'head'))
- grad_w_heads: float32 [768, 2304], P(('dp', 'head'))
- grad_b_scores: float32 [1536], P(('dp', 'head'))
- grad_b_values: float32 [768], P(('dp', 'head'))
- grad_w_merge: float32 [768, 768], P(('dp', 'head'))
- grad_b_merge: float32 [768], P(('dp', 'head'))
- grad_gain_first: float32 [768], P(('dp', 'head'))
- grad_bias_first: float32 [768], P(('dp', 'head'))
- grad_w_expand: float32 [768, 3072], P(('dp', 'head'))
- grad_b_expand: float32 [3072], P(('dp', 'head'))
- grad_w_reduce: float32 [3072, 768], P(('dp', 'head'))
- grad_b_reduce: float32 [768], P(('dp', 'head'))
- grad_gain_second: float32 [768], P(('dp', 'head'))
- grad_bias_second: float32 [768], P(('dp', 'head'))
Inputs may be any that keep to these rules, and one draw needn't show every extreme that they name: `seq_lengths`: row g lists the lengths of the 4 sequences of token group g in order; each row sums to 896 and its largest entry is 640; the last 128 rows of each group are padding.
All inputs are finite; a program needn't handle non-finite values.
Results may differ from a plain program's by a relative error of at most 0.012.
Values may be sent and summed in bfloat16 or wider, within the bound.
No kernel may reach another device: no remote copies, remote signals or barrier semaphores. Data moves between devices by JAX's collectives and lax.ppermute only.
A program may use at most 192 MiB of HBM per device.

v0:
```python
import math

import jax
import jax.numpy as jnp
from jax import lax
from jax.sharding import PartitionSpec as P

D = 768
HEADS = 12
HEAD_DIM = 64
SPAN = 64


EXACT = lax.Precision.HIGHEST


def seq_tables(lengths, group_rows):
    seq_ends = jnp.cumsum(lengths)
    seq_starts = seq_ends - lengths
    positions = jnp.arange(group_rows, dtype=jnp.int32)
    segment = jnp.sum((positions[:, None] >= seq_ends[None, :]).astype(jnp.int32), axis=1)
    member = segment[:, None] == jnp.arange(lengths.shape[0], dtype=jnp.int32)[None, :]
    seq_len = jnp.sum(jnp.where(member, lengths[None, :], 0), axis=1)
    first_row = jnp.sum(jnp.where(member, seq_starts[None, :], 0), axis=1)
    live_mask = (segment < lengths.shape[0]).astype(jnp.float32)
    phase_angle = (
        0.5
        * math.pi
        * (positions - first_row).astype(jnp.float32)
        / jnp.maximum(seq_len, 1).astype(jnp.float32)
    )
    return (segment, jnp.cos(phase_angle) * live_mask, jnp.sin(phase_angle) * live_mask)


def layer_norm(entries, gain, bias):
    average = jnp.mean(entries, axis=-1, keepdims=True)
    centred = entries - average
    variance = jnp.mean(centred * centred, axis=-1, keepdims=True)
    return centred * lax.rsqrt(variance + 1e-05) * gain + bias


def exact_gelu(entries):
    return jax.nn.gelu(entries, approximate=False)


def row_dot(left, right):
    return lax.dot_general(
        left, right, (((0,), (0,)), ((), ())), preferred_element_type=jnp.float32
    )


def back_dot(left, right):
    return lax.dot_general(
        left, right, (((1,), (1,)), ((), ())), preferred_element_type=jnp.float32
    )


def features(projected, cos_w, sin_w):
    rectified = jax.nn.relu(projected)
    return jnp.concatenate(
        [rectified * cos_w[:, None, None], rectified * sin_w[:, None, None]], axis=-1
    )


def feature_grad(grad_low, projected, cos_w, sin_w):
    grad_wide = grad_low.astype(jnp.float32)
    half_width = grad_wide.shape[-1] // 2
    combined = (
        grad_wide[..., :half_width] * cos_w[:, None, None]
        + grad_wide[..., half_width:] * sin_w[:, None, None]
    )
    return combined * (projected > 0).astype(jnp.float32)


def advance(carried, slices):
    state_sum, norm_sum = carried
    add_state, add_norm, factor = slices
    return ((add_state + factor * state_sum, add_norm + factor * norm_sum), (state_sum, norm_sum))


def no_link(state, norm, factor):
    return (jnp.zeros_like(state), jnp.zeros_like(norm))


def block_masks(segment, blocks):
    block_seg = segment.reshape(blocks, SPAN)
    inner_pos = jnp.arange(SPAN, dtype=jnp.int32)
    causal = inner_pos[None, :] <= inner_pos[:, None]
    same_seq = block_seg[:, :, None] == block_seg[:, None, :]
    allowed = (causal[None] & same_seq).astype(jnp.float32)
    return (block_seg, allowed)


def attend_forward(head_query, head_key, head_value, segment, before_seg, linker):
    group_rows, head_count = (head_query.shape[0], head_query.shape[1])
    blocks = group_rows // SPAN
    query_blocks = head_query.reshape(blocks, SPAN, head_count, 2 * HEAD_DIM)
    key_blocks = head_key.reshape(blocks, SPAN, head_count, 2 * HEAD_DIM)
    value_blocks = head_value.reshape(blocks, SPAN, head_count, HEAD_DIM)
    block_seg, allowed = block_masks(segment, blocks)
    scores = (
        jnp.einsum("ncha,nmha->nhcm", query_blocks, key_blocks, preferred_element_type=jnp.float32)
        * allowed[:, None]
    )
    values_wide = value_blocks.astype(jnp.float32)
    local_num = jnp.einsum("nhcm,nmhe->nche", scores, values_wide, precision=EXACT)
    local_den = jnp.transpose(jnp.sum(scores, axis=3), (0, 2, 1))
    last_seg = block_seg[:, -1]
    prev_last = jnp.concatenate([jnp.reshape(before_seg, (1,)), last_seg[:-1]])
    keep_mask = (block_seg == last_seg[:, None]).astype(key_blocks.dtype)
    kept_keys = key_blocks * keep_mask[:, :, None, None]
    block_state = jnp.einsum(
        "nmha,nmhe->nhae", kept_keys, value_blocks, preferred_element_type=jnp.float32
    )
    block_norm = jnp.sum(kept_keys.astype(jnp.float32), axis=1)
    carry_on = (last_seg == prev_last).astype(jnp.float32)
    initial = (
        jnp.zeros(block_state.shape[1:], jnp.float32),
        jnp.zeros(block_norm.shape[1:], jnp.float32),
    )
    (final_state, final_norm), (prefix_state, prefix_norm) = lax.scan(
        advance, initial, (block_state, block_norm, carry_on)
    )
    pass_incl = jnp.cumprod(carry_on)
    pass_excl = jnp.concatenate([jnp.ones((1,), jnp.float32), pass_incl[:-1]])
    in_state, in_norm = linker(final_state, final_norm, pass_incl[-1])
    prefix_state = prefix_state + pass_excl[:, None, None, None] * in_state[None]
    prefix_norm = prefix_norm + pass_excl[:, None, None] * in_norm[None]
    reads_prior = (block_seg == prev_last[:, None]).astype(jnp.float32)
    query_wide = query_blocks.astype(jnp.float32) * reads_prior[:, :, None, None]
    numerator = local_num + jnp.einsum("ncha,nhae->nche", query_wide, prefix_state, precision=EXACT)
    denominator = local_den + jnp.einsum("ncha,nha->nch", query_wide, prefix_norm, precision=EXACT)
    inverse = 1.0 / (denominator + 1.0)
    output = numerator * inverse[..., None]
    return (output.reshape(group_rows, head_count, HEAD_DIM), inverse, prefix_state, prefix_norm)


def attend_backward(
    head_query,
    head_key,
    head_value,
    segment,
    before_seg,
    after_seg,
    linker,
    head_grad,
    attended,
    inverse,
    prefix_state,
    prefix_norm,
):
    group_rows, head_count = (head_query.shape[0], head_query.shape[1])
    blocks = group_rows // SPAN
    query_blocks = head_query.reshape(blocks, SPAN, head_count, 2 * HEAD_DIM)
    key_blocks = head_key.reshape(blocks, SPAN, head_count, 2 * HEAD_DIM)
    value_blocks = head_value.reshape(blocks, SPAN, head_count, HEAD_DIM)
    grad_wide = head_grad.astype(jnp.float32).reshape(blocks, SPAN, head_count, HEAD_DIM)
    out_blocks = attended.reshape(blocks, SPAN, head_count, HEAD_DIM)
    block_seg, allowed = block_masks(segment, blocks)
    weight_grad = grad_wide * inverse[..., None]
    scalar_grad = -jnp.sum(grad_wide * out_blocks, axis=3) * inverse
    scores = (
        jnp.einsum("ncha,nmha->nhcm", query_blocks, key_blocks, preferred_element_type=jnp.float32)
        * allowed[:, None]
    )
    query_wide = query_blocks.astype(jnp.float32)
    key_wide = key_blocks.astype(jnp.float32)
    values_wide = value_blocks.astype(jnp.float32)
    score_grad = jnp.einsum("nche,nmhe->nhcm", weight_grad, values_wide, precision=EXACT)
    score_grad = (score_grad + jnp.transpose(scalar_grad, (0, 2, 1))[..., None]) * allowed[:, None]
    query_grad = jnp.einsum("nhcm,nmha->ncha", score_grad, key_wide, precision=EXACT)
    key_grad = jnp.einsum("nhcm,ncha->nmha", score_grad, query_wide, precision=EXACT)
    value_grad = jnp.einsum("nhcm,nche->nmhe", scores, weight_grad, precision=EXACT)
    last_seg = block_seg[:, -1]
    prev_last = jnp.concatenate([jnp.reshape(before_seg, (1,)), last_seg[:-1]])
    reads_prior = (block_seg == prev_last[:, None]).astype(jnp.float32)
    prior_term = (
        jnp.einsum("nhae,nche->ncha", prefix_state, weight_grad, precision=EXACT)
        + prefix_norm[:, None] * scalar_grad[..., None]
    )
    query_grad = query_grad + reads_prior[:, :, None, None] * prior_term
    first_seg = block_seg[:, 0]
    next_first = jnp.concatenate([first_seg[1:], jnp.reshape(after_seg, (1,))])
    head_keep = (block_seg == first_seg[:, None]).astype(jnp.float32)
    kept_queries = query_wide * head_keep[:, :, None, None]
    block_back = jnp.einsum("ncha,nche->nhae", kept_queries, weight_grad, precision=EXACT)
    block_back_norm = jnp.einsum("ncha,nch->nha", kept_queries, scalar_grad, precision=EXACT)
    carry_back = (first_seg == next_first).astype(jnp.float32)
    initial = (
        jnp.zeros(block_back.shape[1:], jnp.float32),
        jnp.zeros(block_back_norm.shape[1:], jnp.float32),
    )
    (final_back, final_back_norm), (suffix_state, suffix_norm) = lax.scan(
        advance, initial, (block_back, block_back_norm, carry_back), reverse=True
    )
    pass_rev = jnp.cumprod(carry_back[::-1])[::-1]
    pass_excl = jnp.concatenate([pass_rev[1:], jnp.ones((1,), jnp.float32)])
    in_state, in_norm = linker(final_back, final_back_norm, pass_rev[0])
    suffix_state = suffix_state + pass_excl[:, None, None, None] * in_state[None]
    suffix_norm = suffix_norm + pass_excl[:, None, None] * in_norm[None]
    reads_later = (block_seg == next_first[:, None]).astype(jnp.float32)[:, :, None, None]
    key_grad = key_grad + reads_later * (
        jnp.einsum("nhae,nmhe->nmha", suffix_state, values_wide, precision=EXACT)
        + suffix_norm[:, None]
    )
    value_grad = value_grad + reads_later * jnp.einsum(
        "nhae,nmha->nmhe", suffix_state, key_wide, precision=EXACT
    )
    return (
        query_grad.reshape(group_rows, head_count, 2 * HEAD_DIM),
        key_grad.reshape(group_rows, head_count, 2 * HEAD_DIM),
        value_grad.reshape(group_rows, head_count, HEAD_DIM),
    )


def per_device(
    tokens,
    w_heads,
    b_heads,
    w_merge,
    b_merge,
    gain_first,
    bias_first,
    w_expand,
    b_expand,
    w_reduce,
    b_reduce,
    gain_second,
    bias_second,
    seq_lengths,
    cotangent,
):
    tok_count = tokens.shape[0]
    group_rows = lax.axis_size("head") * tok_count
    segment, cos_all, sin_all = seq_tables(seq_lengths[0], group_rows)
    offset = lax.axis_index("head") * tok_count
    own_cos = lax.dynamic_slice_in_dim(cos_all, offset, tok_count)
    own_sin = lax.dynamic_slice_in_dim(sin_all, offset, tok_count)
    no_seg = jnp.full((), -1, jnp.int32)
    projected = jnp.dot(tokens, w_heads, preferred_element_type=jnp.float32) + b_heads.astype(
        jnp.float32
    )
    queries = projected[:, :D].reshape(tok_count, HEADS, HEAD_DIM)
    keys = projected[:, D : 2 * D].reshape(tok_count, HEADS, HEAD_DIM)
    values = projected[:, 2 * D :].reshape(tok_count, HEADS, HEAD_DIM)
    query_feat = features(queries, own_cos, own_sin).astype(jnp.bfloat16)
    key_feat = features(keys, own_cos, own_sin).astype(jnp.bfloat16)
    value_low = values.astype(jnp.bfloat16)
    head_query, head_key, head_value = (
        lax.all_to_all(query_feat, "head", split_axis=1, concat_axis=0, tiled=True),
        lax.all_to_all(key_feat, "head", split_axis=1, concat_axis=0, tiled=True),
        lax.all_to_all(value_low, "head", split_axis=1, concat_axis=0, tiled=True),
    )
    attended, inverse, prefix_state, prefix_norm = attend_forward(
        head_query, head_key, head_value, segment, no_seg, no_link
    )
    mixed_low = lax.all_to_all(
        attended.astype(jnp.bfloat16), "head", split_axis=0, concat_axis=1, tiled=True
    ).reshape(tok_count, D)
    first_in = (
        tokens.astype(jnp.float32)
        + jnp.dot(mixed_low, w_merge, preferred_element_type=jnp.float32)
        + b_merge.astype(jnp.float32)
    )
    normed, first_back = jax.vjp(
        layer_norm, first_in, gain_first.astype(jnp.float32), bias_first.astype(jnp.float32)
    )
    normed_low = normed.astype(jnp.bfloat16)
    pre_act = jnp.dot(normed_low, w_expand, preferred_element_type=jnp.float32) + b_expand.astype(
        jnp.float32
    )
    activated, gelu_back = jax.vjp(exact_gelu, pre_act)
    activated_low = activated.astype(jnp.bfloat16)
    second_in = (
        normed
        + jnp.dot(activated_low, w_reduce, preferred_element_type=jnp.float32)
        + b_reduce.astype(jnp.float32)
    )
    result, second_back = jax.vjp(
        layer_norm, second_in, gain_second.astype(jnp.float32), bias_second.astype(jnp.float32)
    )
    grad_second, grad_gain_second, grad_bias_second = second_back(cotangent.astype(jnp.float32))
    branch_grad = grad_second.astype(jnp.bfloat16)
    grad_b_reduce = jnp.sum(branch_grad.astype(jnp.float32), axis=0)
    grad_w_reduce = row_dot(activated_low, branch_grad)
    (grad_pre,) = gelu_back(back_dot(branch_grad, w_reduce))
    pre_grad = grad_pre.astype(jnp.bfloat16)
    grad_b_expand = jnp.sum(pre_grad.astype(jnp.float32), axis=0)
    grad_w_expand = row_dot(normed_low, pre_grad)
    grad_normed = grad_second + back_dot(pre_grad, w_expand)
    grad_first, grad_gain_first, grad_bias_first = first_back(grad_normed)
    merge_grad = grad_first.astype(jnp.bfloat16)
    grad_b_merge = jnp.sum(merge_grad.astype(jnp.float32), axis=0)
    grad_w_merge = row_dot(mixed_low, merge_grad)
    attended_grad = (
        back_dot(merge_grad, w_merge).astype(jnp.bfloat16).reshape(tok_count, HEADS, HEAD_DIM)
    )
    head_grad = lax.all_to_all(attended_grad, "head", split_axis=1, concat_axis=0, tiled=True)
    query_grad, key_grad, value_grad = attend_backward(
        head_query,
        head_key,
        head_value,
        segment,
        no_seg,
        no_seg,
        no_link,
        head_grad,
        attended,
        inverse,
        prefix_state,
        prefix_norm,
    )
    tok_query_grad, tok_key_grad, tok_value_grad = (
        lax.all_to_all(
            query_grad.astype(jnp.bfloat16), "head", split_axis=0, concat_axis=1, tiled=True
        ),
        lax.all_to_all(
            key_grad.astype(jnp.bfloat16), "head", split_axis=0, concat_axis=1, tiled=True
        ),
        lax.all_to_all(
            value_grad.astype(jnp.bfloat16), "head", split_axis=0, concat_axis=1, tiled=True
        ),
    )
    projected_grad = jnp.concatenate(
        [
            feature_grad(tok_query_grad, queries, own_cos, own_sin).reshape(tok_count, D),
            feature_grad(tok_key_grad, keys, own_cos, own_sin).reshape(tok_count, D),
            tok_value_grad.astype(jnp.float32).reshape(tok_count, D),
        ],
        axis=1,
    ).astype(jnp.bfloat16)
    grad_b_heads = jnp.sum(projected_grad.astype(jnp.float32), axis=0)
    grad_b_scores = grad_b_heads[: 2 * D]
    grad_b_values = grad_b_heads[2 * D :]
    grad_w_heads = row_dot(tokens, projected_grad)
    input_grad = grad_first + back_dot(projected_grad, w_heads)
    summed = tuple(
        (
            lax.psum_scatter(grad_w_heads, ("dp", "head"), scatter_dimension=0, tiled=True),
            lax.psum_scatter(grad_b_scores, ("dp", "head"), scatter_dimension=0, tiled=True),
            lax.psum_scatter(grad_b_values, ("dp", "head"), scatter_dimension=0, tiled=True),
            lax.psum_scatter(grad_w_merge, ("dp", "head"), scatter_dimension=0, tiled=True),
            lax.psum_scatter(grad_b_merge, ("dp", "head"), scatter_dimension=0, tiled=True),
            lax.psum_scatter(grad_gain_first, ("dp", "head"), scatter_dimension=0, tiled=True),
            lax.psum_scatter(grad_bias_first, ("dp", "head"), scatter_dimension=0, tiled=True),
            lax.psum_scatter(grad_w_expand, ("dp", "head"), scatter_dimension=0, tiled=True),
            lax.psum_scatter(grad_b_expand, ("dp", "head"), scatter_dimension=0, tiled=True),
            lax.psum_scatter(grad_w_reduce, ("dp", "head"), scatter_dimension=0, tiled=True),
            lax.psum_scatter(grad_b_reduce, ("dp", "head"), scatter_dimension=0, tiled=True),
            lax.psum_scatter(grad_gain_second, ("dp", "head"), scatter_dimension=0, tiled=True),
            lax.psum_scatter(grad_bias_second, ("dp", "head"), scatter_dimension=0, tiled=True),
        )
    )
    return (result.astype(jnp.bfloat16), input_grad) + summed


def solution(mesh):
    in_specs = (
        P(("dp", "head"), None),
        P(),
        P(),
        P(),
        P(),
        P(),
        P(),
        P(),
        P(),
        P(),
        P(),
        P(),
        P(),
        P("dp", None),
        P(("dp", "head"), None),
    )
    out_specs = (
        P(("dp", "head"), None),
        P(("dp", "head"), None),
        P(("dp", "head"), None),
        P(("dp", "head")),
        P(("dp", "head")),
        P(("dp", "head"), None),
        P(("dp", "head")),
        P(("dp", "head")),
        P(("dp", "head")),
        P(("dp", "head"), None),
        P(("dp", "head")),
        P(("dp", "head"), None),
        P(("dp", "head")),
        P(("dp", "head")),
        P(("dp", "head")),
    )
    return jax.shard_map(
        per_device, mesh=mesh, in_specs=in_specs, out_specs=out_specs, check_vma=False
    )
```

profile of v0, /device:TPU:0, one launch (start us, length us, event | category | flops | bytes accessed | tf_op | source)
XLA Modules:
  0.0 1072.5 jit_solution(8343327839589344171)
XLA Ops:
  17.8 4.3 all-to-all-start
  22.1 3.8 slice_maximum_fusion.1
  32.6 4.2 multiply_convert_fusion.2
  40.8 4.6 all-to-all-start.2
  54.7 11.5 %all-to-all-done.2 = bf16[512,12,128]{0,2,1:T(8,128)(2,1)} async-done(((bf16[512,12,128]{0,2,1:T(8,128)(2,1)}), bf16[512,12,128]{0,2,1:T(8,128)(2,1)}, u32[]{:S(2)}, u32[]{:S(2)}) %all-to-all-start.2) | async-done | bytes 1572896 | tf_op jit(solution)/shard_map/all_to_all | solution.py:251
  66.2 4.6 all-to-all-start.1
  79.3 3.7 reshape.313
  95.4 3.7 fusion.44
  103.1 120.9 %while.38 = (s32[]{:T(128)}, f32[6,128,64]{2,1,0:T(8,128)}, f32[6,128]{1,0:T(8,128)S(1)}, f32[16,6,128,64]{3,2,1,0:T(8,128)}, f32[16,6,128]{2,1,0:T(8,128)}, /*i...) while((s32[]{:T(128)}, f32[6,128,64]{2,1,0:T(8,128)}, ...), condition=%wide.region_6.7_spmd.clone, body=%wide.region_5.6_spmd.clone.sunk | while | flops 199683 | bytes 1398942 | solution.py:121
  228.9 6.5 fusion.15
  235.5 21.7 %fusion.13 = f32[16,6,64,64]{3,2,1,0:T(8,128)S(1)} fusion(f32[16,6,128,64]{3,2,1,0:T(8,128)S(1)} %copy-done.2, f32[16]{0:T(128)S(1)} %copy-done.50, f32[16,64]{1,0:T(8,128)S(1)} %copy-done.36, bf16[16,64,6,128]{3,1,0,2:T(8,128)(2,1)S(1)} %bitcast.174), kind=kOutput, calls=%fused_computation.34 | convolution fusion | flops 606339072 | bytes 6295616 | tf_op jit(solution)/shard_map/ncha,nhae->nche/dot_general | solution.py:131
  257.3 4.0 fusion.89
  261.3 3.9 copy.363
  268.6 4.3 all-to-all-start.3
  286.7 4.2 copy.364
  295.3 19.7 %multiply_convert_fusion = (bf16[512,3072]{1,0:T(8,128)(2,1)S(1)}, f32[512,3072]{1,0:T(8,128)}, f32[512,3072]{1,0:T(8,128)}) fusion(f32[3072]{0:T(1024)S(1)} %copy-done.49, bf16[768,3072]{1,0:T(8,128)(2,1)} %param.26, f32[512,768]{1,0:T(8,128)S(1)} %get-tuple-element.559, f32[768]{0:T(1024)S(1)} %copy-done.59, f32[768]{0:T(1024)S(1)} %copy-done.47, ...), kind=kOutput, calls=%fused_computation.14 | convolution fusion | flops 2521694208 | bytes 22042624 | tf_op jit(solution)/shard_map/dot_general | solution.py:269
  321.8 9.8 convert_reduce_fusion
  331.7 5.7 multiply_reduce_fusion.2
  344.9 4.3 all-to-all-start.4
  350.9 3.6 fusion.92
  354.5 4.4 all-to-all-done.4
  362.6 4.3 reshape.323
  367.0 10.9 %fusion.29 = f32[16,6,64,64]{3,2,1,0:T(8,128)} fusion(f32[16,6,64,64]{2,3,1,0:T(8,128)} %copy-done.10, f32[16,64,6,64]{1,0,3,2:T(8,128)} %reshape.323, f32[16,64,6]{1,2,0:T(8,128)} %copy-done.24, f32[16,64,64]{1,2,0:T(8,128)} %and_convert_fusion), kind=kOutput, calls=%fused_computation.65 | convolution fusion | flops 302776320 | bytes 5005312 | tf_op jit(solution)/shard_map/nhcm,nche->nmhe/dot_general | solution.py:173
  380.1 4.6 fusion.33
  384.7 12.7 %fusion.17 = f32[16,6,128,64]{3,2,1,0:T(8,128)} fusion(f32[16,64,6,64]{1,0,3,2:T(8,128)S(1)} %copy-done.1, f32[16,64]{1,0:T(8,128)S(1)} %copy-done.39, f32[16,64,6]{1,2,0:T(8,128)S(1)} %copy-done.25, bf16[16,64,6,128]{3,1,0,2:T(8,128)(2,1)S(1)} %bitcast.175), kind=kOutput, calls=%fused_computation.43 | convolution fusion | flops 605945856 | bytes 6320128 | tf_op jit(solution)/shard_map/ncha,nche->nhae/dot_general | solution.py:186
  405.2 119.4 %while.39 = (s32[]{:T(128)}, f32[6,128,64]{2,1,0:T(8,128)}, f32[6,128]{1,0:T(8,128)S(1)}, f32[16,6,128,64]{3,2,1,0:T(8,128)}, f32[16,6,128]{2,1,0:T(8,128)}, /*i...) while((s32[]{:T(128)}, f32[6,128,64]{2,1,0:T(8,128)}, ...), condition=%wide.region_19.20_spmd.clone, body=%wide.region_18.19_spmd.clone.sunk | while | flops 199684 | bytes 1392818 | solution.py:193
  526.1 10.9 %fusion.18 = bf16[16,64,6,64]{1,3,2,0:T(8,128)(2,1)} fusion(f32[16,6,64,64]{3,2,1,0:T(8,128)} %fusion.29, f32[16,6,128,64]{3,2,1,0:T(8,128)} %get-tuple-element.221, f32[16]{0:T(128)} %maximum_multiply_fusion.1, f32[16,64]{1,0:T(8,128)S(1)} %copy-done.38, bf16[16,64,6,128]{3,1,0,2:T(8,128)(2,1)} %bitcast.179), kind=kOutput, calls=%fused_computation.47 | convolution fusion | flops 605945856 | bytes 7082048 | tf_op jit(solution)/shard_map/nhae,nmha->nmhe/dot_general | solution.py:206
  537.0 3.9 copy.365
  544.3 4.3 all-to-all-start.7
  548.6 4.5 fusion.27
  553.2 8.3 fusion.19
  564.1 4.8 all-to-all-start.6
  569.1 15.8 %fusion.11 = f32[16,6,64,128]{3,2,1,0:T(8,128)S(1)} fusion(f32[16,6,128,64]{3,2,1,0:T(8,128)} %get-tuple-element.219, f32[16]{0:T(128)S(1)} %copy-done.52, f32[16,64,6,64]{1,0,3,2:T(8,128)} %reshape.323, f32[16,64,6]{1,2,0:T(8,128)} %copy-done.24), kind=kOutput, calls=%fused_computation.32 | convolution fusion | flops 605159424 | bytes 7888960 | tf_op jit(solution)/shard_map/nhae,nche->ncha/dot_general | solution.py:178
  584.9 3.9 fusion.22
  591.8 4.8 all-to-all-start.5
  607.7 4.2 copy.366
  621.3 3.7 fusion.87
  631.4 6.4 fusion.88
  644.3 4.2 select_convert_fusion.1
  649.7 4.9 convolution_bitcast_fusion
  654.7 8.0 copy.367
  663.3 8.8 fusion.80
  672.4 8.5 fusion.93
  683.7 41.2 %all-reduce.9 = (f32[1536]{0:T(1024)}, f32[768]{0:T(1024)}, f32[768]{0:T(1024)}, f32[768]{0:T(1024)}, f32[768]{0:T(1024)}, /*index=5*/f32[3072]{0:T(1024)}, f32[768]{0:T(1024)}, f32[768]{0:T(1024)}, f32[768]{0:T(1024)}) all-reduce(f32[1536]{0:T(1024)S(1)} %slice.104, ...), channel_id=3, replica_groups=mesh['dp'=16,'head'=2] {'dp','head'}, use_global_device_ids=true, to_apply=%region_23.24.clone | all-reduce | flops 9984 | bytes 79872
  736.3 5.4 add_add_fusion.4
  741.7 40.9 %reduce-scatter.13.cloned.1.call-done = f32[24,2304]{1,0:T(8,128)} async-done(((f32[768,2304]{1,0:T(8,128)}), f32[24,2304]{1,0:T(8,128)}) %reduce-scatter.13.cloned.1.call-update) | async-done | bytes 221200
  782.6 141.4 %reduce-scatter.9.cloned.1.call-done = f32[24,3072]{1,0:T(8,128)} async-done(((f32[768,3072]{1,0:T(8,128)}), f32[24,3072]{1,0:T(8,128)}) %reduce-scatter.9.cloned.1.call-update) | async-done | bytes 294928 | tf_op jit(solution)/shard_map/reduce_scatter | solution.py:346
  924.0 141.7 %reduce-scatter.11.cloned.1.call-done = f32[96,768]{1,0:T(8,128)} async-done(((f32[3072,768]{1,0:T(8,128)}), f32[96,768]{1,0:T(8,128)}) %reduce-scatter.11.cloned.1.call-update) | async-done | bytes 294928 | tf_op jit(solution)/shard_map/reduce_scatter | solution.py:348
  (461 shorter events, 411.0 us)
Async XLA Ops:
  17.8 23.0 %all-to-all-start = ((bf16[512,12,64]{0,2,1:T(8,128)(2,1)}), bf16[512,12,64]{0,2,1:T(8,128)(2,1)}, u32[]{:S(2)}, u32[]{:S(2)}) async-start(bf16[512,12,64]{0,2,1:T(8,128)(2,1)} %bitcast.193), calls=%async_computation | async-start | bytes 1572864 | tf_op jit(solution)/shard_map/all_to_all | solution.py:252
  40.8 9.2 copy-start.58
  40.8 25.4 %all-to-all-start.2 = ((bf16[512,12,128]{0,2,1:T(8,128)(2,1)}), bf16[512,12,128]{0,2,1:T(8,128)(2,1)}, u32[]{:S(2)}, u32[]{:S(2)}) async-start(bf16[512,12,128]{0,2,1:T(8,128)(2,1)} %pad_maximum_fusion.2), calls=%async_computation.2 | async-start | bytes 3145728 | tf_op jit(solution)/shard_map/all_to_all | solution.py:251
  52.0 20.1 %copy-start.57 = (s32[16]{0:T(128)}, s32[16]{0:T(128)S(1)}, u32[]{:S(2)}) copy-start(s32[16]{0:T(128)S(1)} %get-tuple-element.471) | copy-start | bytes 196
  66.2 23.6 %all-to-all-start.1 = ((bf16[512,12,128]{0,2,1:T(8,128)(2,1)}), bf16[512,12,128]{0,2,1:T(8,128)(2,1)}, u32[]{:S(2)}, u32[]{:S(2)}) async-start(bf16[512,12,128]{0,2,1:T(8,128)(2,1)} %pad_maximum_fusion.1), calls=%async_computation.1 | async-start | bytes 3145728 | tf_op jit(solution)/shard_map/all_to_all | solution.py:250
  103.1 124.0 %copy-start.50 = (f32[16]{0:T(128)S(1)}, f32[16]{0:T(128)}, u32[]{:S(2)}) copy-start(f32[16]{0:T(128)} %maximum_multiply_fusion) | copy-start | bytes 196
  103.1 125.8 %copy-start.36 = (f32[16,64]{1,0:T(8,128)S(1)}, f32[16,64]{1,0:T(8,128)}, u32[]{:S(2)}) copy-start(f32[16,64]{1,0:T(8,128)} %get-tuple-element.546) | copy-start | bytes 12292
  224.0 11.4 %copy-start.2 = (f32[16,6,128,64]{3,2,1,0:T(8,128)S(1)}, f32[16,6,128,64]{3,2,1,0:T(8,128)}, u32[]{:S(2)}) copy-start(f32[16,6,128,64]{3,2,1,0:T(8,128)} %get-tuple-element.219) | copy-start | bytes 9437188
  224.0 11.4 %copy-start.3 = (bf16[2,512,6,128]{3,1,0,2:T(8,128)(2,1)S(1)}, bf16[2,512,6,128]{3,1,0,2:T(8,128)(2,1)}, u32[]{:S(2)}) copy-start(bf16[2,512,6,128]{3,1,0,2:T(8,128)(2,1)} %copy.287) | copy-start | bytes 4718596
  227.2 30.0 %copy-start.26 = (f32[16,6,64]{2,1,0:T(8,128)}, f32[16,6,64]{2,1,0:T(8,128)S(1)}, u32[]{:S(2)}) copy-start(f32[16,6,64]{2,1,0:T(8,128)S(1)} %get-tuple-element.554) | copy-start | bytes 73732
  227.2 30.1 %copy-start.10 = (f32[16,6,64,64]{2,3,1,0:T(8,128)}, f32[16,6,64,64]{2,3,1,0:T(8,128)S(1)}, u32[]{:S(2)}) copy-start(f32[16,6,64,64]{2,3,1,0:T(8,128)S(1)} %get-tuple-element.555) | copy-start | bytes 4718596
  235.4 21.8 %copy-start.30 = (f32[16,6,1,64]{3,2,1,0:T(1,128)}, f32[16,6,1,64]{3,2,1,0:T(1,128)S(1)}, u32[]{:S(2)}) copy-start(f32[16,6,1,64]{3,2,1,0:T(1,128)S(1)} %fusion.15) | copy-start | bytes 73732
  235.4 21.8 %copy-start.6 = (bf16[16,64,6,64]{3,1,2,0:T(8,128)(2,1)S(1)}, bf16[16,64,6,64]{3,1,2,0:T(8,128)(2,1)}, u32[]{:S(2)}) copy-start(bf16[16,64,6,64]{3,1,2,0:T(8,128)(2,1)} %copy.310) | copy-start | bytes 2359300
  235.5 21.8 %copy-start.12 = (f32[16,64,64]{1,2,0:T(8,128)S(1)}, f32[16,64,64]{1,2,0:T(8,128)}, u32[]{:S(2)}) copy-start(f32[16,64,64]{1,2,0:T(8,128)} %and_convert_fusion) | copy-start | bytes 786436
  265.2 7.7 copy-start.63
  265.2 8.3 copy-start.64
  265.2 8.9 copy-start.65
  268.6 14.7 %all-to-all-start.3 = ((bf16[2,2,98304]{2,1,0:T(2,128)(2,1)}), bf16[2,2,98304]{2,1,0:T(2,128)(2,1)}, u32[]{:S(2)}, u32[]{:S(2)}) async-start(bf16[2,2,98304]{2,1,0:T(2,128)(2,1)} %reshape.341), calls=%async_computation.3 | async-start | bytes 1572864 | tf_op jit(solution)/shard_map/all_to_all | solution.py:257
  283.3 8.8 copy-start.62
  292.2 22.8 %slice-start = ((s8[4718592]{0:T(1024)(128)(4,1)}), s8[4194304]{0:T(1024)(128)(4,1)S(1)}, s32[]{:S(2)}) async-start(s8[4718592]{0:T(1024)(128)(4,1)} %bitcast.216), calls=%async_computation.16 | async-start | bytes 8388608
  294.9 42.4 %copy-start.16 = (f32[512,768]{1,0:T(8,128)}, f32[512,768]{1,0:T(8,128)S(1)}, u32[]{:S(2)}) copy-start(f32[512,768]{1,0:T(8,128)S(1)} %get-tuple-element.559) | copy-start | bytes 4718596
  295.3 42.0 %copy-start.53 = (f32[512]{0:T(512)}, f32[512]{0:T(512)S(1)}, u32[]{:S(2)}) copy-start(f32[512]{0:T(512)S(1)} %fusion.76) | copy-start | bytes 6148
  295.3 19.7 %copy-start.61 = (f32[768]{0:T(1024)S(1)}, f32[768]{0:T(1024)}, u32[]{:S(2)}) copy-start(f32[768]{0:T(1024)} %convert_element_type.231) | copy-start | bytes 9220
  295.3 19.7 %slice-start.1 = ((s8[4718592]{0:T(1024)(128)(4,1)}), s8[524288]{0:T(1024)(128)(4,1)S(1)}, s32[]{:S(2)}) async-start(s8[4718592]{0:T(1024)(128)(4,1)} %bitcast.216), calls=%async_computation.17 | async-start | bytes 1048576
  319.4 12.3 %slice-start.2 = ((s8[4718592]{0:T(1024)(128)(4,1)}), s8[4194304]{0:T(1024)(128)(4,1)S(1)}, s32[]{:S(2)}) async-start(s8[4718592]{0:T(1024)(128)(4,1)} %bitcast.218), calls=%async_computation.18 | async-start | bytes 8388608
  321.8 9.8 copy-start.28
  321.8 9.8 slice-start.3
  340.9 8.4 copy-start.51
  344.9 14.0 %all-to-all-start.4 = ((bf16[512,12,64]{0,2,1:T(8,128)(2,1)}), bf16[512,12,64]{0,2,1:T(8,128)(2,1)}, u32[]{:S(2)}, u32[]{:S(2)}) async-start(bf16[512,12,64]{0,2,1:T(8,128)(2,1)} %bitcast.194), calls=%async_computation.4 | async-start | bytes 1572864 | tf_op jit(solution)/shard_map/all_to_all | solution.py:298
  349.3 392.4 %reduce-scatter.7.cloned.1.call-start = ((), (), s32[]{:S(2)}) async-start(), calls=%async_computation.12 | async-start | bytes 2433024 | tf_op jit(solution)/shard_map/reduce_scatter | solution.py:342
  366.9 10.9 %copy-start.1 = (f32[16,64,6,64]{1,0,3,2:T(8,128)S(1)}, f32[16,64,6,64]{1,0,3,2:T(8,128)}, u32[]{:S(2)}) copy-start(f32[16,64,6,64]{1,0,3,2:T(8,128)} %reshape.323) | copy-start | bytes 4718596
  366.9 10.9 %copy-start.14 = (f32[16,64,6,64]{1,3,2,0:T(8,128)S(1)}, f32[16,64,6,64]{1,3,2,0:T(8,128)}, u32[]{:S(2)}) copy-start(f32[16,64,6,64]{1,3,2,0:T(8,128)} %get-tuple-element.557) | copy-start | bytes 4718596
  379.4 18.0 %copy-start.34 = (f32[16,64,6]{1,2,0:T(8,128)}, f32[16,64,6]{1,2,0:T(8,128)S(1)}, u32[]{:S(2)}) copy-start(f32[16,64,6]{1,2,0:T(8,128)S(1)} %negate_multiply_fusion.1) | copy-start | bytes 73732
  405.2 120.9 %copy-start.38 = (f32[16,64]{1,0:T(8,128)S(1)}, f32[16,64]{1,0:T(8,128)}, u32[]{:S(2)}) copy-start(f32[16,64]{1,0:T(8,128)} %get-tuple-element.545) | copy-start | bytes 12292
  544.3 19.9 %all-to-all-start.7 = ((bf16[2,2,98304]{2,1,0:T(2,128)(2,1)}), bf16[2,2,98304]{2,1,0:T(2,128)(2,1)}, u32[]{:S(2)}, u32[]{:S(2)}) async-start(bf16[2,2,98304]{2,1,0:T(2,128)(2,1)} %reshape.343), calls=%async_computation.7 | async-start | bytes 1572864 | tf_op jit(solution)/shard_map/all_to_all | solution.py:320
  561.7 7.3 copy-start.52
  564.1 27.6 %all-to-all-start.6 = ((bf16[1024,6,128]{2,1,0:T(8,128)(2,1)}), bf16[1024,6,128]{2,1,0:T(8,128)(2,1)}, u32[]{:S(2)}, u32[]{:S(2)}) async-start(bf16[1024,6,128]{2,1,0:T(8,128)(2,1)} %copy.330), calls=%async_computation.6 | async-start | bytes 4194304 | tf_op jit(solution)/shard_map/all_to_all | solution.py:317
  569.0 15.9 %copy-start.9 = (bf16[2,512,6,128]{3,1,0,2:T(8,128)(2,1)S(1)}, bf16[2,512,6,128]{3,1,0,2:T(8,128)(2,1)}, u32[]{:S(2)}) copy-start(bf16[2,512,6,128]{3,1,0,2:T(8,128)(2,1)} %copy.290) | copy-start | bytes 4718596
  569.0 15.8 %copy-start.11 = (f32[16,6,64,64]{2,3,1,0:T(8,128)S(1)}, f32[16,6,64,64]{2,3,1,0:T(8,128)}, u32[]{:S(2)}) copy-start(f32[16,6,64,64]{2,3,1,0:T(8,128)} %fusion.33) | copy-start | bytes 4718596
  569.0 15.8 %copy-start.13 = (f32[16,64,64]{1,2,0:T(8,128)S(1)}, f32[16,64,64]{1,2,0:T(8,128)}, u32[]{:S(2)}) copy-start(f32[16,64,64]{1,2,0:T(8,128)} %and_convert_fusion) | copy-start | bytes 786436
  569.0 15.8 %copy-start.29 = (f32[16,6,64]{2,1,0:T(8,128)S(1)}, f32[16,6,64]{2,1,0:T(8,128)}, u32[]{:S(2)}) copy-start(f32[16,6,64]{2,1,0:T(8,128)} %bitcast_multiply_fusion.1) | copy-start | bytes 73732
  569.0 15.8 %copy-start.32 = (f32[16,6,128]{2,1,0:T(8,128)S(1)}, f32[16,6,128]{2,1,0:T(8,128)}, u32[]{:S(2)}) copy-start(f32[16,6,128]{2,1,0:T(8,128)} %broadcast_add_fusion.1) | copy-start | bytes 147460
  569.1 15.8 %copy-start.35 = (f32[16,64,6]{1,2,0:T(8,128)S(1)}, f32[16,64,6]{1,2,0:T(8,128)}, u32[]{:S(2)}) copy-start(f32[16,64,6]{1,2,0:T(8,128)} %copy-done.34) | copy-start | bytes 73732
  569.1 15.8 %copy-start.37 = (f32[16,64]{1,0:T(8,128)S(1)}, f32[16,64]{1,0:T(8,128)}, u32[]{:S(2)}) copy-start(f32[16,64]{1,0:T(8,128)} %get-tuple-element.546) | copy-start | bytes 12292
  591.8 27.3 %all-to-all-start.5 = ((bf16[1024,6,128]{2,1,0:T(8,128)(2,1)}), bf16[1024,6,128]{2,1,0:T(8,128)(2,1)}, u32[]{:S(2)}, u32[]{:S(2)}) async-start(bf16[1024,6,128]{2,1,0:T(8,128)(2,1)} %copy.318), calls=%async_computation.5 | async-start | bytes 4194304 | tf_op jit(solution)/shard_map/all_to_all | solution.py:314
  596.6 186.0 %reduce-scatter.13.cloned.1.call-start = ((), (), s32[]{:S(2)}) async-start(), calls=%async_computation.15 | async-start | bytes 7299072
  662.7 261.4 %reduce-scatter.9.cloned.1.call-start = ((), (), s32[]{:S(2)}) async-start(), calls=%async_computation.13 | async-start | bytes 9732096 | tf_op jit(solution)/shard_map/reduce_scatter | solution.py:346
  672.2 393.5 %reduce-scatter.11.cloned.1.call-start = ((), (), s32[]{:S(2)}) async-start(), calls=%async_computation.14 | async-start | bytes 9732096 | tf_op jit(solution)/shard_map/reduce_scatter | solution.py:348
  (38 other events, 112.2 us)
Sparse Core Ops, SparseCore 0:
  356.0 100.6 reduce-scatter.6
  662.8 119.7 reduce-scatter.12
  789.1 134.9 reduce-scatter.8
  931.4 134.3 reduce-scatter.10
where the time goes:
time: 1080 us; the launch traced here: 1070 us
  waiting for transfers between devices  343 us (32%)
  other arithmetic  247 us (23%)
  local copies, waits for them, and re-layouts  199 us (18%)
  matrix products  191 us (18%)
  blocking collectives  41.2 us (4%)
  starting transfers between devices  36.5 us (3%)
  between operations  15 us (1%)
    reduce_scatter x1, waiting for transfers between devices, per_device(): lax.psum_scatter(grad_w_reduce, ('dp', 'head'), scatter_dimension=0, tile...  142 us
    reduce_scatter x1, waiting for transfers between devices, per_device(): lax.psum_scatter(grad_w_expand, ('dp', 'head'), scatter_dimension=0, tile...  141 us
    add x32, other arithmetic, advance(): add_state + factor * state_sum  82.1 us
    dynamic_update_slice x64, other arithmetic, attend_forward(): lax.scan(advance, initial, (block_state, block_norm, carry_on))  74.2 us
    unnamed x166, local copies, waits for them, and re-layouts  53.4 us
    dynamic_slice x48, local copies, waits for them, and re-layouts, attend_forward(): lax.scan(advance, initial, (block_state, block_norm, carry_on))  51.5 us
    unnamed x1, blocking collectives  41.2 us
    unnamed x5, waiting for transfers between devices  41 us
  transfers between devices with their start and end apart: 12, of which 8 were waited for; matrix products, arithmetic and copies ran while one was open for 36% of the time, Pallas kernels for 0%

commit v1 on v0

v1 whole, which is shorter than its diff:
```python
import functools
import math

import jax
import jax.numpy as jnp
from jax import lax
from jax.experimental import pallas as pl
from jax.experimental.pallas import tpu as pltpu
from jax.sharding import PartitionSpec as P

D = 768
PAIRS = 6
FF = 3072
LANES = 128
HALF = 64
BF = jnp.bfloat16
F32 = jnp.float32
AXES = ("dp", "head")
VMEM_LIMIT = 48 * 1024 * 1024
FF_BLOCK = 512
FF_STEPS = FF // FF_BLOCK


def dot(a, b):
    return jnp.dot(a, b, preferred_element_type=F32)


def dot_t(a, b):
    return lax.dot_general(a, b, (((0,), (0,)), ((), ())), preferred_element_type=F32)


def dot_r(a, b):
    return lax.dot_general(a, b, (((1,), (1,)), ((), ())), preferred_element_type=F32)


def call(kernel, name, scal, grid, ins, outs, scratch=(), flops=0, vmem=VMEM_LIMIT):
    whole = lambda n: (lambda *_: (0,) * n)
    in_specs = [
        pl.BlockSpec(b if b is not None else a.shape, m if m is not None else whole(a.ndim))
        for a, b, m in ins
    ]
    out_specs = [
        pl.BlockSpec(b if b is not None else s, m if m is not None else whole(len(s)))
        for s, d, b, m in outs
    ]
    nbytes = sum(a.size * a.dtype.itemsize for a, _, _ in ins)
    nbytes += sum(math.prod(s) * jnp.dtype(d).itemsize for s, d, _, _ in outs)
    return pl.pallas_call(
        kernel,
        name=name,
        grid_spec=pltpu.PrefetchScalarGridSpec(
            num_scalar_prefetch=1,
            grid=grid,
            in_specs=in_specs,
            out_specs=out_specs,
            scratch_shapes=list(scratch),
        ),
        out_shape=[jax.ShapeDtypeStruct(s, d) for s, d, _, _ in outs],
        compiler_params=pltpu.CompilerParams(vmem_limit_bytes=vmem),
        cost_estimate=pl.CostEstimate(flops=int(flops), bytes_accessed=int(nbytes), transcendentals=0),
    )(scal, *[a for a, _, _ in ins])


def lane_masks():
    lane = lax.broadcasted_iota(jnp.int32, (1, LANES), 1)
    even = (lane < HALF).astype(F32)
    return lane, even, even.astype(BF), (1.0 - even).astype(BF)


def square_masks():
    row = lax.broadcasted_iota(jnp.int32, (LANES, LANES), 0)
    lane = lax.broadcasted_iota(jnp.int32, (LANES, LANES), 1)
    upper = row < HALF
    return lane, upper, upper == (lane < HALF)


def high_low(v):
    high = v.astype(BF).astype(F32)
    return high, v - high


def tables(scal, rows, seqs, tcol, trow):
    pos = lax.broadcasted_iota(jnp.int32, (1, rows), 1) + scal[seqs] * rows
    seg = jnp.zeros((1, rows), jnp.int32)
    first = jnp.zeros((1, rows), jnp.int32)
    length = jnp.ones((1, rows), jnp.int32)
    at_boundary = jnp.int32(0)
    begin = jnp.int32(0)
    for s in range(seqs):
        end = begin + scal[s]
        inside = (pos >= begin) & (pos < end)
        first = jnp.where(inside, begin, first)
        length = jnp.where(inside, jnp.maximum(scal[s], 1), length)
        seg = seg + (pos >= end).astype(jnp.int32)
        at_boundary = at_boundary + (rows - 1 >= end).astype(jnp.int32)
        begin = end
    live = (seg < seqs).astype(F32)
    angle = 0.5 * math.pi * (pos - first).astype(F32) / length.astype(F32)
    cos_w = jnp.cos(angle) * live
    sin_w = jnp.sin(angle) * live
    crossing = (seg == at_boundary).astype(F32)
    which = lax.broadcasted_iota(jnp.int32, (LANES, rows), 0)
    table = jnp.zeros((LANES, rows), F32)
    for n, entry in enumerate((cos_w, sin_w, seg.astype(F32), cos_w * crossing, sin_w * crossing)):
        table = jnp.where(which == n, entry, table)
    trow[...] = table[:8]
    tcol[...] = table.T


def pack_state(total_cos, total_sin, norm_cos, norm_sin, pair, norms):
    lane, upper, diag = square_masks()
    packed = jnp.where(diag, total_cos, pltpu.roll(total_sin, HALF, 1))
    cos_high, cos_low = high_low(norm_cos)
    sin_high, sin_low = high_low(norm_sin)
    for n, part in enumerate((cos_high, cos_low, sin_high, sin_low)):
        norms = jnp.where(lane == 4 * pair + n, part, norms)
    return packed.astype(BF), norms


def unpack_state(state_ref, pair):
    lane, upper, diag = square_masks()
    packed = state_ref[pair].astype(F32)
    norms = state_ref[PAIRS].astype(F32)
    of_cos = jnp.where(diag, packed, 0.0)
    of_sin = jnp.where(diag, pltpu.roll(packed, HALF, 1), 0.0)
    pick = lambda n: jnp.sum(
        jnp.where((lane == 4 * pair + n) | (lane == 4 * pair + n + 1), norms, 0.0), axis=1, keepdims=True
    )
    return of_cos, of_sin, pick(0), pick(2)


def kv_kernel(seqs, scal, tok, wk, wv, bk, bv, rk_o, v_o, st_o, tcol, trow, norms):
    step = pl.program_id(0)
    rows = tok.shape[0]

    @pl.when(step == 0)
    def _():
        tables(scal, rows, seqs, tcol, trow)
        norms[...] = jnp.zeros_like(norms)

    rk = jnp.maximum(dot(tok[...], wk[...]) + bk[...].astype(F32), 0.0).astype(BF)
    v = (dot(tok[...], wv[...]) + bv[...].astype(F32)).astype(BF)
    rk_o[...] = rk
    v_o[...] = v
    cos_b, sin_b = tcol[:, 3:4], tcol[:, 4:5]
    lane, even, even_b, odd_b = lane_masks()
    sq_lane, upper, diag = square_masks()
    for n in range(2):
        pair = 2 * step + n
        kp = rk[:, n * LANES : (n + 1) * LANES].astype(F32)
        vp = v[:, n * LANES : (n + 1) * LANES]
        left = jnp.concatenate([(kp * cos_b).astype(BF), (kp * sin_b).astype(BF)], axis=1)
        right = jnp.concatenate([vp * even_b + odd_b, vp * odd_b + even_b], axis=1)
        both = dot_t(left, right)
        of_cos = jnp.where(upper, both[:LANES, :LANES], both[:LANES, LANES:])
        of_sin = jnp.where(upper, both[LANES:, :LANES], both[LANES:, LANES:])
        norm_cos = jnp.where(diag, pltpu.roll(of_cos, HALF, 1), of_cos)
        norm_sin = jnp.where(diag, pltpu.roll(of_sin, HALF, 1), of_sin)
        packed, new_norms = pack_state(of_cos, of_sin, norm_cos, norm_sin, pair, norms[...])
        st_o[pair] = packed
        norms[...] = new_norms

    st_o[PAIRS] = norms[...].astype(BF)


def weights_block(tcol, trow, transposed):
    rows = tcol.shape[0]
    down = lax.broadcasted_iota(jnp.int32, (rows, rows), 0)
    along = lax.broadcasted_iota(jnp.int32, (rows, rows), 1)
    same = tcol[:, 2:3] == trow[2:3, :]
    causal = (down <= along) if transposed else (along <= down)
    value = tcol[:, 0:1] * trow[0:1, :] + tcol[:, 1:2] * trow[1:2, :]
    return jnp.where(same & causal, value, 0.0)


def local_kernel(scal, tok, wq, bq, rk, v, tcol, trow, rq_o, num_o, den_o, weights):
    step = pl.program_id(0)
    rows = tok.shape[0]
    mid = rows // 2

    @pl.when(step == 0)
    def _():
        weights[...] = weights_block(tcol, trow, False)

    rq = jnp.maximum(dot(tok[...], wq[...]) + bq[...].astype(F32), 0.0).astype(BF)
    rq_o[...] = rq
    lane, even, even_b, odd_b = lane_masks()
    is_even = lane < HALF
    for n in range(2):
        cols = slice(n * LANES, (n + 1) * LANES)
        qp, kp, vp = rq[:, cols], rk[:, cols], v[:, cols]
        for lo, hi in ((0, mid), (mid, rows)):
            outs = []
            for own, other in ((even_b, odd_b), (odd_b, even_b)):
                scores = dot_r(qp[lo:hi] * own, kp[:hi]) * weights[lo:hi, :hi]
                outs.append(dot(scores.astype(BF), vp[:hi] * own + other))
            num_o[lo:hi, cols] = jnp.where(is_even, outs[0], outs[1])
            den_o[lo:hi, cols] = pltpu.roll(jnp.where(is_even, outs[1], outs[0]), HALF, 1)


def normalise(entries):
    mean = jnp.mean(entries, axis=1, keepdims=True)
    centred = entries - mean
    var = jnp.mean(centred * centred, axis=1, keepdims=True)
    scale = lax.rsqrt(var + 1e-05)
    return centred * scale, scale


def ffn_kernel(
    scal, rq, num, den, st, tcol, tok, w_merge, b_merge, gain, bias, w_exp, b_exp, w_red, b_red,
    att_o, inv_o, mixed_o, xhat_o, scale_o, normed_o, act_o, slope_o, second_o,
    acc, head_at,
):
    step = pl.program_id(0)

    @pl.when(step == 0)
    def _():
        cross = (scal[head_at] == 1).astype(F32)
        cos_b, sin_b = tcol[:, 3:4] * cross, tcol[:, 4:5] * cross
        sq_lane, upper, diag = square_masks()
        for pair in range(PAIRS):
            cols = slice(pair * LANES, (pair + 1) * LANES)
            qp = rq[:, cols].astype(F32)
            of_cos, of_sin, norm_cos, norm_sin = unpack_state(st, pair)
            top = jnp.concatenate([of_cos, jnp.where(diag, norm_cos, 0.0)], axis=1)
            low = jnp.concatenate([of_sin, jnp.where(diag, norm_sin, 0.0)], axis=1)
            right = jnp.concatenate([top, low], axis=0).astype(BF)
            left = jnp.concatenate([(qp * cos_b).astype(BF), (qp * sin_b).astype(BF)], axis=1)
            prior = dot(left, right)
            inverse = 1.0 / (den[:, cols] + prior[:, LANES:] + 1.0)
            attended = (num[:, cols] + prior[:, :LANES]) * inverse
            att_o[:, cols] = attended
            inv_o[:, cols] = inverse
            mixed_o[:, cols] = attended.astype(BF)
        first_in = tok[...].astype(F32) + dot(mixed_o[...], w_merge[...]) + b_merge[...].astype(F32)
        xhat, scale = normalise(first_in)
        normed = xhat * gain[...].astype(F32) + bias[...].astype(F32)
        xhat_o[...] = xhat
        scale_o[...] = jnp.broadcast_to(scale, scale_o.shape)
        normed_o[...] = normed.astype(BF)
        acc[...] = normed + b_red[...].astype(F32)

    pre = dot(normed_o[...], w_exp[...]) + b_exp[...].astype(F32)
    cdf = 0.5 + 0.5 * lax.erf(pre * (2.0**-0.5))
    pdf = jnp.exp(-0.5 * pre * pre) * (1.0 / math.sqrt(2.0 * math.pi))
    act = (pre * cdf).astype(BF)
    act_o[...] = act
    slope_o[...] = (cdf + pre * pdf).astype(BF)
    acc[...] += dot(act, w_red[...])

    @pl.when(step == pl.num_programs(0) - 1)
    def _():
        second_o[...] = acc[...]


def second_kernel(core_at, scal, second, cot, gain, bias, out_o, grad_o, full_o, keep_o, send_o, sums_o):
    xhat, scale = normalise(second[...])
    gain_w = gain[...].astype(F32)
    out_o[...] = (xhat * gain_w + bias[...].astype(F32)).astype(BF)
    cot_w = cot[...].astype(F32)
    t = cot_w * gain_w
    grad = scale * (
        t - jnp.mean(t, axis=1, keepdims=True) - xhat * jnp.mean(t * xhat, axis=1, keepdims=True)
    )
    low = grad.astype(BF)
    grad_o[...] = grad
    full_o[...] = low
    first = scal[core_at] == 0
    half = D // 2
    left, right = grad[:, :half], grad[:, half:]
    keep_o[...] = jnp.where(first, left, right).astype(BF)
    send_o[...] = jnp.where(first, right, left).astype(BF)
    sums_o[0:1] = jnp.sum(cot_w * xhat, axis=0, keepdims=True)
    sums_o[1:2] = jnp.sum(cot_w, axis=0, keepdims=True)
    sums_o[2:3] = jnp.sum(low.astype(F32), axis=0, keepdims=True)


def back_kernel(
    core_at, scal, full, slope, w_exp, w_red, grad2, gain, xhat, scale, w_merge, att, inv, rq, tcol,
    pk_o, ps_o, first_o, mk_o, ms_o, we_o, wo_o, st_o, bexp_o, sums_o,
    acc,
):
    step = pl.program_id(0)
    steps = pl.num_programs(0)

    @pl.when(step == 0)
    def _():
        acc[...] = grad2[...]

    pre_grad = (dot_r(full[...], w_red[...]) * slope[...].astype(F32)).astype(BF)
    bexp_o[...] = jnp.sum(pre_grad.astype(F32), axis=0, keepdims=True)
    half = steps // 2
    mine = (step >= half) == (scal[core_at] == 1)
    slot = lax.rem(step, half)

    @pl.when(mine)
    def _():
        pk_o[slot] = pre_grad

    @pl.when(jnp.logical_not(mine))
    def _():
        ps_o[slot] = pre_grad

    acc[...] += dot_r(pre_grad, w_exp[...])

    @pl.when(step == steps - 1)
    def _():
        grad_normed = acc[...]
        xh = xhat[...]
        t = grad_normed * gain[...].astype(F32)
        first = scale[:, 0:1] * (
            t - jnp.mean(t, axis=1, keepdims=True) - xh * jnp.mean(t * xh, axis=1, keepdims=True)
        )
        low = first.astype(BF)
        first_o[...] = first
        sums_o[0:1] = jnp.sum(grad_normed * xh, axis=0, keepdims=True)
        sums_o[1:2] = jnp.sum(grad_normed, axis=0, keepdims=True)
        sums_o[2:3] = jnp.sum(low.astype(F32), axis=0, keepdims=True)
        is_first = scal[core_at] == 0
        left, right = first[:, : D // 2], first[:, D // 2 :]
        mk_o[...] = jnp.where(is_first, left, right).astype(BF)
        ms_o[...] = jnp.where(is_first, right, left).astype(BF)
        cos_b, sin_b = tcol[:, 3:4], tcol[:, 4:5]
        lane, even, even_b, odd_b = lane_masks()
        is_even = lane < HALF
        sq_lane, upper, diag = square_masks()
        across = jnp.where(diag, 0.0, 1.0).astype(BF)
        norms = jnp.zeros((LANES, LANES), F32)
        att_grad = dot_r(low, w_merge[...]).astype(BF)
        for pair in range(PAIRS):
            cols = slice(pair * LANES, (pair + 1) * LANES)
            w = att_grad[:, cols].astype(F32) * inv[:, cols]
            w_low = w.astype(BF).astype(F32)
            high, rest = high_low(w_low * att[:, cols])
            left = jnp.concatenate([high.astype(BF), rest.astype(BF)], axis=1)
            e = -dot(left, jnp.concatenate([across, across], axis=0))
            e_high, e_low = high_low(e)
            we = jnp.where(
                is_even, w_low, jnp.where(lane == HALF, e_high, jnp.where(lane == HALF + 1, e_low, 0.0))
            ).astype(BF)
            wo = jnp.where(
                is_even, jnp.where(lane == 0, e_high, jnp.where(lane == 1, e_low, 0.0)), w_low
            ).astype(BF)
            we_o[:, cols] = we
            wo_o[:, cols] = wo
            qp = rq[:, cols].astype(F32)
            left = jnp.concatenate([(qp * cos_b).astype(BF), (qp * sin_b).astype(BF)], axis=1)
            both = dot_t(left, jnp.concatenate([we, wo], axis=1))
            of_cos = jnp.where(upper, both[:LANES, :LANES], both[:LANES, LANES:])
            of_sin = jnp.where(upper, both[LANES:, :LANES], both[LANES:, LANES:])
            norm_cos = jnp.sum(jnp.where(diag, 0.0, of_cos), axis=1, keepdims=True)
            norm_sin = jnp.sum(jnp.where(diag, 0.0, of_sin), axis=1, keepdims=True)
            packed, norms = pack_state(of_cos, of_sin, norm_cos, norm_sin, pair, norms)
            st_o[pair] = packed
        st_o[PAIRS] = norms.astype(BF)


def attn_back_kernel(
    head_at, core_at, scal, rq, rk, v, we, wo, prior, later, tcol, trow,
    pk_o, ps_o, sums_o,
    weights, weights_t,
):
    pair = pl.program_id(0)
    rows = rq.shape[0]
    mid = rows // 2

    @pl.when(pair == 0)
    def _():
        weights[...] = weights_block(tcol, trow, False)
        weights_t[...] = weights_block(tcol, trow, True)

    lane, even, even_b, odd_b = lane_masks()
    is_even = lane < HALF
    sq_lane, upper, diag = square_masks()
    qp, kp, vp = rq[...], rk[...], v[...]
    w_of = (we[...], wo[...])
    ones_even = ((lane == HALF) | (lane == HALF + 1)).astype(F32).astype(BF)
    ones_odd = ((lane == 0) | (lane == 1)).astype(F32).astype(BF)
    v_of = (vp * even_b + ones_even, vp * odd_b + ones_odd)
    own = (even_b, odd_b)
    is_late = (scal[head_at] == 1).astype(F32)
    dq_parts, dk_parts, dv_parts = [], [], []
    for lo, hi in ((0, mid), (mid, rows)):
        outs = []
        for n in range(2):
            grads = dot_r(w_of[n][lo:hi], v_of[n][:hi]) * weights[lo:hi, :hi]
            outs.append(dot(grads.astype(BF), kp[:hi]))
        dq_parts.append(jnp.where(is_even, outs[0], outs[1]))
        outs_k, outs_v = [], []
        for n in range(2):
            grads = dot_r(v_of[n][lo:hi], w_of[n][lo:]) * weights_t[lo:hi, lo:]
            outs_k.append(dot(grads.astype(BF), qp[lo:]))
            scores = dot_r(kp[lo:hi] * own[n], qp[lo:]) * weights_t[lo:hi, lo:]
            outs_v.append(dot(scores.astype(BF), w_of[n][lo:]))
        dk_parts.append(jnp.where(is_even, outs_k[0], outs_k[1]))
        dv_parts.append(jnp.where(is_even, outs_v[0], outs_v[1]))
    dq = jnp.concatenate(dq_parts, axis=0)
    dk = jnp.concatenate(dk_parts, axis=0)
    dv = jnp.concatenate(dv_parts, axis=0)

    def by_head(of_cos, of_sin, norm_cos, norm_sin, lanes):
        ones = tuple((sum((lane == n).astype(F32) for n in run)) for run in lanes)
        def side(total, norm):
            full_e = jnp.where(upper, total + norm * ones[0], 0.0)
            full_o = jnp.where(upper, 0.0, total + norm * ones[1])
            return jnp.concatenate([full_e, full_o], axis=1)
        return jnp.concatenate([side(of_cos, norm_cos), side(of_sin, norm_sin)], axis=0).astype(BF)

    cos_b, sin_b = tcol[:, 3:4], tcol[:, 4:5]
    prior_parts = unpack_state(prior, pair)
    into = dot_r(jnp.concatenate(w_of, axis=1), by_head(*prior_parts, ((HALF, HALF + 1), (0, 1))))
    dq = dq + is_late * (cos_b * into[:, :LANES] + sin_b * into[:, LANES:])
    later_parts = unpack_state(later, pair)
    into = dot_r(jnp.concatenate(v_of, axis=1), by_head(*later_parts, ((HALF,), (0,))))
    early = 1.0 - is_late
    dk = dk + early * (cos_b * into[:, :LANES] + sin_b * into[:, LANES:])
    kw = kp.astype(F32)
    left = jnp.concatenate([(kw * (cos_b * early)).astype(BF), (kw * (sin_b * early)).astype(BF)], axis=1)
    dv = dv + dot(left, jnp.concatenate(later_parts[:2], axis=0).astype(BF))

    dq = jnp.where(qp.astype(F32) > 0, dq, 0.0).astype(BF)
    dk = jnp.where(kw > 0, dk, 0.0).astype(BF)
    dv = dv.astype(BF)
    blocks = 3 * PAIRS // 2
    for n, part in enumerate((dq, dk, dv)):
        sums_o[n] = jnp.broadcast_to(jnp.sum(part.astype(F32), axis=0, keepdims=True), sums_o.shape[1:])
        at = n * PAIRS + pair
        mine = (at >= blocks) == (scal[core_at] == 1)
        slot = lax.rem(at, blocks)

        @pl.when(mine)
        def _():
            pk_o[slot] = part

        @pl.when(jnp.logical_not(mine))
        def _():
            ps_o[slot] = part


def input_kernel(scal, first, keep, send, w_keep, w_send, out_o):
    @pl.when(pl.program_id(0) == 0)
    def _():
        out_o[...] = first[...]

    left = lambda ref: jnp.concatenate([ref[n] for n in range(ref.shape[0])], axis=1)
    out_o[...] += dot_r(left(keep), w_keep[...]) + dot_r(left(send), w_send[...])


def place(values, piece_rows, tz, tys, x, y, z, extra, outs):
    xk, xs, yk, ys = outs
    width = xk.shape[-1]
    slot_z = tz ^ z
    pieces = {}
    at = 0
    for ty in tys:
        for tc in range(2):
            for tx in range(2):
                part = values[at * piece_rows : (at + 1) * piece_rows]
                blocks = [part[:, n : n + width] for n in range(0, part.shape[1], width)]
                if extra is not None:
                    blocks.append(extra[at])
                pieces[ty, tc, tx] = jnp.concatenate(blocks, axis=0) if len(blocks) > 1 else blocks[0]
                at += 1
    for ty in tys:
        slot = ty ^ y
        a, b = pieces[ty, 0, 0], pieces[ty, 0, 1]
        xk[slot, slot_z] = jnp.where(x == 0, a, b).astype(BF)
        xs[slot, slot_z] = jnp.where(x == 0, b, a).astype(BF)
    return pieces


def place_y(pieces, tz, tys, x, y, z, outs):
    xk, xs, yk, ys = outs
    slot_z = tz ^ z
    for tx in range(2):
        slot = tx ^ x
        a, b = pieces[0, 1, tx], pieces[1, 1, tx]
        yk[slot, slot_z] = jnp.where(y == 0, a, b).astype(BF)
        ys[slot, slot_z] = jnp.where(y == 0, b, a).astype(BF)


def reduce_grad_kernel(pos_at, scal, a_own, a_oth, b_own, b_oth, *outs):
    tz = pl.program_id(0)
    x, y, z = (scal[pos_at + n] for n in range(3))
    values = dot_t(a_own[...], b_own[...]) + dot_t(a_oth[...], b_oth[...])
    piece_rows = values.shape[0] // 8
    pieces = place(values, piece_rows, tz, (0, 1), x, y, z, None, outs)
    place_y(pieces, tz, (0, 1), x, y, z, outs)


def expand_grad_kernel(pos_at, scal, a_own, a_oth, b_own, b_oth, m_own, m_oth, c_own, c_oth, *outs):
    tz = pl.program_id(0)
    x, y, z = (scal[pos_at + n] for n in range(3))
    an, ao = a_own[0], a_oth[0]
    parts = [dot(an, b_own[n]) + dot(ao, b_oth[n]) for n in range(b_own.shape[0])]
    parts.append(dot(m_own[0], c_own[...]) + dot(m_oth[0], c_oth[...]))
    values = jnp.concatenate(parts, axis=1)
    pieces = place(values, values.shape[0] // 8, tz, (0, 1), x, y, z, None, outs)
    place_y(pieces, tz, (0, 1), x, y, z, outs)


def heads_grad_kernel(pos_at, scal, a_own, a_oth, b_own, b_oth, vectors, *outs):
    tz = pl.program_id(0)
    x, y, z = (scal[pos_at + n] for n in range(3))
    join = lambda ref: jnp.concatenate([ref[n] for n in range(ref.shape[0])], axis=1)
    values = dot(a_own[0], join(b_own)) + dot(a_oth[0], join(b_oth))
    extra = [vectors[n] for n in range(8)]
    pieces = place(values, values.shape[0] // 8, tz, (0, 1), x, y, z, extra, outs)
    place_y(pieces, tz, (0, 1), x, y, z, outs)


class Ring:
    def __init__(self, n_dp):
        self.n_dp = n_dp
        self.devices = 2 * n_dp

    def swap(self, value, bits):
        return lax.ppermute(value, AXES, [(i, i ^ bits) for i in range(self.devices)])

    def core(self, value):
        return self.swap(value, 2)

    def x(self, value):
        return self.swap(value, 1)

    def y(self, value):
        return self.swap(value, 4)

    def z(self, value, step):
        return self.swap(value, 8 * step)


def scatter_group(ring, first_core, xk, xs, yk, ys):
    wide = lambda v: v.astype(F32)
    xr, yr = ring.x(xs), ring.y(ys)
    x_next, y_next = (wide(xk[1]) + wide(xr[1])).astype(BF), (wide(yk[1]) + wide(yr[1])).astype(BF)
    x_next, y_next = ring.y(x_next), ring.x(y_next)
    totals = []
    for keep, got, more in ((xk, xr, x_next), (yk, yr, y_next)):
        held = wide(keep[0]) + wide(got[0]) + wide(more)
        arrived = [ring.z(held[k].astype(BF), k) for k in (1, 2, 3)]
        totals.append(held[0] + wide(arrived[0]) + wide(arrived[1]) + wide(arrived[2]))
    keep = jnp.where(first_core, totals[0], totals[1])
    send = jnp.where(first_core, totals[1], totals[0])
    return keep, ring.core(send)


def halves(first_core, own, other):
    left = jnp.where(first_core, own, other)
    right = jnp.where(first_core, other, own)
    return jnp.concatenate([left, right], axis=1)


def columns(part, rows, blocks):
    return part.reshape(blocks, rows, part.shape[-1]).transpose(1, 0, 2).reshape(rows, -1)


def transposed_pieces(value):
    return value.T.reshape(4, D // 4, value.shape[0])


def per_device(
    tokens, w_heads, b_heads, w_merge, b_merge, gain_first, bias_first, w_expand, b_expand,
    w_reduce, b_reduce, gain_second, bias_second, seq_lengths, cotangent,
):
    rows = tokens.shape[0]
    seqs = seq_lengths.shape[1]
    n_dp = lax.axis_size("dp")
    ring = Ring(n_dp)
    head = lax.axis_index("head")
    dp = lax.axis_index("dp")
    core = dp % 2
    place_of = jnp.stack([head, core, head, (dp // 2) % 2, dp // 4]).astype(jnp.int32)
    scal = jnp.concatenate([seq_lengths[0].astype(jnp.int32), place_of])
    head_at, core_at, pos_at = seqs, seqs + 1, seqs + 2
    first_core = core == 0
    line = lambda v: v.reshape(1, -1)
    b_heads, b_merge, gain_first, bias_first, b_expand, b_reduce, gain_second, bias_second = map(
        line, (b_heads, b_merge, gain_first, bias_first, b_expand, b_reduce, gain_second, bias_second)
    )
    wide_shape = (rows, D)
    quarter = 256

    rk, v, state, tcol, trow = call(
        functools.partial(kv_kernel, seqs), "keys_values", scal, (3,),
        [
            (tokens, None, None),
            (w_heads, (D, quarter), lambda j, s: (0, 3 + j)),
            (w_heads, (D, quarter), lambda j, s: (0, 6 + j)),
            (b_heads, (1, quarter), lambda j, s: (0, 3 + j)),
            (b_heads, (1, quarter), lambda j, s: (0, 6 + j)),
        ],
        [
            (wide_shape, BF, (rows, quarter), lambda j, s: (0, j)),
            (wide_shape, BF, (rows, quarter), lambda j, s: (0, j)),
            ((PAIRS + 1, LANES, LANES), BF, None, None),
            ((rows, LANES), F32, None, None),
            ((8, rows), F32, None, None),
        ],
        [pltpu.VMEM((LANES, LANES), F32)],
        flops=4 * rows * D * D,
    )
    forward = [(i, i + 1) for i in range(0, 2 * n_dp, 2)]
    backward = [(b, a) for a, b in forward]
    prior = lax.ppermute(state, AXES, forward)

    rq, num, den = call(
        local_kernel, "local_attention", scal, (3,),
        [
            (tokens, None, None),
            (w_heads, (D, quarter), lambda j, s: (0, j)),
            (b_heads, (1, quarter), lambda j, s: (0, j)),
            (rk, (rows, quarter), lambda j, s: (0, j)),
            (v, (rows, quarter), lambda j, s: (0, j)),
            (tcol, None, None),
            (trow, None, None),
        ],
        [
            (wide_shape, BF, (rows, quarter), lambda j, s: (0, j)),
            (wide_shape, F32, (rows, quarter), lambda j, s: (0, j)),
            (wide_shape, F32, (rows, quarter), lambda j, s: (0, j)),
        ],
        [pltpu.VMEM((rows, rows), F32)],
        flops=2 * rows * D * D + 8 * rows * rows * D,
    )

    att, inv, mixed, xhat, scale, normed, act, slope, second = call(
        lambda *refs: ffn_kernel(*refs, head_at), "feed_forward", scal, (FF_STEPS,),
        [
            (rq, None, None), (num, None, None), (den, None, None), (prior, None, None),
            (tcol, None, None), (tokens, None, None), (w_merge, None, None), (b_merge, None, None),
            (gain_first, None, None), (bias_first, None, None),
            (w_expand, (D, FF_BLOCK), lambda j, s: (0, j)),
            (b_expand, (1, FF_BLOCK), lambda j, s: (0, j)),
            (w_reduce, (FF_BLOCK, D), lambda j, s: (j, 0)),
            (b_reduce, None, None),
        ],
        [
            (wide_shape, F32, None, None), (wide_shape, F32, None, None), (wide_shape, BF, None, None),
            (wide_shape, F32, None, None), ((rows, LANES), F32, None, None), (wide_shape, BF, None, None),
            ((rows, FF), BF, (rows, FF_BLOCK), lambda j, s: (0, j)),
            ((rows, FF), BF, (rows, FF_BLOCK), lambda j, s: (0, j)),
            (wide_shape, F32, None, None),
        ],
        [pltpu.VMEM(wide_shape, F32)],
        flops=2 * rows * D * (D + 2 * FF),
    )

    half_shape = (rows, D // 2)
    result, grad_second, branch, bg_keep, bg_send, sums_second = call(
        functools.partial(second_kernel, core_at), "second_norm", scal, (1,),
        [(second, None, None), (cotangent, None, None), (gain_second, None, None), (bias_second, None, None)],
        [
            (wide_shape, BF, None, None), (wide_shape, F32, None, None), (wide_shape, BF, None, None),
            (half_shape, BF, None, None), (half_shape, BF, None, None), ((8, D), F32, None, None),
        ],
        flops=20 * rows * D,
    )

    ff_half = FF_STEPS // 2
    pg_keep, pg_send, grad_first, mg_keep, mg_send, w_even, w_odd, later, sum_expand, sums_first = call(
        functools.partial(back_kernel, core_at), "feed_forward_back", scal, (FF_STEPS,),
        [
            (branch, None, None),
            (slope, (rows, FF_BLOCK), lambda j, s: (0, j)),
            (w_expand, (D, FF_BLOCK), lambda j, s: (0, j)),
            (w_reduce, (FF_BLOCK, D), lambda j, s: (j, 0)),
            (grad_second, None, None), (gain_first, None, None), (xhat, None, None), (scale, None, None),
            (w_merge, None, None), (att, None, None), (inv, None, None), (rq, None, None), (tcol, None, None),
        ],
        [
            ((ff_half, rows, FF_BLOCK), BF, None, None), ((ff_half, rows, FF_BLOCK), BF, None, None),
            (wide_shape, F32, None, None), (half_shape, BF, None, None), (half_shape, BF, None, None),
            (wide_shape, BF, None, None), (wide_shape, BF, None, None),
            ((PAIRS + 1, LANES, LANES), BF, None, None),
            ((1, FF), F32, (1, FF_BLOCK), lambda j, s: (0, j)),
            ((8, D), F32, None, None),
        ],
        [pltpu.VMEM(wide_shape, F32)],
        flops=2 * rows * D * (D + 2 * FF),
    )
    later = lax.ppermute(later, AXES, backward)

    blocks = 3 * PAIRS // 2
    pair_block = lambda a: (a, (rows, LANES), lambda j, s: (0, j))
    pj_keep, pj_send, sum_heads = call(
        functools.partial(attn_back_kernel, head_at, core_at), "attention_back", scal, (PAIRS,),
        [
            pair_block(rq), pair_block(rk), pair_block(v), pair_block(w_even), pair_block(w_odd),
            (prior, None, None), (later, None, None), (tcol, None, None), (trow, None, None),
        ],
        [
            ((blocks, rows, LANES), BF, None, None), ((blocks, rows, LANES), BF, None, None),
            ((3, 8, D), F32, (3, 8, LANES), lambda j, s: (0, 0, j)),
        ],
        [pltpu.VMEM((rows, rows), F32), pltpu.VMEM((rows, rows), F32)],
        flops=16 * rows * rows * D,
    )

    third = blocks // 3
    wide_block = third * LANES
    (input_grad,) = call(
        input_kernel, "input_grad", scal, (3,),
        [
            (grad_first, None, None),
            (pj_keep, (third, rows, LANES), lambda j, s: (j, 0, 0)),
            (pj_send, (third, rows, LANES), lambda j, s: (j, 0, 0)),
            (w_heads, (D, wide_block), lambda j, s: (0, 3 * s[core_at] + j)),
            (w_heads, (D, wide_block), lambda j, s: (0, 3 * (1 - s[core_at]) + j)),
        ],
        [(wide_shape, F32, None, None)],
        flops=6 * rows * D * D,
    )

    vectors = [
        jnp.concatenate([sum_heads[0, 0], sum_heads[1, 0]]), sum_heads[2, 0],
        sums_first[2], sums_first[0], sums_first[1],
        sum_expand[0], sums_second[2], sums_second[0], sums_second[1],
    ]
    if n_dp == 16:
        grads = exchange_fast(
            ring, first_core, scal, pos_at, vectors, tokens, mixed, normed, act,
            bg_keep, bg_send, pg_keep, pg_send, mg_keep, mg_send, pj_keep, pj_send,
        )
    else:
        by_core = lambda keep, send: jnp.concatenate(
            [jnp.where(first_core, keep, send), jnp.where(first_core, send, keep)], axis=1
        )
        flat = lambda v: v.transpose(1, 0, 2).reshape(rows, -1)
        scatter = lambda v: lax.psum_scatter(v, AXES, scatter_dimension=0, tiled=True)
        grads = (
            scatter(dot_t(tokens, by_core(flat(pj_keep), flat(pj_send)))),
            scatter(vectors[0]), scatter(vectors[1]),
            scatter(dot_t(mixed, by_core(mg_keep, mg_send))),
            scatter(vectors[2]), scatter(vectors[3]), scatter(vectors[4]),
            scatter(dot_t(normed, by_core(flat(pg_keep), flat(pg_send)))),
            scatter(vectors[5]),
            scatter(dot_t(act, branch)),
            scatter(vectors[6]), scatter(vectors[7]), scatter(vectors[8]),
        )
    return (result, input_grad) + tuple(grads)


def exchange_fast(
    ring, first_core, scal, pos_at, vectors, tokens, mixed, normed, act,
    bg_keep, bg_send, pg_keep, pg_send, mg_keep, mg_send, pj_keep, pj_send,
):
    rows = tokens.shape[0]
    devices = ring.devices
    width = D // 2
    small, large = D // devices, FF // devices
    tokens_t, normed_t, mixed_t = map(transposed_pieces, (tokens, normed, mixed))
    tokens_o, normed_o, mixed_o, act_o = map(ring.core, (tokens_t, normed_t, mixed_t, act))
    bg_o, pg_o, mg_o, pj_o = map(ring.core, (bg_send, pg_send, mg_send, pj_send))

    def group(kernel, name, ins, piece_rows, flops):
        shape = (2, 4, piece_rows, width)
        return call(
            functools.partial(kernel, pos_at), name, scal, (4,), ins, [(shape, BF, None, None)] * 4, flops=flops
        )

    by_z = lambda a: (a, (1, D // 4, rows), lambda j, s: (j, 0, 0))
    whole = lambda a: (a, None, None)
    by_col = lambda a: (a, (rows, FF // 4), lambda j, s: (0, j))
    flops = lambda n: 2 * rows * D * n
    reduce_sent = group(
        reduce_grad_kernel, "grad_reduce", [by_col(act), by_col(act_o), whole(bg_keep), whole(bg_o)],
        large, flops(FF),
    )
    reduce_own, reduce_got = scatter_group(ring, first_core, *reduce_sent)
    expand_sent = group(
        expand_grad_kernel, "grad_expand",
        [
            by_z(normed_t), by_z(normed_o), whole(pg_keep), whole(pg_o),
            by_z(mixed_t), by_z(mixed_o), whole(mg_keep), whole(mg_o),
        ],
        5 * small, flops(FF + D),
    )
    expand_own, expand_got = scatter_group(ring, first_core, *expand_sent)

    flat = jnp.concatenate([v.reshape(devices, -1) for v in vectors], axis=1)
    count = flat.shape[1]
    high = lax.optimization_barrier(flat.astype(BF)).astype(F32)
    packed = jnp.concatenate([high, flat - high], axis=1)
    packed = jnp.pad(packed, ((0, 0), (0, 8 * width - 2 * count))).reshape(devices, 8, width)
    heads_sent = group(
        heads_grad_kernel, "grad_heads",
        [
            by_z(tokens_t), by_z(tokens_o), whole(pj_keep), whole(pj_o),
            (packed, (8, 8, width), lambda j, s: (j, 0, 0)),
        ],
        3 * small + 8, flops(3 * D),
    )
    heads_own, heads_got = scatter_group(ring, first_core, *heads_sent)

    w_reduce_grad = halves(first_core, reduce_own, reduce_got)
    split = 4 * small
    w_expand_grad = halves(
        first_core, columns(expand_own[:split], small, 4), columns(expand_got[:split], small, 4)
    )
    w_merge_grad = halves(first_core, expand_own[split:], expand_got[split:])
    split = 3 * small
    w_heads_grad = halves(
        first_core, columns(heads_own[:split], small, 3), columns(heads_got[:split], small, 3)
    )
    entries = (heads_own[split:] + heads_got[split:]).reshape(-1)
    entries = entries[:count] + entries[count : 2 * count]
    shares, at = [], 0
    for v in vectors:
        n = v.shape[0] // devices
        shares.append(entries[at : at + n])
        at += n
    return (
        w_heads_grad, *shares[:2], w_merge_grad, *shares[2:5], w_expand_grad, shares[5], w_reduce_grad, *shares[6:]
    )


def solution(mesh):
    in_specs = (P(AXES, None),) + (P(),) * 12 + (P("dp", None), P(AXES, None))
    row, one = P(AXES, None), P(AXES)
    out_specs = (row, row, row, one, one, row, one, one, one, row, one, row, one, one, one)
    return jax.shard_map(
        per_device, mesh=mesh, in_specs=in_specs, out_specs=out_specs, check_vma=False
    )
```

time: 1080 us -> 260 us (0.24)
  waiting for transfers between devices: 343 us -> 66.2 us
  other arithmetic: 247 us -> 16.3 us
  matrix products: 191 us -> 0 us
  local copies, waits for them, and re-layouts: 199 us -> 28.6 us
  Pallas kernels: 0 us -> 96.1 us
  blocking collectives: 41.2 us -> 0 us
  between operations: 15 us -> 1.34 us
  starting transfers between devices: 36.5 us -> 50 us
    reduce_scatter x3 -> x0, waiting for transfers between devices: 283 us -> none  [the longest x1 142 us: per_device(): lax.psum_scatter(grad_w_reduce, ('dp', 'head'), scatter_dimension=0, tile...]
    dot_general x26 -> x0, matrix products: 191 us -> none  [the longest x4 25.9 us: row_dot(): lax.dot_general(left, right, (((0,), (0,)), ((), ())), preferred_element_...]
    add x67 -> x2, other arithmetic: 119 us -> 0.08 us  [the longest x1 0.07 us: exchange_fast(): entries = entries[:count] + entries[count:2 * count]]
    pallas_call x0 -> x10, Pallas kernels: none -> 96.1 us  [call(): pl.pallas_call(kernel, name=name, grid_spec=pltpu.PrefetchScalarGridSpec(...]
    dynamic_update_slice x64 -> x0, other arithmetic: 74.2 us -> none  [attend_forward(): lax.scan(advance, initial, (block_state, block_norm, carry_on))]
    ppermute x0 -> x43, waiting for transfers between devices: none -> 66.2 us  [the longest x41 58.7 us: swap(): lax.ppermute(value, AXES, [(i, i ^ bits) for i in range(self.devices)])]
    dynamic_slice x50 -> x0, local copies, waits for them, and re-layouts: 51.7 us -> none  [the longest x48 51.5 us: attend_forward(): lax.scan(advance, initial, (block_state, block_norm, carry_on))]
    ppermute x0 -> x43, starting transfers between devices: none -> 50 us  [the longest x41 43.7 us: swap(): lax.ppermute(value, AXES, [(i, i ^ bits) for i in range(self.devices)])]
  transfers between devices with their start and end apart: 12 -> 43, of which waited for: 8 -> 14; matrix products, arithmetic and copies ran while one was open for 36% -> 13% of each run, Pallas kernels for 0% -> 13%
where the time goes in v1:
time: 260 us; the launch traced here: 259 us
  Pallas kernels  96.1 us (37%)
  waiting for transfers between devices  66.2 us (25%)
  starting transfers between devices  50 us (19%)
  local copies, waits for them, and re-layouts  28.6 us (11%)
  other arithmetic  16.3 us (6%)
    pallas_call x10, Pallas kernels, call(): pl.pallas_call(kernel, name=name, grid_spec=pltpu.PrefetchScalarGridSpec(...  96.1 us
    ppermute x41, waiting for transfers between devices, swap(): lax.ppermute(value, AXES, [(i, i ^ bits) for i in range(self.devices)])  58.7 us
    ppermute x41, starting transfers between devices, swap(): lax.ppermute(value, AXES, [(i, i ^ bits) for i in range(self.devices)])  43.7 us
    unnamed x63, local copies, waits for them, and re-layouts  8.46 us
    ppermute x1, waiting for transfers between devices, per_device(): later = lax.ppermute(later, AXES, backward)  7.48 us
    another operation x8, local copies, waits for them, and re-layouts, exchange_fast(): flat = jnp.concatenate([v.reshape(devices, -1) for v in vectors], axis=1)  6.16 us
  transfers between devices with their start and end apart: 43, of which 14 were waited for; matrix products, arithmetic and copies ran while one was open for 13% of the time, Pallas kernels for 13%

profile of v1, /device:TPU:0, one launch (start us, length us, event | category | flops | bytes accessed | tf_op | source)
XLA Modules:
  0.0 258.6 jit_solution(14267463083396419441)
XLA Ops:
  3.3 5.1 %keys_values.1 = (bf16[512,768]{1,0:T(8,128)(2,1)S(1)}, bf16[512,768]{1,0:T(8,128)(2,1)S(1)}, bf16[7,128,128]{2,1,0:T(8,128)(2,1)S(1)}, f32[512,128]{1,0:T(8,128)S(1)}, f32[8,512]{1,0:T(8,128)S(1)}) custom-call(s32[9]{0:T(128)S(1)} %concatenate.29.scal.refs_0_, bf16[512,768]{1,0:T(8,128)(2,1)S(1)} %copy-done, bf16[768,2304]{1,0:T(8,128)(2,1)} %w_send.1, ...), custom_call_target="tpu_custom_call" | custom-call | flops 1207959552 | bytes 9954304 | tf_op jit(solution)/shard_map/keys_values/pallas_call | solution.py:48
  8.4 4.9 %collective-permute-start = (bf16[7,128,128]{2,1,0:T(8,128)(2,1)S(1)}, bf16[7,128,128]{2,1,0:T(8,128)(2,1)S(1)}, u32[]{:S(2)}, u32[]{:S(2)}) collective-permute-start(bf16[7,128,128]{2,1,0:T(8,128)(2,1)S(1)} %get-tuple-element.70), channel_id=1, source_target_pairs={{0,1},{2,3},{4,5},{6,7},{8,9},{10,11},{12,13},{14,15},{16,17},{18,... | collective-permute-start | bytes 688136 | tf_op jit(solution)/shard_map/ppermute | solution.py:605
  13.4 9.0 %local_attention.1 = (bf16[512,768]{1,0:T(8,128)(2,1)S(1)}, f32[512,768]{1,0:T(8,128)S(1)}, f32[512,768]{1,0:T(8,128)}) custom-call(s32[9]{0:T(128)S(1)} %concatenate.29.scal.refs_0_, bf16[512,768]{1,0:T(8,128)(2,1)S(1)} %copy-done, bf16[768,2304]{1,0:T(8,128)(2,1)} %w_send.1, bf16[1,2304]{1,0:T(2,128)(2,1)S(1)} %reshape.158.bk.bv.bq, ...), custom_call_target="tpu_custom_call" | custom-call | flops 2214592512 | bytes 10113536 | tf_op jit(solution)/shard_map/local_attention/pallas_call | solution.py:48
  23.5 17.5 %feed_forward.1 = (f32[512,768]{1,0:T(8,128)}, f32[512,768]{1,0:T(8,128)}, bf16[512,768]{1,0:T(8,128)(2,1)S(1)}, f32[512,768]{1,0:T(8,128)}, f32[512,128]{1,0:T(...) custom-call(s32[9]{0:T(128)S(1)} %concatenate.29.scal.refs_0_, ...), custom_call_target="tpu_custom_call" | custom-call | flops 5435817984 | bytes 30257152 | tf_op jit(solution)/shard_map/feed_forward/pallas_call | solution.py:48
  42.0 1.4 copy-done.4
  43.4 2.7 %second_norm.1 = (bf16[512,768]{1,0:T(8,128)(2,1)}, f32[512,768]{1,0:T(8,128)S(1)}, bf16[512,768]{1,0:T(8,128)(2,1)S(1)}, bf16[512,384]{1,0:T(8,128)(2,1)S(1)}, ...) custom-call(s32[9]{0:T(128)S(1)} %concatenate.29.scal.refs_0_, f32[512,768]{1,0:T(8,128)S(1)} %copy-done.4, ...), custom_call_target="tpu_custom_call" | custom-call | flops 7864320 | bytes 6319104 | tf_op jit(solution)/shard_map/second_norm/pallas_call | solution.py:48
  47.3 19.2 %feed_forward_back.1 = (bf16[3,512,512]{2,1,0:T(8,128)(2,1)}, bf16[3,512,512]{2,1,0:T(8,128)(2,1)}, f32[512,768]{1,0:T(8,128)}, bf16[512,384]{1,0:T(8,128)(2,1)S...) custom-call(s32[9]{0:T(128)S(1)} %concatenate.29.scal.refs_0_, ...), custom_call_target="tpu_custom_call" | custom-call | flops 5435817984 | bytes 29496832 | tf_op jit(solution)/shard_map/feed_forward_back/pallas_call | solution.py:48
  66.5 1.5 collective-permute-start.1
  67.9 7.5 %collective-permute-done.1.later = bf16[7,128,128]{2,1,0:T(8,128)(2,1)S(1)} collective-permute-done((bf16[7,128,128]{2,1,0:T(8,128)(2,1)S(1)}, bf16[7,128,128]{2,1,0:T(8,128)(2,1)S(1)}, u32[]{:S(2)}, u32[]{:S(2)}) %collective-permute-start.1) | collective-permute-done | bytes 229408 | tf_op jit(solution)/shard_map/ppermute | solution.py:682
  75.4 17.0 %attention_back.1 = (bf16[9,512,128]{2,1,0:T(8,128)(2,1)S(1)}, bf16[9,512,128]{2,1,0:T(8,128)(2,1)}, f32[3,8,768]{2,1,0:T(8,128)S(1)}) custom-call(s32[9]{0:T(128)S(1)} %concatenate.29.scal.refs_0_, bf16[512,768]{1,0:T(8,128)(2,1)S(1)} %get-tuple-element.67.refs_1_.rq, bf16[512,768]{1,0:T(8,128)(2,1)S(1)} %get-tuple-element.63.rk, ...), custom_call_target="tpu_custom_call" | custom-call | flops 3221225472 | bytes 7102464 | tf_op jit(solution)/shard_map/attention_back/pallas_call | solution.py:48
  94.4 1.4 copy.41
  96.8 1.3 reduce.21
  98.1 1.4 reshape_squeeze.28
  105.3 1.4 slice_reduce_fusion.6
  107.5 1.4 concatenate.31
  109.5 1.3 pad_maximum_fusion.4
  110.8 1.6 concatenate.33
  114.2 5.0 %grad_heads.1 = (bf16[2,4,80,384]{3,2,1,0:T(8,128)(2,1)S(1)}, bf16[2,4,80,384]{3,2,1,0:T(8,128)(2,1)S(1)}, bf16[2,4,80,384]{3,2,1,0:T(8,128)(2,1)S(1)}, bf16[2,4,80,384]{3,2,1,0:T(8,128)(2,1)S(1)}) custom-call(s32[9]{0:T(128)S(1)} %concatenate.29.scal.refs_0_, bf16[4,192,512]{2,1,0:T(8,128)(2,1)S(1)} %bitcast.169, ...), custom_call_target="tpu_custom_call" | custom-call | flops 1811939328 | bytes 6291456 | tf_op jit(solution)/shard_map/grad_heads/pallas_call | solution.py:48
  119.3 1.6 collective-permute-start.9
  120.9 11.7 %collective-permute-done.9 = bf16[2,4,80,384]{3,2,1,0:T(8,128)(2,1)S(1)} collective-permute-done((bf16[2,4,80,384]{3,2,1,0:T(8,128)(2,1)S(1)}, bf16[2,4,80,384]{3,2,1,0:T(8,128)(2,1)S(1)}, u32[]{:S(2)}, u32[]{:S(2)}) %collective-permute-start.9) | collective-permute-done | bytes 491552 | tf_op jit(solution)/shard_map/ppermute | solution.py:518
  132.7 2.1 collective-permute-start.10
  134.8 7.9 %grad_expand.1 = (bf16[2,4,120,384]{3,2,1,0:T(8,128)(2,1)S(1)}, bf16[2,4,120,384]{3,2,1,0:T(8,128)(2,1)}, bf16[2,4,120,384]{3,2,1,0:T(8,128)(2,1)S(1)}, bf16[2,4,120,384]{3,2,1,0:T(8,128)(2,1)}) custom-call(s32[9]{0:T(128)S(1)} %concatenate.29.scal.refs_0_, bf16[4,192,512]{2,1,0:T(8,128)(2,1)S(1)} %bitcast.165, ...), custom_call_target="tpu_custom_call" | custom-call | flops 3019898880 | bytes 10027008 | tf_op jit(solution)/shard_map/grad_expand/pallas_call | solution.py:48
  142.7 1.5 collective-permute-start.24
  144.2 2.5 collective-permute-done.4
  146.8 1.6 collective-permute-start.5
  148.4 3.6 %collective-permute-done.10 = bf16[4,80,384]{2,1,0:T(8,128)(2,1)S(1)} collective-permute-done((bf16[4,80,384]{2,1,0:T(8,128)(2,1)S(1)}, bf16[4,80,384]{2,1,0:T(8,128)(2,1)S(1)}, u32[]{:S(2)}, u32[]{:S(2)}) %collective-permute-start.10) | collective-permute-done | bytes 245792 | tf_op jit(solution)/shard_map/ppermute | solution.py:518
  153.5 1.6 collective-permute-start.11
  155.1 11.6 %collective-permute-done.5 = bf16[4,80,384]{2,1,0:T(8,128)(2,1)S(1)} collective-permute-done((bf16[4,80,384]{2,1,0:T(8,128)(2,1)S(1)}, bf16[4,80,384]{2,1,0:T(8,128)(2,1)S(1)}, u32[]{:S(2)}, u32[]{:S(2)}) %collective-permute-start.5) | collective-permute-done | bytes 245792 | tf_op jit(solution)/shard_map/ppermute | solution.py:518
  166.7 2.6 collective-permute-start.12
  170.9 1.4 collective-permute-start.13
  172.2 2.1 collective-permute-start.6
  174.3 3.0 %collective-permute-done.13 = bf16[80,384]{1,0:T(8,128)(2,1)} collective-permute-done((bf16[80,384]{1,0:T(8,128)(2,1)}, bf16[80,384]{1,0:T(8,128)(2,1)}, u32[]{:S(2)}, u32[]{:S(2)}) %collective-permute-start.13) | collective-permute-done | bytes 61472 | tf_op jit(solution)/shard_map/ppermute | solution.py:518
  177.9 4.0 %collective-permute-start.8 = (bf16[80,384]{1,0:T(8,128)(2,1)}, bf16[80,384]{1,0:T(8,128)(2,1)S(1)}, u32[]{:S(2)}, u32[]{:S(2)}) collective-permute-start(bf16[80,384]{1,0:T(8,128)(2,1)} %get-tuple-element.163), channel_id=1, source_target_pairs={{0,24},{1,25},{2,26},{3,27},{4,28},{5,29},{6,30},{7,31},{8,16},{9,... | collective-permute-start | bytes 184328 | tf_op jit(solution)/shard_map/ppermute | solution.py:518
  183.2 6.3 %input_grad.1 = f32[512,768]{1,0:T(8,128)} custom-call(s32[9]{0:T(128)S(1)} %concatenate.29.scal.refs_0_, f32[512,768]{1,0:T(8,128)S(1)} %copy-done.2, bf16[9,512,128]{2,1,0:T(8,128)(2,1)S(1)} %get-tuple-element.84.keep.b_own, bf16[9,512,128]{2,1,0:T(8,128)(2,1)S(1)} %copy-done.6, bf16[768,2304]{1,0:T(8,128)(2,1)} %w_send.1, bf16[768,2304]{1,0:T(8,128)(2,1)} %w_send.1), custom_call_target="tpu_custom_call" | custom-call | flops 1811939328 | bytes 12582912 | tf_op jit(solution)/shard_map/input_grad/pallas_call | solution.py:48
  192.8 1.8 fusion
  194.6 1.5 collective-permute-start.20
  197.1 5.9 %collective-permute-done.25 = bf16[4,120,384]{2,1,0:T(8,128)(2,1)} collective-permute-done((bf16[4,120,384]{2,1,0:T(8,128)(2,1)S(1)}, bf16[4,120,384]{2,1,0:T(8,128)(2,1)}, u32[]{:S(2)}, u32[]{:S(2)}) %collective-permute-start.25) | collective-permute-done | bytes 368672 | tf_op jit(solution)/shard_map/ppermute | solution.py:518
  205.8 3.7 %collective-permute-start.28 = (bf16[120,384]{1,0:T(8,128)(2,1)S(1)}, bf16[120,384]{1,0:T(8,128)(2,1)S(1)}, u32[]{:S(2)}, u32[]{:S(2)}) collective-permute-start(bf16[120,384]{1,0:T(8,128)(2,1)S(1)} %get-tuple-element.146), channel_id=1, source_target_pairs={{0,24},{1,25},{2,26},{3,27},{4,28},{5,29},{6,30},{7,31},{8,16},{9,... | collective-permute-start | bytes 276488 | tf_op jit(solution)/shard_map/ppermute | solution.py:518
  210.7 6.4 %grad_reduce.1 = (bf16[2,4,96,384]{3,2,1,0:T(8,128)(2,1)S(1)}, bf16[2,4,96,384]{3,2,1,0:T(8,128)(2,1)S(1)}, bf16[2,4,96,384]{3,2,1,0:T(8,128)(2,1)S(1)}, bf16[2,4,96,384]{3,2,1,0:T(8,128)(2,1)S(1)}) custom-call(s32[9]{0:T(128)S(1)} %concatenate.29.scal.refs_0_, bf16[512,3072]{1,0:T(8,128)(2,1)} %get-tuple-element.104.a_own, ...), custom_call_target="tpu_custom_call" | custom-call | flops 2415919104 | bytes 9437184 | tf_op jit(solution)/shard_map/grad_reduce/pallas_call | solution.py:48
  217.2 1.6 collective-permute-start.37
  219.6 3.7 %collective-permute-start.23 = (bf16[120,384]{1,0:T(8,128)(2,1)S(1)}, bf16[120,384]{1,0:T(8,128)(2,1)S(1)}, u32[]{:S(2)}, u32[]{:S(2)}) collective-permute-start(bf16[120,384]{1,0:T(8,128)(2,1)S(1)} %get-tuple-element.149), channel_id=1, source_target_pairs={{0,24},{1,25},{2,26},{3,27},{4,28},{5,29},{6,30},{7,31},{8,16},{9,... | collective-permute-start | bytes 276488 | tf_op jit(solution)/shard_map/ppermute | solution.py:518
  225.4 2.0 collective-permute-done.22
  227.6 3.2 %collective-permute-done.37 = bf16[2,4,96,384]{3,2,1,0:T(8,128)(2,1)S(1)} collective-permute-done((bf16[2,4,96,384]{3,2,1,0:T(8,128)(2,1)S(1)}, bf16[2,4,96,384]{3,2,1,0:T(8,128)(2,1)S(1)}, u32[]{:S(2)}, u32[]{:S(2)}) %collective-permute-start.37) | collective-permute-done | bytes 589856 | tf_op jit(solution)/shard_map/ppermute | solution.py:518
  231.5 9.1 %collective-permute-done.32 = bf16[2,4,96,384]{3,2,1,0:T(8,128)(2,1)S(1)} collective-permute-done((bf16[2,4,96,384]{3,2,1,0:T(8,128)(2,1)S(1)}, bf16[2,4,96,384]{3,2,1,0:T(8,128)(2,1)S(1)}, u32[]{:S(2)}, u32[]{:S(2)}) %collective-permute-start.32) | collective-permute-done | bytes 589856 | tf_op jit(solution)/shard_map/ppermute | solution.py:518
  241.2 2.5 collective-permute-done.38
  245.0 3.4 %collective-permute-start.41 = (bf16[96,384]{1,0:T(8,128)(2,1)S(1)}, bf16[96,384]{1,0:T(8,128)(2,1)S(1)}, u32[]{:S(2)}, u32[]{:S(2)}) collective-permute-start(bf16[96,384]{1,0:T(8,128)(2,1)S(1)} %get-tuple-element.152), channel_id=1, source_target_pairs={{0,24},{1,25},{2,26},{3,27},{4,28},{5,29},{6,30},{7,31},{8,16},{9,... | collective-permute-start | bytes 221192 | tf_op jit(solution)/shard_map/ppermute | solution.py:518
  249.6 3.4 %collective-permute-start.36 = (bf16[96,384]{1,0:T(8,128)(2,1)S(1)}, bf16[96,384]{1,0:T(8,128)(2,1)S(1)}, u32[]{:S(2)}, u32[]{:S(2)}) collective-permute-start(bf16[96,384]{1,0:T(8,128)(2,1)S(1)} %get-tuple-element.155), channel_id=1, source_target_pairs={{0,24},{1,25},{2,26},{3,27},{4,28},{5,29},{6,30},{7,31},{8,16},{9,... | collective-permute-start | bytes 221192 | tf_op jit(solution)/shard_map/ppermute | solution.py:518
  253.7 2.6 collective-permute-done.35
  (183 shorter events, 41.1 us)
Async XLA Ops:
  8.4 15.2 %collective-permute-start = (bf16[7,128,128]{2,1,0:T(8,128)(2,1)S(1)}, bf16[7,128,128]{2,1,0:T(8,128)(2,1)S(1)}, u32[]{:S(2)}, u32[]{:S(2)}) collective-permute-start(bf16[7,128,128]{2,1,0:T(8,128)(2,1)S(1)} %get-tuple-element.70), channel_id=1, source_target_pairs={{0,1},{2,3},{4,5},{6,7},{8,9},{10,11},{12,13},{14,15},{16,17},{18,... | collective-permute-start | bytes 688136 | tf_op jit(solution)/shard_map/ppermute | solution.py:605
  66.4 26.0 %copy-start.13 = (f32[8,768]{1,0:T(8,128)}, f32[8,768]{1,0:T(8,128)S(1)}, u32[]{:S(2)}) copy-start(f32[8,768]{1,0:T(8,128)S(1)} %get-tuple-element.87) | copy-start | bytes 73732
  66.4 26.0 %copy-start.17 = (bf16[512,384]{1,0:T(8,128)(2,1)}, bf16[512,384]{1,0:T(8,128)(2,1)S(1)}, u32[]{:S(2)}) copy-start(bf16[512,384]{1,0:T(8,128)(2,1)S(1)} %get-tuple-element.98.c_own) | copy-start | bytes 1179652
  66.4 26.0 %copy-start.19 = (bf16[512,384]{1,0:T(8,128)(2,1)}, bf16[512,384]{1,0:T(8,128)(2,1)S(1)}, u32[]{:S(2)}) copy-start(bf16[512,384]{1,0:T(8,128)(2,1)S(1)} %get-tuple-element.99) | copy-start | bytes 1179652
  66.5 9.0 %collective-permute-start.1 = (bf16[7,128,128]{2,1,0:T(8,128)(2,1)S(1)}, bf16[7,128,128]{2,1,0:T(8,128)(2,1)S(1)}, u32[]{:S(2)}, u32[]{:S(2)}) collective-permute-start(bf16[7,128,128]{2,1,0:T(8,128)(2,1)S(1)} %get-tuple-element.83), channel_id=1, source_target_pairs={{1,0},{3,2},{5,4},{7,6},{9,8},{11,10},{13,12},{15,14},{17,16},{19,... | collective-permute-start | bytes 688136 | tf_op jit(solution)/shard_map/ppermute | solution.py:682
  92.5 21.7 %collective-permute-start.3 = (bf16[9,512,128]{2,1,0:T(8,128)(2,1)}, bf16[9,512,128]{2,1,0:T(8,128)(2,1)}, u32[]{:S(2)}, u32[]{:S(2)}) collective-permute-start(bf16[9,512,128]{2,1,0:T(8,128)(2,1)} %get-tuple-element.85.send), channel_id=1, source_target_pairs={{0,2},{1,3},{2,0},{3,1},{4,6},{5,7},{6,4},{7,5},{8,10},{9,11},{10,... | collective-permute-start | bytes 3538952 | tf_op jit(solution)/shard_map/ppermute | solution.py:518
  93.4 20.8 %collective-permute-start.2 = (bf16[4,192,512]{2,1,0:T(8,128)(2,1)S(1)}, bf16[4,192,512]{2,1,0:T(8,128)(2,1)}, u32[]{:S(2)}, u32[]{:S(2)}) collective-permute-start(bf16[4,192,512]{2,1,0:T(8,128)(2,1)S(1)} %bitcast.168), channel_id=1, source_target_pairs={{0,2},{1,3},{2,0},{3,1},{4,6},{5,7},{6,4},{7,5},{8,10},{9,11},{10,... | collective-permute-start | bytes 2359304 | tf_op jit(solution)/shard_map/ppermute | solution.py:518
  93.5 41.4 %collective-permute-start.16 = (bf16[3,512,512]{2,1,0:T(8,128)(2,1)}, bf16[3,512,512]{2,1,0:T(8,128)(2,1)}, u32[]{:S(2)}, u32[]{:S(2)}) collective-permute-start(bf16[3,512,512]{2,1,0:T(8,128)(2,1)} %get-tuple-element.96), channel_id=1, source_target_pairs={{0,2},{1,3},{2,0},{3,1},{4,6},{5,7},{6,4},{7,5},{8,10},{9,11},{10,... | collective-permute-start | bytes 4718600 | tf_op jit(solution)/shard_map/ppermute | solution.py:518
  94.2 38.5 %collective-permute-start.15 = (bf16[4,192,512]{2,1,0:T(8,128)(2,1)S(1)}, bf16[4,192,512]{2,1,0:T(8,128)(2,1)}, u32[]{:S(2)}, u32[]{:S(2)}) collective-permute-start(bf16[4,192,512]{2,1,0:T(8,128)(2,1)S(1)} %bitcast.164), channel_id=1, source_target_pairs={{0,2},{1,3},{2,0},{3,1},{4,6},{5,7},{6,4},{7,5},{8,10},{9,11},{10,... | collective-permute-start | bytes 2359304 | tf_op jit(solution)/shard_map/ppermute | solution.py:518
  95.8 39.0 %collective-permute-start.17 = (bf16[4,192,512]{2,1,0:T(8,128)(2,1)S(1)}, bf16[4,192,512]{2,1,0:T(8,128)(2,1)}, u32[]{:S(2)}, u32[]{:S(2)}) collective-permute-start(bf16[4,192,512]{2,1,0:T(8,128)(2,1)S(1)} %bitcast.166), channel_id=1, source_target_pairs={{0,2},{1,3},{2,0},{3,1},{4,6},{5,7},{6,4},{7,5},{8,10},{9,11},{10,... | collective-permute-start | bytes 2359304 | tf_op jit(solution)/shard_map/ppermute | solution.py:518
  119.3 13.3 %collective-permute-start.9 = (bf16[2,4,80,384]{3,2,1,0:T(8,128)(2,1)S(1)}, bf16[2,4,80,384]{3,2,1,0:T(8,128)(2,1)S(1)}, u32[]{:S(2)}, u32[]{:S(2)}) collective-permute-start(bf16[2,4,80,384]{3,2,1,0:T(8,128)(2,1)S(1)} %get-tuple-element.93), channel_id=1, source_target_pairs={{0,4},{1,5},{2,6},{3,7},{4,0},{5,1},{6,2},{7,3},{8,12},{9,13},{10,... | collective-permute-start | bytes 1474568 | tf_op jit(solution)/shard_map/ppermute | solution.py:518
  120.9 11.8 %collective-permute-start.18 = (bf16[512,384]{1,0:T(8,128)(2,1)S(1)}, bf16[512,384]{1,0:T(8,128)(2,1)S(1)}, u32[]{:S(2)}, u32[]{:S(2)}) collective-permute-start(bf16[512,384]{1,0:T(8,128)(2,1)S(1)} %copy-done.20), channel_id=1, source_target_pairs={{0,2},{1,3},{2,0},{3,1},{4,6},{5,7},{6,4},{7,5},{8,10},{9,11},{10,... | collective-permute-start | bytes 1179656 | tf_op jit(solution)/shard_map/ppermute | solution.py:518
  132.5 14.2 %collective-permute-start.4 = (bf16[2,4,80,384]{3,2,1,0:T(8,128)(2,1)S(1)}, bf16[2,4,80,384]{3,2,1,0:T(8,128)(2,1)S(1)}, u32[]{:S(2)}, u32[]{:S(2)}) collective-permute-start(bf16[2,4,80,384]{3,2,1,0:T(8,128)(2,1)S(1)} %get-tuple-element.91), channel_id=1, source_target_pairs={{0,1},{1,0},{2,3},{3,2},{4,5},{5,4},{6,7},{7,6},{8,9},{9,8},{10,11... | collective-permute-start | bytes 1474568 | tf_op jit(solution)/shard_map/ppermute | solution.py:518
  132.6 78.1 %collective-permute-start.30 = (bf16[512,3072]{1,0:T(8,128)(2,1)}, bf16[512,3072]{1,0:T(8,128)(2,1)}, u32[]{:S(2)}, u32[]{:S(2)}) collective-permute-start(bf16[512,3072]{1,0:T(8,128)(2,1)} %get-tuple-element.104.a_own), channel_id=1, source_target_pairs={{0,2},{1,3},{2,0},{3,1},{4,6},{5,7},{6,4},{7,5},{8,10},{9,11},{10,... | collective-permute-start | bytes 9437192 | tf_op jit(solution)/shard_map/ppermute | solution.py:518
  132.7 19.3 %collective-permute-start.10 = (bf16[4,80,384]{2,1,0:T(8,128)(2,1)S(1)}, bf16[4,80,384]{2,1,0:T(8,128)(2,1)S(1)}, u32[]{:S(2)}, u32[]{:S(2)}) collective-permute-start(bf16[4,80,384]{2,1,0:T(8,128)(2,1)S(1)} %fusion.5), channel_id=1, source_target_pairs={{0,1},{1,0},{2,3},{3,2},{4,5},{5,4},{6,7},{7,6},{8,9},{9,8},{10,11... | collective-permute-start | bytes 737288 | tf_op jit(solution)/shard_map/ppermute | solution.py:518
  142.7 27.5 %copy-start.9 = (bf16[2,4,120,384]{3,2,1,0:T(8,128)(2,1)}, bf16[2,4,120,384]{3,2,1,0:T(8,128)(2,1)S(1)}, u32[]{:S(2)}) copy-start(bf16[2,4,120,384]{3,2,1,0:T(8,128)(2,1)S(1)} %get-tuple-element.102) | copy-start | bytes 2211844
  142.7 48.5 %collective-permute-start.24 = (bf16[2,4,120,384]{3,2,1,0:T(8,128)(2,1)}, bf16[2,4,120,384]{3,2,1,0:T(8,128)(2,1)}, u32[]{:S(2)}, u32[]{:S(2)}) collective-permute-start(bf16[2,4,120,384]{3,2,1,0:T(8,128)(2,1)} %get-tuple-element.103), channel_id=1, source_target_pairs={{0,4},{1,5},{2,6},{3,7},{4,0},{5,1},{6,2},{7,3},{8,12},{9,13},{10,... | collective-permute-start | bytes 2211848 | tf_op jit(solution)/shard_map/ppermute | solution.py:518
  144.2 48.6 %collective-permute-start.19 = (bf16[2,4,120,384]{3,2,1,0:T(8,128)(2,1)}, bf16[2,4,120,384]{3,2,1,0:T(8,128)(2,1)}, u32[]{:S(2)}, u32[]{:S(2)}) collective-permute-start(bf16[2,4,120,384]{3,2,1,0:T(8,128)(2,1)} %get-tuple-element.101), channel_id=1, source_target_pairs={{0,1},{1,0},{2,3},{3,2},{4,5},{5,4},{6,7},{7,6},{8,9},{9,8},{10,11... | collective-permute-start | bytes 2211848 | tf_op jit(solution)/shard_map/ppermute | solution.py:518
  146.8 35.1 %copy-start.2 = (f32[512,768]{1,0:T(8,128)S(1)}, f32[512,768]{1,0:T(8,128)}, u32[]{:S(2)}) copy-start(f32[512,768]{1,0:T(8,128)} %get-tuple-element.80.first) | copy-start | bytes 4718596
  146.8 19.9 %collective-permute-start.5 = (bf16[4,80,384]{2,1,0:T(8,128)(2,1)S(1)}, bf16[4,80,384]{2,1,0:T(8,128)(2,1)S(1)}, u32[]{:S(2)}, u32[]{:S(2)}) collective-permute-start(bf16[4,80,384]{2,1,0:T(8,128)(2,1)S(1)} %fusion.4), channel_id=1, source_target_pairs={{0,4},{1,5},{2,6},{3,7},{4,0},{5,1},{6,2},{7,3},{8,12},{9,13},{10,... | collective-permute-start | bytes 737288 | tf_op jit(solution)/shard_map/ppermute | solution.py:518
  153.5 17.4 %collective-permute-start.11 = (bf16[80,384]{1,0:T(8,128)(2,1)S(1)}, bf16[80,384]{1,0:T(8,128)(2,1)}, u32[]{:S(2)}, u32[]{:S(2)}) collective-permute-start(bf16[80,384]{1,0:T(8,128)(2,1)S(1)} %get-tuple-element.159), channel_id=1, source_target_pairs={{0,8},{1,9},{2,10},{3,11},{4,12},{5,13},{6,14},{7,15},{8,0},{9,1},... | collective-permute-start | bytes 184328 | tf_op jit(solution)/shard_map/ppermute | solution.py:518
  166.7 5.5 %collective-permute-start.12 = (bf16[80,384]{1,0:T(8,128)(2,1)S(1)}, bf16[80,384]{1,0:T(8,128)(2,1)}, u32[]{:S(2)}, u32[]{:S(2)}) collective-permute-start(bf16[80,384]{1,0:T(8,128)(2,1)S(1)} %get-tuple-element.161), channel_id=1, source_target_pairs={{0,16},{1,17},{2,18},{3,19},{4,20},{5,21},{6,22},{7,23},{8,24},{9,... | collective-permute-start | bytes 184328 | tf_op jit(solution)/shard_map/ppermute | solution.py:518
  170.9 6.4 %collective-permute-start.13 = (bf16[80,384]{1,0:T(8,128)(2,1)}, bf16[80,384]{1,0:T(8,128)(2,1)}, u32[]{:S(2)}, u32[]{:S(2)}) collective-permute-start(bf16[80,384]{1,0:T(8,128)(2,1)} %get-tuple-element.160), channel_id=1, source_target_pairs={{0,24},{1,25},{2,26},{3,27},{4,28},{5,29},{6,30},{7,31},{8,16},{9,... | collective-permute-start | bytes 184328 | tf_op jit(solution)/shard_map/ppermute | solution.py:518
  172.2 5.7 %collective-permute-start.6 = (bf16[80,384]{1,0:T(8,128)(2,1)}, bf16[80,384]{1,0:T(8,128)(2,1)}, u32[]{:S(2)}, u32[]{:S(2)}) collective-permute-start(bf16[80,384]{1,0:T(8,128)(2,1)} %get-tuple-element.162), channel_id=1, source_target_pairs={{0,8},{1,9},{2,10},{3,11},{4,12},{5,13},{6,14},{7,15},{8,0},{9,1},... | collective-permute-start | bytes 184328 | tf_op jit(solution)/shard_map/ppermute | solution.py:518
  177.3 12.1 %collective-permute-start.7 = (bf16[80,384]{1,0:T(8,128)(2,1)}, bf16[80,384]{1,0:T(8,128)(2,1)S(1)}, u32[]{:S(2)}, u32[]{:S(2)}) collective-permute-start(bf16[80,384]{1,0:T(8,128)(2,1)} %get-tuple-element.164), channel_id=1, source_target_pairs={{0,16},{1,17},{2,18},{3,19},{4,20},{5,21},{6,22},{7,23},{8,24},{9,... | collective-permute-start | bytes 184328 | tf_op jit(solution)/shard_map/ppermute | solution.py:518
  177.9 11.5 %collective-permute-start.8 = (bf16[80,384]{1,0:T(8,128)(2,1)}, bf16[80,384]{1,0:T(8,128)(2,1)S(1)}, u32[]{:S(2)}, u32[]{:S(2)}) collective-permute-start(bf16[80,384]{1,0:T(8,128)(2,1)} %get-tuple-element.163), channel_id=1, source_target_pairs={{0,24},{1,25},{2,26},{3,27},{4,28},{5,29},{6,30},{7,31},{8,16},{9,... | collective-permute-start | bytes 184328 | tf_op jit(solution)/shard_map/ppermute | solution.py:518
  189.5 21.2 %collective-permute-start.31 = (bf16[512,384]{1,0:T(8,128)(2,1)}, bf16[512,384]{1,0:T(8,128)(2,1)S(1)}, u32[]{:S(2)}, u32[]{:S(2)}) collective-permute-start(bf16[512,384]{1,0:T(8,128)(2,1)} %get-tuple-element.106), channel_id=1, source_target_pairs={{0,2},{1,3},{2,0},{3,1},{4,6},{5,7},{6,4},{7,5},{8,10},{9,11},{10,... | collective-permute-start | bytes 1179656 | tf_op jit(solution)/shard_map/ppermute | solution.py:518
  190.6 5.5 %collective-permute-start.14 = (f32[80,384]{1,0:T(8,128)S(1)}, f32[80,384]{1,0:T(8,128)S(1)}, u32[]{:S(2)}, u32[]{:S(2)}) collective-permute-start(f32[80,384]{1,0:T(8,128)S(1)} %get-tuple-element.138), channel_id=1, source_target_pairs={{0,2},{1,3},{2,0},{3,1},{4,6},{5,7},{6,4},{7,5},{8,10},{9,11},{10,... | collective-permute-start | bytes 368648 | tf_op jit(solution)/shard_map/ppermute | solution.py:518
  192.3 10.7 %collective-permute-start.25 = (bf16[4,120,384]{2,1,0:T(8,128)(2,1)S(1)}, bf16[4,120,384]{2,1,0:T(8,128)(2,1)}, u32[]{:S(2)}, u32[]{:S(2)}) collective-permute-start(bf16[4,120,384]{2,1,0:T(8,128)(2,1)S(1)} %fusion.1), channel_id=1, source_target_pairs={{0,1},{1,0},{2,3},{3,2},{4,5},{5,4},{6,7},{7,6},{8,9},{9,8},{10,11... | collective-permute-start | bytes 1105928 | tf_op jit(solution)/shard_map/ppermute | solution.py:518
  194.6 10.5 %collective-permute-start.20 = (bf16[4,120,384]{2,1,0:T(8,128)(2,1)}, bf16[4,120,384]{2,1,0:T(8,128)(2,1)S(1)}, u32[]{:S(2)}, u32[]{:S(2)}) collective-permute-start(bf16[4,120,384]{2,1,0:T(8,128)(2,1)} %fusion), channel_id=1, source_target_pairs={{0,4},{1,5},{2,6},{3,7},{4,0},{5,1},{6,2},{7,3},{8,12},{9,13},{10,... | collective-permute-start | bytes 1105928 | tf_op jit(solution)/shard_map/ppermute | solution.py:518
  204.3 14.6 %collective-permute-start.26 = (bf16[120,384]{1,0:T(8,128)(2,1)S(1)}, bf16[120,384]{1,0:T(8,128)(2,1)S(1)}, u32[]{:S(2)}, u32[]{:S(2)}) collective-permute-start(bf16[120,384]{1,0:T(8,128)(2,1)S(1)} %get-tuple-element.145), channel_id=1, source_target_pairs={{0,8},{1,9},{2,10},{3,11},{4,12},{5,13},{6,14},{7,15},{8,0},{9,1},... | collective-permute-start | bytes 276488 | tf_op jit(solution)/shard_map/ppermute | solution.py:518
  204.3 15.3 %collective-permute-start.27 = (bf16[120,384]{1,0:T(8,128)(2,1)S(1)}, bf16[120,384]{1,0:T(8,128)(2,1)S(1)}, u32[]{:S(2)}, u32[]{:S(2)}) collective-permute-start(bf16[120,384]{1,0:T(8,128)(2,1)S(1)} %get-tuple-element.147), channel_id=1, source_target_pairs={{0,16},{1,17},{2,18},{3,19},{4,20},{5,21},{6,22},{7,23},{8,24},{9,... | collective-permute-start | bytes 276488 | tf_op jit(solution)/shard_map/ppermute | solution.py:518
  205.8 19.2 %collective-permute-start.28 = (bf16[120,384]{1,0:T(8,128)(2,1)S(1)}, bf16[120,384]{1,0:T(8,128)(2,1)S(1)}, u32[]{:S(2)}, u32[]{:S(2)}) collective-permute-start(bf16[120,384]{1,0:T(8,128)(2,1)S(1)} %get-tuple-element.146), channel_id=1, source_target_pairs={{0,24},{1,25},{2,26},{3,27},{4,28},{5,29},{6,30},{7,31},{8,16},{9,... | collective-permute-start | bytes 276488 | tf_op jit(solution)/shard_map/ppermute | solution.py:518
  217.2 13.6 %collective-permute-start.37 = (bf16[2,4,96,384]{3,2,1,0:T(8,128)(2,1)S(1)}, bf16[2,4,96,384]{3,2,1,0:T(8,128)(2,1)S(1)}, u32[]{:S(2)}, u32[]{:S(2)}) collective-permute-start(bf16[2,4,96,384]{3,2,1,0:T(8,128)(2,1)S(1)} %get-tuple-element.110), channel_id=1, source_target_pairs={{0,4},{1,5},{2,6},{3,7},{4,0},{5,1},{6,2},{7,3},{8,12},{9,13},{10,... | collective-permute-start | bytes 1769480 | tf_op jit(solution)/shard_map/ppermute | solution.py:518
  218.8 6.6 %collective-permute-start.21 = (bf16[120,384]{1,0:T(8,128)(2,1)S(1)}, bf16[120,384]{1,0:T(8,128)(2,1)S(1)}, u32[]{:S(2)}, u32[]{:S(2)}) collective-permute-start(bf16[120,384]{1,0:T(8,128)(2,1)S(1)} %get-tuple-element.148), channel_id=1, source_target_pairs={{0,8},{1,9},{2,10},{3,11},{4,12},{5,13},{6,14},{7,15},{8,0},{9,1},... | collective-permute-start | bytes 276488 | tf_op jit(solution)/shard_map/ppermute | solution.py:518
  218.9 8.5 %collective-permute-start.22 = (bf16[120,384]{1,0:T(8,128)(2,1)S(1)}, bf16[120,384]{1,0:T(8,128)(2,1)S(1)}, u32[]{:S(2)}, u32[]{:S(2)}) collective-permute-start(bf16[120,384]{1,0:T(8,128)(2,1)S(1)} %get-tuple-element.150), channel_id=1, source_target_pairs={{0,16},{1,17},{2,18},{3,19},{4,20},{5,21},{6,22},{7,23},{8,24},{9,... | collective-permute-start | bytes 276488 | tf_op jit(solution)/shard_map/ppermute | solution.py:518
  219.6 7.8 %collective-permute-start.23 = (bf16[120,384]{1,0:T(8,128)(2,1)S(1)}, bf16[120,384]{1,0:T(8,128)(2,1)S(1)}, u32[]{:S(2)}, u32[]{:S(2)}) collective-permute-start(bf16[120,384]{1,0:T(8,128)(2,1)S(1)} %get-tuple-element.149), channel_id=1, source_target_pairs={{0,24},{1,25},{2,26},{3,27},{4,28},{5,29},{6,30},{7,31},{8,16},{9,... | collective-permute-start | bytes 276488 | tf_op jit(solution)/shard_map/ppermute | solution.py:518
  225.0 15.6 %collective-permute-start.32 = (bf16[2,4,96,384]{3,2,1,0:T(8,128)(2,1)S(1)}, bf16[2,4,96,384]{3,2,1,0:T(8,128)(2,1)S(1)}, u32[]{:S(2)}, u32[]{:S(2)}) collective-permute-start(bf16[2,4,96,384]{3,2,1,0:T(8,128)(2,1)S(1)} %get-tuple-element.108), channel_id=1, source_target_pairs={{0,1},{1,0},{2,3},{3,2},{4,5},{5,4},{6,7},{7,6},{8,9},{9,8},{10,11... | collective-permute-start | bytes 1769480 | tf_op jit(solution)/shard_map/ppermute | solution.py:518
  227.5 3.9 %collective-permute-start.29 = (f32[120,384]{1,0:T(8,128)S(1)}, f32[120,384]{1,0:T(8,128)S(1)}, u32[]{:S(2)}, u32[]{:S(2)}) collective-permute-start(f32[120,384]{1,0:T(8,128)S(1)} %get-tuple-element.136), channel_id=1, source_target_pairs={{0,2},{1,3},{2,0},{3,1},{4,6},{5,7},{6,4},{7,5},{8,10},{9,11},{10,... | collective-permute-start | bytes 552968 | tf_op jit(solution)/shard_map/ppermute | solution.py:518
  230.9 12.8 %collective-permute-start.38 = (bf16[4,96,384]{2,1,0:T(8,128)(2,1)S(1)}, bf16[4,96,384]{2,1,0:T(8,128)(2,1)S(1)}, u32[]{:S(2)}, u32[]{:S(2)}) collective-permute-start(bf16[4,96,384]{2,1,0:T(8,128)(2,1)S(1)} %fusion.3), channel_id=1, source_target_pairs={{0,1},{1,0},{2,3},{3,2},{4,5},{5,4},{6,7},{7,6},{8,9},{9,8},{10,11... | collective-permute-start | bytes 884744 | tf_op jit(solution)/shard_map/ppermute | solution.py:518
  240.7 7.7 %collective-permute-start.33 = (bf16[4,96,384]{2,1,0:T(8,128)(2,1)S(1)}, bf16[4,96,384]{2,1,0:T(8,128)(2,1)S(1)}, u32[]{:S(2)}, u32[]{:S(2)}) collective-permute-start(bf16[4,96,384]{2,1,0:T(8,128)(2,1)S(1)} %fusion.2), channel_id=1, source_target_pairs={{0,4},{1,5},{2,6},{3,7},{4,0},{5,1},{6,2},{7,3},{8,12},{9,13},{10,... | collective-permute-start | bytes 884744 | tf_op jit(solution)/shard_map/ppermute | solution.py:518
  243.9 5.7 %collective-permute-start.39 = (bf16[96,384]{1,0:T(8,128)(2,1)S(1)}, bf16[96,384]{1,0:T(8,128)(2,1)S(1)}, u32[]{:S(2)}, u32[]{:S(2)}) collective-permute-start(bf16[96,384]{1,0:T(8,128)(2,1)S(1)} %get-tuple-element.151), channel_id=1, source_target_pairs={{0,8},{1,9},{2,10},{3,11},{4,12},{5,13},{6,14},{7,15},{8,0},{9,1},... | collective-permute-start | bytes 221192 | tf_op jit(solution)/shard_map/ppermute | solution.py:518
  244.0 9.7 %collective-permute-start.40 = (bf16[96,384]{1,0:T(8,128)(2,1)S(1)}, bf16[96,384]{1,0:T(8,128)(2,1)S(1)}, u32[]{:S(2)}, u32[]{:S(2)}) collective-permute-start(bf16[96,384]{1,0:T(8,128)(2,1)S(1)} %get-tuple-element.153), channel_id=1, source_target_pairs={{0,16},{1,17},{2,18},{3,19},{4,20},{5,21},{6,22},{7,23},{8,24},{9,... | collective-permute-start | bytes 221192 | tf_op jit(solution)/shard_map/ppermute | solution.py:518
  245.0 8.7 %collective-permute-start.41 = (bf16[96,384]{1,0:T(8,128)(2,1)S(1)}, bf16[96,384]{1,0:T(8,128)(2,1)S(1)}, u32[]{:S(2)}, u32[]{:S(2)}) collective-permute-start(bf16[96,384]{1,0:T(8,128)(2,1)S(1)} %get-tuple-element.152), channel_id=1, source_target_pairs={{0,24},{1,25},{2,26},{3,27},{4,28},{5,29},{6,30},{7,31},{8,16},{9,... | collective-permute-start | bytes 221192 | tf_op jit(solution)/shard_map/ppermute | solution.py:518
  248.5 5.2 %collective-permute-start.34 = (bf16[96,384]{1,0:T(8,128)(2,1)S(1)}, bf16[96,384]{1,0:T(8,128)(2,1)S(1)}, u32[]{:S(2)}, u32[]{:S(2)}) collective-permute-start(bf16[96,384]{1,0:T(8,128)(2,1)S(1)} %get-tuple-element.154), channel_id=1, source_target_pairs={{0,8},{1,9},{2,10},{3,11},{4,12},{5,13},{6,14},{7,15},{8,0},{9,1},... | collective-permute-start | bytes 221192 | tf_op jit(solution)/shard_map/ppermute | solution.py:518
  248.6 7.7 %collective-permute-start.35 = (bf16[96,384]{1,0:T(8,128)(2,1)S(1)}, bf16[96,384]{1,0:T(8,128)(2,1)S(1)}, u32[]{:S(2)}, u32[]{:S(2)}) collective-permute-start(bf16[96,384]{1,0:T(8,128)(2,1)S(1)} %get-tuple-element.156), channel_id=1, source_target_pairs={{0,16},{1,17},{2,18},{3,19},{4,20},{5,21},{6,22},{7,23},{8,24},{9,... | collective-permute-start | bytes 221192 | tf_op jit(solution)/shard_map/ppermute | solution.py:518
  249.6 6.7 %collective-permute-start.36 = (bf16[96,384]{1,0:T(8,128)(2,1)S(1)}, bf16[96,384]{1,0:T(8,128)(2,1)S(1)}, u32[]{:S(2)}, u32[]{:S(2)}) collective-permute-start(bf16[96,384]{1,0:T(8,128)(2,1)S(1)} %get-tuple-element.155), channel_id=1, source_target_pairs={{0,24},{1,25},{2,26},{3,27},{4,28},{5,29},{6,30},{7,31},{8,16},{9,... | collective-permute-start | bytes 221192 | tf_op jit(solution)/shard_map/ppermute | solution.py:518
  256.4 1.4 collective-permute-start.42
  (25 other events, 215.7 us)

commit v2 on v1

v2 whole, which is shorter than its diff:
```python
import functools
import math

import jax
import jax.numpy as jnp
from jax import lax
from jax.experimental import pallas as pl
from jax.experimental.pallas import tpu as pltpu
from jax.sharding import PartitionSpec as P

D = 768
PAIRS = 6
FF = 3072
LANES = 128
HALF = 64
BF = jnp.bfloat16
F32 = jnp.float32
AXES = ("dp", "head")
VMEM_LIMIT = 20 * 1024 * 1024
FF_BLOCK = 768
MATMUL_PER_US = 1.15e9
FF_STEPS = FF // FF_BLOCK


def dot(a, b):
    return jnp.dot(a, b, preferred_element_type=F32)


def dot_t(a, b):
    return lax.dot_general(a, b, (((0,), (0,)), ((), ())), preferred_element_type=F32)


def dot_r(a, b):
    return lax.dot_general(a, b, (((1,), (1,)), ((), ())), preferred_element_type=F32)


def call(kernel, name, scal, grid, ins, outs, scratch=(), us=1, vmem=VMEM_LIMIT):
    spec = lambda b, m: pl.BlockSpec(memory_space=pltpu.VMEM) if b is None else pl.BlockSpec(b, m)
    in_specs = [spec(b, m) for _, b, m in ins]
    out_specs = [spec(b, m) for _, _, b, m in outs]
    return pl.pallas_call(
        kernel,
        name=name,
        grid_spec=pltpu.PrefetchScalarGridSpec(
            num_scalar_prefetch=1,
            grid=grid,
            in_specs=in_specs,
            out_specs=out_specs,
            scratch_shapes=list(scratch),
        ),
        out_shape=[jax.ShapeDtypeStruct(s, d) for s, d, _, _ in outs],
        compiler_params=pltpu.CompilerParams(vmem_limit_bytes=vmem),
        cost_estimate=pl.CostEstimate(flops=int(us * MATMUL_PER_US), bytes_accessed=1, transcendentals=0),
    )(scal, *[a for a, _, _ in ins])


def lane_masks():
    lane = lax.broadcasted_iota(jnp.int32, (1, LANES), 1)
    even = (lane < HALF).astype(F32)
    return lane, even.astype(BF), (1.0 - even).astype(BF)


def both_heads(pair):
    lane, even, odd = lane_masks()
    return jnp.concatenate([pair * even, pair * odd], axis=0)


def own_lanes(stacked):
    rows = stacked.shape[0] // 2
    lane = lax.broadcasted_iota(jnp.int32, (1, LANES), 1)
    return jnp.where(lane < HALF, stacked[:rows], stacked[rows:])


def square_masks():
    row = lax.broadcasted_iota(jnp.int32, (LANES, LANES), 0)
    lane = lax.broadcasted_iota(jnp.int32, (LANES, LANES), 1)
    upper = row < HALF
    return lane, upper, upper == (lane < HALF)


def high_low(v):
    high = v.astype(BF).astype(F32)
    return high, v - high


def tables(scal, rows, seqs, tcol, trow):
    pos = lax.broadcasted_iota(jnp.int32, (1, rows), 1) + scal[seqs] * rows
    seg = jnp.zeros((1, rows), jnp.int32)
    first = jnp.zeros((1, rows), jnp.int32)
    length = jnp.ones((1, rows), jnp.int32)
    at_boundary = jnp.int32(0)
    begin = jnp.int32(0)
    for s in range(seqs):
        end = begin + scal[s]
        inside = (pos >= begin) & (pos < end)
        first = jnp.where(inside, begin, first)
        length = jnp.where(inside, jnp.maximum(scal[s], 1), length)
        seg = seg + (pos >= end).astype(jnp.int32)
        at_boundary = at_boundary + (rows - 1 >= end).astype(jnp.int32)
        begin = end
    live = (seg < seqs).astype(F32)
    angle = 0.5 * math.pi * (pos - first).astype(F32) / length.astype(F32)
    cos_w = jnp.cos(angle) * live
    sin_w = jnp.sin(angle) * live
    crossing = (seg == at_boundary).astype(F32)
    which = lax.broadcasted_iota(jnp.int32, (LANES, rows), 0)
    table = jnp.zeros((LANES, rows), F32)
    for n, entry in enumerate((cos_w, sin_w, seg.astype(F32), cos_w * crossing, sin_w * crossing)):
        table = jnp.where(which == n, entry, table)
    trow[...] = table[:8]
    tcol[...] = table.T


def pack_state(both, norm_cos, norm_sin, pair, norms):
    lane, upper, diag = square_masks()
    packed = jnp.where(diag, both[:LANES, :LANES], pltpu.roll(both[LANES:, :LANES], HALF, 1))
    cos_high, cos_low = high_low(norm_cos)
    sin_high, sin_low = high_low(norm_sin)
    for n, part in enumerate((cos_high, cos_low, sin_high, sin_low)):
        norms = jnp.where(lane == 4 * pair + n, part, norms)
    return packed.astype(BF), norms


def unpack_state(state_ref, pair):
    lane, upper, diag = square_masks()
    packed = state_ref[pair].astype(F32)
    norms = state_ref[PAIRS].astype(F32)
    of_cos = jnp.where(diag, packed, 0.0)
    of_sin = jnp.where(diag, pltpu.roll(packed, HALF, 1), 0.0)
    pick = lambda n: jnp.sum(
        jnp.where((lane == 4 * pair + n) | (lane == 4 * pair + n + 1), norms, 0.0), axis=1, keepdims=True
    )
    return of_cos, of_sin, pick(0), pick(2)


def kv_kernel(seqs, scal, tok, wk, wv, bk, bv, rk_o, v_o, st_o, tcol, trow, norms):
    step = pl.program_id(0)
    rows = tok.shape[0]

    @pl.when(step == 0)
    def _():
        tables(scal, rows, seqs, tcol, trow)
        norms[...] = jnp.zeros_like(norms)

    rk = jnp.maximum(dot(tok[...], wk[...]) + bk[...].astype(F32), 0.0).astype(BF)
    v = (dot(tok[...], wv[...]) + bv[...].astype(F32)).astype(BF)
    rk_o[...] = rk
    v_o[...] = v
    cos_b, sin_b = tcol[:, 3:4], tcol[:, 4:5]
    ones = jnp.ones((rows, LANES), BF)
    for n in range(2):
        pair = 2 * step + n
        cols = slice(n * LANES, (n + 1) * LANES)
        kp = rk[:, cols].astype(F32)
        left = jnp.concatenate([(kp * cos_b).astype(BF), (kp * sin_b).astype(BF)], axis=1)
        both = dot_t(left, jnp.concatenate([v[:, cols], ones], axis=1))
        packed, new_norms = pack_state(both, both[:LANES, LANES:], both[LANES:, LANES:], pair, norms[...])
        st_o[pair] = packed
        norms[...] = new_norms

    st_o[PAIRS] = norms[...].astype(BF)


def weights_block(tcol, trow, transposed):
    rows = tcol.shape[0]
    down = lax.broadcasted_iota(jnp.int32, (rows, rows), 0)
    along = lax.broadcasted_iota(jnp.int32, (rows, rows), 1)
    same = tcol[:, 2:3] == trow[2:3, :]
    causal = (down <= along) if transposed else (along <= down)
    value = tcol[:, 0:1] * trow[0:1, :] + tcol[:, 1:2] * trow[1:2, :]
    return jnp.where(same & causal, value, 0.0)


def weigh(stacked, weights):
    rows = weights.shape[0]
    return jnp.concatenate([stacked[:rows] * weights, stacked[rows:] * weights], axis=0).astype(BF)


def local_kernel(scal, tok, wq, bq, rk, v, tcol, trow, rq_o, num_o, den_o, weights):
    step = pl.program_id(0)
    rows = tok.shape[0]
    mid = rows // 2

    @pl.when(step == 0)
    def _():
        weights[...] = weights_block(tcol, trow, False)

    rq = jnp.maximum(dot(tok[...], wq[...]) + bq[...].astype(F32), 0.0).astype(BF)
    rq_o[...] = rq
    ones = jnp.ones((rows, LANES), BF)
    for n in range(2):
        cols = slice(n * LANES, (n + 1) * LANES)
        kp = rk[:, cols]
        values = jnp.concatenate([v[:, cols], ones], axis=1)
        first = weigh(dot_r(both_heads(rq[:, cols]), kp[:mid]), weights[:, :mid])
        second = weigh(dot_r(both_heads(rq[mid:, cols]), kp[mid:]), weights[mid:, mid:])
        sums = dot(first, values[:mid])
        late = dot(second, values[mid:])
        for own, out in ((slice(0, LANES), num_o), (slice(LANES, 2 * LANES), den_o)):
            total = own_lanes(sums[:, own])
            out[:mid, cols] = total[:mid]
            out[mid:, cols] = total[mid:] + own_lanes(late[:, own])


def normalise(entries):
    mean = jnp.mean(entries, axis=1, keepdims=True)
    centred = entries - mean
    var = jnp.mean(centred * centred, axis=1, keepdims=True)
    scale = lax.rsqrt(var + 1e-05)
    return centred * scale, scale


def merge_heads(
    head_at, scal, rq, num, den, st, tcol, tok, w_merge, b_merge, gain, bias, b_red,
    att_o, inv_o, mixed_o, xhat_o, scale_o, normed_o, acc_o,
):
    cross = (scal[head_at] == 1).astype(F32)
    cos_b, sin_b = tcol[:, 3:4] * cross, tcol[:, 4:5] * cross
    sq_lane, upper, diag = square_masks()
    for pair in range(PAIRS):
        cols = slice(pair * LANES, (pair + 1) * LANES)
        qp = rq[:, cols].astype(F32)
        of_cos, of_sin, norm_cos, norm_sin = unpack_state(st, pair)
        top = jnp.concatenate([of_cos, jnp.where(diag, norm_cos, 0.0)], axis=1)
        low = jnp.concatenate([of_sin, jnp.where(diag, norm_sin, 0.0)], axis=1)
        right = jnp.concatenate([top, low], axis=0).astype(BF)
        left = jnp.concatenate([(qp * cos_b).astype(BF), (qp * sin_b).astype(BF)], axis=1)
        prior = dot(left, right)
        inverse = 1.0 / (den[:, cols] + prior[:, LANES:] + 1.0)
        attended = (num[:, cols] + prior[:, :LANES]) * inverse
        att_o[:, cols] = attended
        inv_o[:, cols] = inverse
        mixed_o[:, cols] = attended.astype(BF)
    first_in = tok[...].astype(F32) + dot(mixed_o[...], w_merge[...]) + b_merge[...].astype(F32)
    xhat, scale = normalise(first_in)
    normed = xhat * gain[...].astype(F32) + bias[...].astype(F32)
    xhat_o[...] = xhat
    scale_o[...] = jnp.broadcast_to(scale, scale_o.shape)
    normed_o[...] = normed.astype(BF)
    acc_o[...] = normed + b_red[...].astype(F32)


def expand_reduce(normed, w_exp, b_exp, w_red, act_o, slope_o):
    pre = dot(normed[...], w_exp[...]) + b_exp[...].astype(F32)
    cdf = 0.5 + 0.5 * lax.erf(pre * (2.0**-0.5))
    pdf = jnp.exp(-0.5 * pre * pre) * (1.0 / math.sqrt(2.0 * math.pi))
    act = (pre * cdf).astype(BF)
    act_o[...] = act
    slope_o[...] = (cdf + pre * pdf).astype(BF)
    return dot(act, w_red[...])


def ffn_kernel(head_at, scal, *refs):
    w_exp, b_exp, w_red = refs[11:14]
    normed_o, acc_o, act_o, slope_o = refs[19:]

    @pl.when(pl.program_id(0) == 0)
    def _():
        merge_heads(head_at, scal, *refs[:11], *refs[14:21])

    acc_o[...] += expand_reduce(normed_o, w_exp, b_exp, w_red, act_o, slope_o)


def second_kernel(core_at, scal, second, cot, gain, bias, out_o, grad_o, full_o, keep_o, send_o, sums_o):
    xhat, scale = normalise(second[...])
    gain_w = gain[...].astype(F32)
    out_o[...] = (xhat * gain_w + bias[...].astype(F32)).astype(BF)
    cot_w = cot[...].astype(F32)
    t = cot_w * gain_w
    grad = scale * (
        t - jnp.mean(t, axis=1, keepdims=True) - xhat * jnp.mean(t * xhat, axis=1, keepdims=True)
    )
    low = grad.astype(BF)
    grad_o[...] = grad
    full_o[...] = low
    first = scal[core_at] == 0
    half = D // 2
    left, right = grad[:, :half], grad[:, half:]
    keep_o[...] = jnp.where(first, left, right).astype(BF)
    send_o[...] = jnp.where(first, right, left).astype(BF)
    sums_o[0:1] = jnp.sum(cot_w * xhat, axis=0, keepdims=True)
    sums_o[1:2] = jnp.sum(cot_w, axis=0, keepdims=True)
    sums_o[2:3] = jnp.sum(low.astype(F32), axis=0, keepdims=True)


def head_lanes(pair, lane, first):
    at = 4 * pair + jnp.where(first, 0, 2)
    return (lane == at) | (lane == at + 1)


def back_step(full, slope, w_exp, w_red, out_o, bexp_o):
    pre_grad = (dot_r(full[...], w_red[...]) * slope[...].astype(F32)).astype(BF)
    bexp_o[...] = jnp.sum(pre_grad.astype(F32), axis=0, keepdims=True)
    out_o[0] = pre_grad
    return dot_r(pre_grad, w_exp[...])


def back_sent_kernel(scal, full, slope, w_exp, w_red, grad2, sent_o, bexp_o, acc):
    @pl.when(pl.program_id(0) == 0)
    def _():
        acc[...] = grad2[...]

    acc[...] += back_step(full, slope, w_exp, w_red, sent_o, bexp_o)


def back_kernel(
    core_at, scal, full, slope, w_exp, w_red, acc_in, gain, xhat, scale, w_merge, att, inv, rq, tcol,
    kept_o, first_o, mk_o, ms_o, w_o, e_o, st_o, bexp_o, sums_o,
    acc,
):
    step = pl.program_id(0)

    @pl.when(step == 0)
    def _():
        acc[...] = acc_in[...]

    acc[...] += back_step(full, slope, w_exp, w_red, kept_o, bexp_o)

    @pl.when(step == pl.num_programs(0) - 1)
    def _():
        grad_normed = acc[...]
        xh = xhat[...]
        t = grad_normed * gain[...].astype(F32)
        first = scale[:, 0:1] * (
            t - jnp.mean(t, axis=1, keepdims=True) - xh * jnp.mean(t * xh, axis=1, keepdims=True)
        )
        low = first.astype(BF)
        first_o[...] = first
        sums_o[0:1] = jnp.sum(grad_normed * xh, axis=0, keepdims=True)
        sums_o[1:2] = jnp.sum(grad_normed, axis=0, keepdims=True)
        sums_o[2:3] = jnp.sum(low.astype(F32), axis=0, keepdims=True)
        is_first = scal[core_at] == 0
        left, right = first[:, : D // 2], first[:, D // 2 :]
        mk_o[...] = jnp.where(is_first, left, right).astype(BF)
        ms_o[...] = jnp.where(is_first, right, left).astype(BF)
        cos_b, sin_b = tcol[:, 3:4], tcol[:, 4:5]
        w = (dot_r(low, w_merge[...]).astype(BF).astype(F32) * inv[...]).astype(BF)
        w_o[...] = w
        high, rest = high_low(w.astype(F32) * att[...])
        column = lax.broadcasted_iota(jnp.int32, (D, LANES), 0)
        target = lax.broadcasted_iota(jnp.int32, (D, LANES), 1)
        picks = (target == 2 * (column // HALF)).astype(F32).astype(BF)
        e_high, e_low = high_low(-(dot(high.astype(BF), picks) + dot(rest.astype(BF), picks)))
        e = (e_high + pltpu.roll(e_low, 1, 1)).astype(BF)
        e_o[...] = e
        norms = jnp.zeros((LANES, LANES), F32)
        sq_lane, upper, diag = square_masks()
        for pair in range(PAIRS):
            cols = slice(pair * LANES, (pair + 1) * LANES)
            qp = rq[:, cols].astype(F32)
            left = jnp.concatenate([(qp * cos_b).astype(BF), (qp * sin_b).astype(BF)], axis=1)
            both = dot_t(left, jnp.concatenate([w[:, cols], e], axis=1))
            mine = head_lanes(pair, sq_lane, upper)
            norm = lambda part: jnp.sum(jnp.where(mine, part, 0.0), axis=1, keepdims=True)
            packed, norms = pack_state(both, norm(both[:LANES, LANES:]), norm(both[LANES:, LANES:]), pair, norms)
            st_o[pair] = packed
        st_o[PAIRS] = norms.astype(BF)


def attn_back_kernel(
    head_at, core_at, scal, rq, rk, v, w, e, prior, later, tcol, trow,
    pk_o, ps_o, sums_o,
    weights, weights_t,
):
    pair = pl.program_id(0)
    rows = rq.shape[0]
    mid = rows // 2

    @pl.when(pair == 0)
    def _():
        weights[...] = weights_block(tcol, trow, False)
        weights_t[...] = weights_block(tcol, trow, True)

    qp, kp, vp, wp = rq[...], rk[...], v[...], w[...]
    lane, even, odd = lane_masks()
    of_even = ((lane == 4 * pair) | (lane == 4 * pair + 1)).astype(F32).astype(BF)
    of_odd = ((lane == 4 * pair + 2) | (lane == 4 * pair + 3)).astype(F32).astype(BF)
    ones = jnp.ones((rows, LANES), BF)
    we = jnp.concatenate([wp, e[...]], axis=1)
    by_head = (jnp.concatenate([even, of_even], axis=1), jnp.concatenate([odd, of_odd], axis=1))
    ve = jnp.concatenate([vp, ones], axis=1)
    stack = lambda a, lo, hi: jnp.concatenate([a[lo:hi] * m for m in by_head], axis=0)

    grads = weigh(dot_r(stack(we, 0, rows), ve[:mid]), weights[:, :mid])
    dq = own_lanes(dot(grads, kp[:mid]))
    grads = weigh(dot_r(stack(we, mid, rows), ve[mid:]), weights[mid:, mid:])
    dq_late = own_lanes(dot(grads, kp[mid:]))

    grads = weigh(dot_r(stack(ve, 0, rows), we[mid:]), weights_t[:, mid:])
    dk = own_lanes(dot(grads, qp[mid:]))
    grads = weigh(dot_r(stack(ve, 0, mid), we[:mid]), weights_t[:mid, :mid])
    dk_early = own_lanes(dot(grads, qp[:mid]))

    scores = weigh(dot_r(both_heads(kp), qp[mid:]), weights_t[:, mid:])
    dv = own_lanes(dot(scores, wp[mid:]))
    scores = weigh(dot_r(both_heads(kp[:mid]), qp[:mid]), weights_t[:mid, :mid])
    dv_early = own_lanes(dot(scores, wp[:mid]))

    dq = jnp.concatenate([dq[:mid], dq[mid:] + dq_late], axis=0)
    dk = jnp.concatenate([dk[:mid] + dk_early, dk[mid:]], axis=0)
    dv = jnp.concatenate([dv[:mid] + dv_early, dv[mid:]], axis=0)

    sq_lane, upper, diag = square_masks()
    cos_b, sin_b = tcol[:, 3:4], tcol[:, 4:5]
    is_late = (scal[head_at] == 1).astype(F32)
    early = 1.0 - is_late

    def with_norms(parts, where):
        side = lambda total, norm: jnp.concatenate([total, jnp.where(where, norm, 0.0)], axis=1)
        of_cos, of_sin, norm_cos, norm_sin = parts
        return jnp.concatenate([side(of_cos, norm_cos), side(of_sin, norm_sin)], axis=0).astype(BF)

    prior_parts = unpack_state(prior, pair)
    into = dot_r(we, with_norms(prior_parts, head_lanes(pair, sq_lane, upper)))
    dq = dq + is_late * (cos_b * into[:, :LANES] + sin_b * into[:, LANES:])
    later_parts = unpack_state(later, pair)
    into = dot_r(ve, with_norms(later_parts, sq_lane == 0))
    dk = dk + early * (cos_b * into[:, :LANES] + sin_b * into[:, LANES:])
    kw = kp.astype(F32)
    left = jnp.concatenate([(kw * (cos_b * early)).astype(BF), (kw * (sin_b * early)).astype(BF)], axis=1)
    dv = dv + dot(left, jnp.concatenate(later_parts[:2], axis=0).astype(BF))

    dq = jnp.where(qp.astype(F32) > 0, dq, 0.0).astype(BF)
    dk = jnp.where(kw > 0, dk, 0.0).astype(BF)
    dv = dv.astype(BF)
    blocks = 3 * PAIRS // 2
    for n, part in enumerate((dq, dk, dv)):
        sums_o[n] = jnp.broadcast_to(jnp.sum(part.astype(F32), axis=0, keepdims=True), sums_o.shape[1:])
        at = n * PAIRS + pair
        mine = (at >= blocks) == (scal[core_at] == 1)
        slot = lax.rem(at, blocks)

        @pl.when(mine)
        def _():
            pk_o[slot] = part

        @pl.when(jnp.logical_not(mine))
        def _():
            ps_o[slot] = part


def input_kernel(scal, first, keep, send, w_keep, w_send, out_o):
    @pl.when(pl.program_id(0) == 0)
    def _():
        out_o[...] = first[...]

    left = lambda ref: jnp.concatenate([ref[n] for n in range(ref.shape[0])], axis=1)
    out_o[...] += dot_r(left(keep), w_keep[...]) + dot_r(left(send), w_send[...])


def place(values, piece_rows, tz, tys, x, y, z, extra, outs):
    xk, xs, yk, ys = outs
    width = xk.shape[-1]
    slot_z = tz ^ z
    pieces = {}
    at = 0
    for ty in tys:
        for tc in range(2):
            for tx in range(2):
                part = values[at * piece_rows : (at + 1) * piece_rows]
                blocks = [part[:, n : n + width] for n in range(0, part.shape[1], width)]
                if extra is not None:
                    blocks.append(extra[at])
                pieces[ty, tc, tx] = jnp.concatenate(blocks, axis=0) if len(blocks) > 1 else blocks[0]
                at += 1
    for ty in tys:
        slot = ty ^ y
        a, b = pieces[ty, 0, 0], pieces[ty, 0, 1]
        xk[slot, slot_z] = jnp.where(x == 0, a, b).astype(BF)
        xs[slot, slot_z] = jnp.where(x == 0, b, a).astype(BF)
    return pieces


def place_y(pieces, tz, tys, x, y, z, outs):
    xk, xs, yk, ys = outs
    slot_z = tz ^ z
    for tx in range(2):
        slot = tx ^ x
        a, b = pieces[0, 1, tx], pieces[1, 1, tx]
        yk[slot, slot_z] = jnp.where(y == 0, a, b).astype(BF)
        ys[slot, slot_z] = jnp.where(y == 0, b, a).astype(BF)


def reduce_grad_kernel(pos_at, scal, a_own, a_oth, b_own, b_oth, *outs):
    tz = pl.program_id(0)
    x, y, z = (scal[pos_at + n] for n in range(3))
    values = dot_t(a_own[...], b_own[...]) + dot_t(a_oth[...], b_oth[...])
    piece_rows = values.shape[0] // 8
    pieces = place(values, piece_rows, tz, (0, 1), x, y, z, None, outs)
    place_y(pieces, tz, (0, 1), x, y, z, outs)


def expand_grad_kernel(pos_at, scal, a_own, a_oth, b_own, b_oth, m_own, m_oth, c_own, c_oth, *outs):
    tz = pl.program_id(0)
    x, y, z = (scal[pos_at + n] for n in range(3))
    an, ao = a_own[0], a_oth[0]
    parts = [dot(an, b_own[n]) + dot(ao, b_oth[n]) for n in range(b_own.shape[0])]
    parts.append(dot(m_own[0], c_own[...]) + dot(m_oth[0], c_oth[...]))
    values = jnp.concatenate(parts, axis=1)
    pieces = place(values, values.shape[0] // 8, tz, (0, 1), x, y, z, None, outs)
    place_y(pieces, tz, (0, 1), x, y, z, outs)


def share_lanes(entries, devices, at, width):
    n = entries.shape[1]
    share = n // devices
    owner = lax.broadcasted_iota(jnp.int32, (devices, n), 0)
    column = lax.broadcasted_iota(jnp.int32, (devices, n), 1)
    mine = (column >= owner * share) & (column < (owner + 1) * share)
    high, low = high_low(jnp.where(mine, entries, 0.0))
    both = jnp.concatenate([high, low], axis=0).astype(BF)
    source = lax.broadcasted_iota(jnp.int32, (n, width), 0)
    target = lax.broadcasted_iota(jnp.int32, (n, width), 1)
    picks = (target >= at) & (target < at + share) & (lax.rem(source, share) == target - at)
    spread = dot(both, picks.astype(F32).astype(BF))
    return spread[:devices] + spread[devices:]


def heads_grad_kernel(
    pos_at, scal, a_own, a_oth, b_own, b_oth, sums_q, sums_k, sums_v, sums_1, sums_e, sums_2, *refs, devices
):
    outs, table = refs[:-1], refs[-1]
    tz = pl.program_id(0)
    x, y, z = (scal[pos_at + n] for n in range(3))
    width = outs[0].shape[-1]

    @pl.when(tz == 0)
    def _():
        scores = jnp.concatenate([sums_q[0, 0:1], sums_k[0, 0:1]], axis=1)
        total = jnp.zeros((devices, width), F32)
        at = 0
        for entries in (
            scores, sums_v[0, 0:1], sums_1[2:3], sums_1[0:1], sums_1[1:2],
            sums_e[...], sums_2[2:3], sums_2[0:1], sums_2[1:2],
        ):
            total = total + share_lanes(entries, devices, at, width)
            at += entries.shape[1] // devices
        table[...] = total

    join = lambda ref: jnp.concatenate([ref[n] for n in range(ref.shape[0])], axis=1)
    values = dot(a_own[0], join(b_own)) + dot(a_oth[0], join(b_oth))
    line = lax.broadcasted_iota(jnp.int32, (8, width), 0)
    rows8 = table[pl.ds(pl.multiple_of(tz * 8, 8), 8)]
    extra = []
    for n in range(8):
        high, low = high_low(rows8[n : n + 1])
        extra.append(jnp.where(line == 0, high, jnp.where(line == 1, low, 0.0)))
    pieces = place(values, values.shape[0] // 8, tz, (0, 1), x, y, z, extra, outs)
    place_y(pieces, tz, (0, 1), x, y, z, outs)


class Ring:
    def __init__(self, n_dp):
        self.n_dp = n_dp
        self.devices = 2 * n_dp

    def swap(self, value, bits):
        return lax.ppermute(value, AXES, [(i, i ^ bits) for i in range(self.devices)])

    def core(self, value):
        return self.swap(value, 2)

    def x(self, value):
        return self.swap(value, 1)

    def y(self, value):
        return self.swap(value, 4)

    def z(self, value, step):
        return self.swap(value, 8 * step)


def add_first_kernel(scal, xk, xr, yk, yr, xn, yn):
    wide = lambda ref: ref[0].astype(F32)
    xn[...] = (wide(xk) + wide(xr)).astype(BF)
    yn[...] = (wide(yk) + wide(yr)).astype(BF)


def add_second_kernel(scal, xk, xr, xm, yk, yr, ym, own, z1, z2, z3):
    for n, (keep, got, more) in enumerate(((xk, xr, xm), (yk, yr, ym))):
        total = lambda k: keep[0, k].astype(F32) + got[0, k].astype(F32) + more[k].astype(F32)
        own[n] = total(0)
        for k, out in ((1, z1), (2, z2), (3, z3)):
            out[n] = total(k).astype(BF)


def add_last_kernel(core_at, scal, own, z1, z2, z3, keep, send):
    first = scal[core_at] == 0
    total = lambda n: own[n] + z1[n].astype(F32) + z2[n].astype(F32) + z3[n].astype(F32)
    of_first, of_second = total(0), total(1)
    keep[...] = jnp.where(first, of_first, of_second)
    send[...] = jnp.where(first, of_second, of_first)


class Scatter:
    def __init__(self, ring, core_at, name, sent):
        self.ring, self.core_at, self.name = ring, core_at, name
        self.xk, self.xs, self.yk, self.ys = sent

    def send(self):
        self.xr, self.yr = self.ring.x(self.xs), self.ring.y(self.ys)

    def first(self, scal):
        shape = self.xk.shape[1:]
        part = lambda a: (a, (1,) + shape, lambda j, s: (1, 0, 0, 0))
        xn, yn = call(
            add_first_kernel, self.name + "_add1", scal, (1,), [part(a) for a in (self.xk, self.xr, self.yk, self.yr)],
            [(shape, BF, None, None)] * 2,
        )
        self.xn, self.yn = xn, yn
        return xn

    def send_first(self):
        self.xm, self.ym = self.ring.y(self.xn), self.ring.x(self.yn)

    def second(self, scal, us=1):
        shape = self.xk.shape[1:]
        piece = (2,) + shape[1:]
        part = lambda a: (a, (1,) + shape, lambda j, s: (0, 0, 0, 0))
        whole = lambda a: (a, None, None)
        self.own, *self.sends = call(
            add_second_kernel, self.name + "_add2", scal, (1,),
            [part(self.xk), part(self.xr), whole(self.xm), part(self.yk), part(self.yr), whole(self.ym)],
            [(piece, F32, None, None)] + [(piece, BF, None, None)] * 3, us=us,
        )
        return self.own

    def send_second(self):
        self.arrived = [self.ring.z(v, k + 1) for k, v in enumerate(self.sends)]

    def last(self, scal):
        piece = self.own.shape[1:]
        keep, send = call(
            functools.partial(add_last_kernel, self.core_at), self.name + "_add3", scal, (1,),
            [(a, None, None) for a in (self.own, *self.arrived)], [(piece, F32, None, None)] * 2,
        )
        return keep, self.ring.core(send)


def after(value, *others):
    return lax.optimization_barrier((value,) + others)[0]


def halves(first_core, own, other):
    left = jnp.where(first_core, own, other)
    right = jnp.where(first_core, other, own)
    return jnp.concatenate([left, right], axis=1)


def columns(part, rows, blocks):
    return part.reshape(blocks, rows, part.shape[-1]).transpose(1, 0, 2).reshape(rows, -1)


def transposed_pieces(value):
    return value.T.reshape(4, D // 4, value.shape[0])


def per_device(
    tokens, w_heads, b_heads, w_merge, b_merge, gain_first, bias_first, w_expand, b_expand,
    w_reduce, b_reduce, gain_second, bias_second, seq_lengths, cotangent,
):
    rows = tokens.shape[0]
    seqs = seq_lengths.shape[1]
    n_dp = lax.axis_size("dp")
    ring = Ring(n_dp)
    head = lax.axis_index("head")
    dp = lax.axis_index("dp")
    core = dp % 2
    place_of = jnp.stack([head, core, head, (dp // 2) % 2, dp // 4]).astype(jnp.int32)
    scal = jnp.concatenate([seq_lengths[0].astype(jnp.int32), place_of])
    head_at, core_at, pos_at = seqs, seqs + 1, seqs + 2
    first_core = core == 0
    line = lambda v: v.reshape(1, -1)
    b_heads, b_merge, gain_first, bias_first, b_expand, b_reduce, gain_second, bias_second = map(
        line, (b_heads, b_merge, gain_first, bias_first, b_expand, b_reduce, gain_second, bias_second)
    )
    wide_shape = (rows, D)
    quarter = 256

    rk, v, state, tcol, trow = call(
        functools.partial(kv_kernel, seqs), "keys_values", scal, (3,),
        [
            (tokens, None, None),
            (w_heads, (D, quarter), lambda j, s: (0, 3 + j)),
            (w_heads, (D, quarter), lambda j, s: (0, 6 + j)),
            (b_heads, (1, quarter), lambda j, s: (0, 3 + j)),
            (b_heads, (1, quarter), lambda j, s: (0, 6 + j)),
        ],
        [
            (wide_shape, BF, (rows, quarter), lambda j, s: (0, j)),
            (wide_shape, BF, (rows, quarter), lambda j, s: (0, j)),
            ((PAIRS + 1, LANES, LANES), BF, None, None),
            ((rows, LANES), F32, None, None),
            ((8, rows), F32, None, None),
        ],
        [pltpu.VMEM((LANES, LANES), F32)],
        us=4,
    )
    forward = [(i, i + 1) for i in range(0, 2 * n_dp, 2)]
    backward = [(b, a) for a, b in forward]
    prior = lax.ppermute(state, AXES, forward)

    fast = n_dp == 16
    order = scal
    if fast:
        tokens_t = transposed_pieces(tokens)
        tokens_o = ring.core(tokens_t)
    rq, num, den = call(
        local_kernel, "local_attention", scal, (3,),
        [
            (tokens, None, None),
            (w_heads, (D, quarter), lambda j, s: (0, j)),
            (b_heads, (1, quarter), lambda j, s: (0, j)),
            (rk, (rows, quarter), lambda j, s: (0, j)),
            (v, (rows, quarter), lambda j, s: (0, j)),
            (tcol, None, None),
            (trow, None, None),
        ],
        [
            (wide_shape, BF, (rows, quarter), lambda j, s: (0, j)),
            (wide_shape, F32, (rows, quarter), lambda j, s: (0, j)),
            (wide_shape, F32, (rows, quarter), lambda j, s: (0, j)),
        ],
        [pltpu.VMEM((rows, rows), F32)],
        us=6,
    )

    if fast:
        order = after(scal, tokens_o)
    att, inv, mixed, xhat, scale, normed, second, act, slope = call(
        functools.partial(ffn_kernel, head_at), "feed_forward", order, (FF_STEPS,),
        [
            (rq, None, None), (num, None, None), (den, None, None), (prior, None, None),
            (tcol, None, None), (tokens, None, None), (w_merge, None, None), (b_merge, None, None),
            (gain_first, None, None), (bias_first, None, None), (b_reduce, None, None),
            (w_expand, (D, FF_BLOCK), lambda j, s: (0, j)),
            (b_expand, (1, FF_BLOCK), lambda j, s: (0, j)),
            (w_reduce, (FF_BLOCK, D), lambda j, s: (j, 0)),
        ],
        [
            (wide_shape, F32, None, None), (wide_shape, F32, None, None), (wide_shape, BF, None, None),
            (wide_shape, F32, None, None), ((rows, LANES), F32, None, None), (wide_shape, BF, None, None),
            (wide_shape, F32, None, None),
            ((rows, FF), BF, (rows, FF_BLOCK), lambda j, s: (0, j)),
            ((rows, FF), BF, (rows, FF_BLOCK), lambda j, s: (0, j)),
        ],
        us=11,
    )

    normed_t, mixed_t = map(transposed_pieces, (normed, mixed))
    half_shape = (rows, D // 2)
    result, grad_second, branch, bg_keep, bg_send, sums_second = call(
        functools.partial(second_kernel, core_at), "second_norm", scal, (1,),
        [(second, None, None), (cotangent, None, None), (gain_second, None, None), (bias_second, None, None)],
        [
            (wide_shape, BF, None, None), (wide_shape, F32, None, None), (wide_shape, BF, None, None),
            (half_shape, BF, None, None), (half_shape, BF, None, None), ((8, D), F32, None, None),
        ],
        us=2.6,
    )

    devices = ring.devices
    small, large = D // devices, FF // devices
    whole = lambda a: (a, None, None)
    by_z = lambda a: (a, (1, D // 4, rows), lambda j, s: (j, 0, 0))
    by_col = lambda a: (a, (rows, FF // 4), lambda j, s: (0, j))

    def group(kernel, name, scal, ins, piece_rows, us, scratch=()):
        shape = (2, 4, piece_rows, D // 2)
        sent = call(
            functools.partial(kernel, pos_at), name, scal, (4,), ins, [(shape, BF, None, None)] * 4, scratch, us
        )
        return Scatter(ring, core_at, name, sent)

    ff_half = FF_STEPS // 2
    half_of = lambda core_of: [
        (slope, (rows, FF_BLOCK), lambda j, s: (0, core_of(s) * ff_half + j)),
        (w_expand, (D, FF_BLOCK), lambda j, s: (0, core_of(s) * ff_half + j)),
        (w_reduce, (FF_BLOCK, D), lambda j, s: (core_of(s) * ff_half + j, 0)),
    ]
    hidden = ((ff_half, rows, FF_BLOCK), BF, (1, rows, FF_BLOCK), lambda j, s: (j, 0, 0))
    hidden_sums = ((1, FF // 2), F32, (1, FF_BLOCK), lambda j, s: (0, j))
    pg_send, sum_sent, partial = call(
        back_sent_kernel, "feed_forward_back_sent", scal, (ff_half,),
        [(branch, None, None), *half_of(lambda s: 1 - s[core_at]), (grad_second, None, None)],
        [hidden, hidden_sums, (wide_shape, F32, None, None)],
        us=5,
    )
    order = scal
    if fast:
        pg_o = ring.core(pg_send)
        act_o, normed_o, mixed_o, bg_o = map(ring.core, (act, normed_t, mixed_t, bg_send))
        reduced = group(
            reduce_grad_kernel, "grad_reduce", after(scal, partial),
            [by_col(act), by_col(act_o), whole(bg_keep), whole(bg_o)], large, 6,
        )
        order = after(scal, reduced.xs)
        reduced.send()

    pg_keep, grad_first, mg_keep, mg_send, w_att, e_att, later, sum_kept, sums_first = call(
        functools.partial(back_kernel, core_at), "feed_forward_back", order, (ff_half,),
        [
            (branch, None, None), *half_of(lambda s: s[core_at]),
            (partial, None, None), (gain_first, None, None), (xhat, None, None), (scale, None, None),
            (w_merge, None, None), (att, None, None), (inv, None, None), (rq, None, None), (tcol, None, None),
        ],
        [
            hidden, (wide_shape, F32, None, None), (half_shape, BF, None, None), (half_shape, BF, None, None),
            (wide_shape, BF, None, None), ((rows, LANES), BF, None, None),
            ((PAIRS + 1, LANES, LANES), BF, None, None), hidden_sums, ((8, D), F32, None, None),
        ],
        [pltpu.VMEM(wide_shape, F32)],
        us=9,
    )
    sum_expand = jnp.where(
        first_core, jnp.concatenate([sum_kept, sum_sent], axis=1), jnp.concatenate([sum_sent, sum_kept], axis=1)
    )
    later = lax.ppermute(later, AXES, backward)

    if fast:
        mg_o = ring.core(mg_send)
        expanded = group(
            expand_grad_kernel, "grad_expand", scal,
            [
                by_z(normed_t), by_z(normed_o), whole(pg_keep), whole(pg_o),
                by_z(mixed_t), by_z(mixed_o), whole(mg_keep), whole(mg_o),
            ],
            5 * small, 0.5,
        )
        expanded.send()
        order = after(scal, reduced.first(after(scal, expanded.xs)))
        reduced.send_first()

    blocks = 3 * PAIRS // 2
    pair_block = lambda a: (a, (rows, LANES), lambda j, s: (0, j))
    pj_keep, pj_send, sum_heads = call(
        functools.partial(attn_back_kernel, head_at, core_at), "attention_back", order, (PAIRS,),
        [
            pair_block(rq), pair_block(rk), pair_block(v), pair_block(w_att), whole(e_att),
            (prior, None, None), (later, None, None), (tcol, None, None), (trow, None, None),
        ],
        [
            ((blocks, rows, LANES), BF, None, None), ((blocks, rows, LANES), BF, None, None),
            ((3, 8, D), F32, (3, 8, LANES), lambda j, s: (0, 0, j)),
        ],
        [pltpu.VMEM((rows, rows), F32), pltpu.VMEM((rows, rows), F32)],
        us=14,
    )

    if fast:
        pj_o = ring.core(pj_send)
        order = expanded.first(after(scal, pj_send))
        expanded.send_first()
        order = reduced.second(after(scal, order), us=12)
        reduced.send_second()
        heads = group(
            functools.partial(heads_grad_kernel, devices=devices), "grad_heads", after(scal, order),
            [
                by_z(tokens_t), by_z(tokens_o), whole(pj_keep), whole(pj_o),
                *((sum_heads, (1, 8, D), lambda j, s, n=n: (n, 0, 0)) for n in range(3)),
                whole(sums_first), whole(sum_expand), whole(sums_second),
            ],
            3 * small + 8, 5, [pltpu.VMEM((devices, D // 2), F32)],
        )
        heads.send()
        order = after(scal, heads.xs)

    third = blocks // 3
    wide_block = third * LANES
    (input_grad,) = call(
        input_kernel, "input_grad", order, (3,),
        [
            (grad_first, None, None),
            (pj_keep, (third, rows, LANES), lambda j, s: (j, 0, 0)),
            (pj_send, (third, rows, LANES), lambda j, s: (j, 0, 0)),
            (w_heads, (D, wide_block), lambda j, s: (0, 3 * s[core_at] + j)),
            (w_heads, (D, wide_block), lambda j, s: (0, 3 * (1 - s[core_at]) + j)),
        ],
        [(wide_shape, F32, None, None)],
        us=5.3,
    )

    if fast:
        order = expanded.second(after(scal, input_grad))
        expanded.send_second()
        reduce_own, reduce_got = reduced.last(after(scal, order))
        order = heads.first(after(scal, reduce_own))
        heads.send_first()
        expand_own, expand_got = expanded.last(after(scal, order))
        heads.second(after(scal, expand_own))
        heads.send_second()
        heads_own, heads_got = heads.last(scal)
        w_reduce_grad = halves(first_core, reduce_own, reduce_got)
        split = 4 * small
        w_expand_grad = halves(
            first_core, columns(expand_own[:split], small, 4), columns(expand_got[:split], small, 4)
        )
        w_merge_grad = halves(first_core, expand_own[split:], expand_got[split:])
        split = 3 * small
        w_heads_grad = halves(
            first_core, columns(heads_own[:split], small, 3), columns(heads_got[:split], small, 3)
        )
        entries = heads_own[split:] + heads_got[split:]
        entries = entries[0] + entries[1]
        shares, at = [], 0
        for n in (2 * small, small, small, small, small, large, small, small, small):
            shares.append(entries[at : at + n])
            at += n
        grads = (
            w_heads_grad, *shares[:2], w_merge_grad, *shares[2:5], w_expand_grad, shares[5], w_reduce_grad,
            *shares[6:],
        )
    else:
        by_core = lambda keep, send: jnp.concatenate(
            [jnp.where(first_core, keep, send), jnp.where(first_core, send, keep)], axis=1
        )
        flat = lambda v: v.transpose(1, 0, 2).reshape(rows, -1)
        scatter = lambda v: lax.psum_scatter(v, AXES, scatter_dimension=0, tiled=True)
        grads = (
            scatter(dot_t(tokens, by_core(flat(pj_keep), flat(pj_send)))),
            scatter(jnp.concatenate([sum_heads[0, 0], sum_heads[1, 0]])), scatter(sum_heads[2, 0]),
            scatter(dot_t(mixed, by_core(mg_keep, mg_send))),
            scatter(sums_first[2]), scatter(sums_first[0]), scatter(sums_first[1]),
            scatter(dot_t(normed, by_core(flat(pg_keep), flat(pg_send)))),
            scatter(sum_expand[0]),
            scatter(dot_t(act, branch)),
            scatter(sums_second[2]), scatter(sums_second[0]), scatter(sums_second[1]),
        )
    return (result, input_grad) + tuple(grads)


def solution(mesh):
    in_specs = (P(AXES, None),) + (P(),) * 12 + (P("dp", None), P(AXES, None))
    row, one = P(AXES, None), P(AXES)
    out_specs = (row, row, row, one, one, row, one, one, one, row, one, row, one, one, one)
    return jax.shard_map(
        per_device, mesh=mesh, in_specs=in_specs, out_specs=out_specs, check_vma=False
    )
```

time: 260 us -> 182 us (0.70)
  waiting for transfers between devices: 66.2 us -> 31 us
  starting transfers between devices: 50 us -> 34.5 us
  other arithmetic: 16.3 us -> 2.9 us
  Pallas kernels: 96.1 us -> 84.4 us
    ppermute x41 -> x32, waiting for transfers between devices: 58.7 us -> 31 us  [swap(): lax.ppermute(value, AXES, [(i, i ^ bits) for i in range(self.devices)])]
    ppermute x41 -> x32, starting transfers between devices: 43.7 us -> 28.8 us  [swap(): lax.ppermute(value, AXES, [(i, i ^ bits) for i in range(self.devices)])]
    unnamed x63 -> x158, local copies, waits for them, and re-layouts: 8.46 us -> 21.6 us
    pallas_call x10 -> x20, Pallas kernels: 96.1 us -> 84.4 us  [call(): pl.pallas_call(kernel, name=name, grid_spec=pltpu.PrefetchScalarGridSpec(...]
    ppermute x1, waiting for transfers between devices: 7.48 us -> 0.01 us  [per_device(): later = lax.ppermute(later, AXES, backward)]
    another operation x8 -> x0, local copies, waits for them, and re-layouts: 6.16 us -> none  [exchange_fast(): flat = jnp.concatenate([v.reshape(devices, -1) for v in vectors], axis=1)]
    another operation x6 -> x0, other arithmetic: 4.52 us -> none
    convert_element_type x8 -> x0, other arithmetic: 3.99 us -> none  [the longest x3 1.96 us: scatter_group(): (wide(xk[1]) + wide(xr[1])).astype(BF)]
  transfers between devices with their start and end apart: 43 -> 34, of which waited for: 14 -> 9; matrix products, arithmetic and copies ran while one was open for 13% -> 2% of each run, Pallas kernels for 13% -> 39%
where the time goes in v2:
time: 182 us; the launch traced here: 181 us
  Pallas kernels  84.4 us (46%)
  starting transfers between devices  34.5 us (19%)
  waiting for transfers between devices  31 us (17%)
  local copies, waits for them, and re-layouts  26.7 us (15%)
  other arithmetic  2.9 us (2%)
    pallas_call x20, Pallas kernels, call(): pl.pallas_call(kernel, name=name, grid_spec=pltpu.PrefetchScalarGridSpec(...  84.4 us
    ppermute x32, waiting for transfers between devices, swap(): lax.ppermute(value, AXES, [(i, i ^ bits) for i in range(self.devices)])  31 us
    ppermute x32, starting transfers between devices, swap(): lax.ppermute(value, AXES, [(i, i ^ bits) for i in range(self.devices)])  28.8 us
    unnamed x158, local copies, waits for them, and re-layouts  21.6 us
    ppermute x1, starting transfers between devices, per_device(): prior = lax.ppermute(state, AXES, forward)  4.47 us
  transfers between devices with their start and end apart: 34, of which 9 were waited for; matrix products, arithmetic and copies ran while one was open for 2% of the time, Pallas kernels for 39%

profile of v2, /device:TPU:0, one launch (start us, length us, event | category | flops | bytes accessed | tf_op | source)
XLA Modules:
  0.0 181.3 jit_solution(7555109240456721975)
XLA Ops:
  0.7 1.5 copy.37
  2.8 2.0 %copy-done.13 = bf16[768,2304]{1,0:T(8,128)(2,1)S(1)} copy-done((bf16[768,2304]{1,0:T(8,128)(2,1)S(1)}, bf16[768,2304]{1,0:T(8,128)(2,1)}, u32[]{:S(2)}) %copy-start.13) | copy-done | bytes 3538968
  4.8 3.9 %keys_values.1 = (bf16[512,768]{1,0:T(8,128)(2,1)S(1)}, bf16[512,768]{1,0:T(8,128)(2,1)S(1)}, bf16[7,128,128]{2,1,0:T(8,128)(2,1)S(1)}, f32[512,128]{1,0:T(8,128)S(1)}, f32[8,512]{1,0:T(8,128)S(1)}) custom-call(s32[9]{0:T(128)S(1)} %concatenate.37.scal, bf16[512,768]{1,0:T(8,128)(2,1)S(1)} %copy-done.2, bf16[768,2304]{1,0:T(8,128)(2,1)S(1)} %copy-done.13, ...), custom_call_target="tpu_custom_call" | custom-call | flops 4600000000 | bytes 1 | tf_op jit(solution)/shard_map/keys_values/pallas_call | solution.py:41
  8.8 4.5 %collective-permute-start.1 = (bf16[7,128,128]{2,1,0:T(8,128)(2,1)S(1)}, bf16[7,128,128]{2,1,0:T(8,128)(2,1)S(1)}, u32[]{:S(2)}, u32[]{:S(2)}) collective-permute-start(bf16[7,128,128]{2,1,0:T(8,128)(2,1)S(1)} %get-tuple-element.111), channel_id=1, source_target_pairs={{0,1},{2,3},{4,5},{6,7},{8,9},{10,11},{12,13},{14,15},{16,17},{18,... | collective-permute-start | bytes 688136 | tf_op jit(solution)/shard_map/ppermute | solution.py:701
  13.4 5.7 %local_attention.1 = (bf16[512,768]{1,0:T(8,128)(2,1)S(1)}, f32[512,768]{1,0:T(8,128)S(1)}, f32[512,768]{1,0:T(8,128)S(1)}) custom-call(s32[9]{0:T(128)S(1)} %concatenate.37.scal, bf16[512,768]{1,0:T(8,128)(2,1)S(1)} %copy-done.2, bf16[768,2304]{1,0:T(8,128)(2,1)S(1)} %copy-done.13, bf16[1,2304]{1,0:T(2,128)(2,1)S(1)} %reshape.150.bk.bv.bq, ...), custom_call_target="tpu_custom_call" | custom-call | flops 6899999744 | bytes 1 | tf_op jit(solution)/shard_map/local_attention/pallas_call | solution.py:41
  20.3 11.4 %feed_forward.1 = (f32[512,768]{1,0:T(8,128)S(1)}, f32[512,768]{1,0:T(8,128)S(1)}, bf16[512,768]{1,0:T(8,128)(2,1)S(1)}, f32[512,768]{1,0:T(8,128)S(1)}, f32[512...) custom-call(s32[9]{0:T(128)S(1)} %concatenate.37.scal, ...), custom_call_target="tpu_custom_call" | custom-call | flops 12650000384 | bytes 1 | tf_op jit(solution)/shard_map/feed_forward/pallas_call | solution.py:41
  31.7 1.2 copy-done.39
  32.9 0.9 copy-done.50
  34.1 3.0 %second_norm.1 = (bf16[512,768]{1,0:T(8,128)(2,1)}, f32[512,768]{1,0:T(8,128)S(1)}, bf16[512,768]{1,0:T(8,128)(2,1)S(1)}, bf16[512,384]{1,0:T(8,128)(2,1)S(1)}, ...) custom-call(s32[9]{0:T(128)S(1)} %concatenate.37.scal, f32[512,768]{1,0:T(8,128)S(1)} %get-tuple-element.112.second, ...), custom_call_target="tpu_custom_call" | custom-call | flops 2990000128 | bytes 1 | tf_op jit(solution)/shard_map/second_norm/pallas_call | solution.py:41
  37.4 4.4 %feed_forward_back_sent.1 = (bf16[2,512,768]{2,1,0:T(8,128)(2,1)}, f32[1,1536]{1,0:T(1,128)S(1)}, f32[512,768]{1,0:T(8,128)S(1)}) custom-call(s32[9]{0:T(128)S(1)} %concatenate.37.scal, bf16[512,768]{1,0:T(8,128)(2,1)S(1)} %get-tuple-element.115.full, bf16[512,3072]{1,0:T(8,128)(2,1)S(1)} %get-tuple-element.116.slope, bf16[768,3072]{1,0:T(8,128)(2,1)S(1)} %bitcast.57, ...), custom_call_target="tpu_custom_call" | custom-call | flops 5750000128 | bytes 1 | tf_op jit(solution)/shard_map/feed_forward_back_sent/pallas_call | solution.py:41
  41.9 1.1 copy-done.29
  43.9 1.4 copy.39
  45.7 1.0 copy-done.46
  46.8 8.7 %grad_reduce.1 = (bf16[2,4,96,384]{3,2,1,0:T(8,128)(2,1)S(1)}, bf16[2,4,96,384]{3,2,1,0:T(8,128)(2,1)}, bf16[2,4,96,384]{3,2,1,0:T(8,128)(2,1)S(1)}, bf16[2,4,96,384]{3,2,1,0:T(8,128)(2,1)}) custom-call(s32[9]{0:T(128)S(1)} %concatenate.37.scal, bf16[512,3072]{1,0:T(8,128)(2,1)} %get-tuple-element.120.a_own, bf16[512,3072]{1,0:T(8,128)(2,1)} %collective-permute-done.3.a_oth, ...), custom_call_target="tpu_custom_call" | custom-call | flops 6899999744 | bytes 1 | tf_op jit(solution)/shard_map/grad_reduce/pallas_call | solution.py:41
  57.1 1.0 collective-permute-start.8
  58.1 1.5 collective-permute-start.9
  60.4 2.3 %copy-done.11 = bf16[768,3072]{1,0:T(8,128)(2,1)S(1)} copy-done((bf16[768,3072]{1,0:T(8,128)(2,1)S(1)}, bf16[768,3072]{1,0:T(8,128)(2,1)}, u32[]{:S(2)}) %copy-start.11) | copy-done | bytes 4718616
  62.7 2.3 %copy-done.12 = bf16[3072,768]{1,0:T(8,128)(2,1)S(1)} copy-done((bf16[3072,768]{1,0:T(8,128)(2,1)S(1)}, bf16[3072,768]{1,0:T(8,128)(2,1)}, u32[]{:S(2)}) %copy-start.12) | copy-done | bytes 4718616
  65.1 8.5 %feed_forward_back.1 = (bf16[2,512,768]{2,1,0:T(8,128)(2,1)S(1)}, f32[512,768]{1,0:T(8,128)S(1)}, bf16[512,384]{1,0:T(8,128)(2,1)S(1)}, bf16[512,384]{1,0:T(8,12...) custom-call(s32[9]{0:T(128)S(1)} %copy-done.9, ...), custom_call_target="tpu_custom_call" | custom-call | flops 10350000128 | bytes 1 | tf_op jit(solution)/shard_map/feed_forward_back/pallas_call | solution.py:41
  73.6 1.1 copy-done
  74.7 1.2 copy-done.33
  75.9 0.9 copy-done.53
  78.8 1.3 collective-permute-start.10
  80.8 1.4 copy-done.1
  82.9 5.9 %grad_expand.1 = (bf16[2,4,120,384]{3,2,1,0:T(8,128)(2,1)S(1)}, bf16[2,4,120,384]{3,2,1,0:T(8,128)(2,1)S(1)}, bf16[2,4,120,384]{3,2,1,0:T(8,128)(2,1)S(1)}, bf16[2,4,120,384]{3,2,1,0:T(8,128)(2,1)S(1)}) custom-call(s32[9]{0:T(128)S(1)} %copy-done.10, bf16[4,192,512]{2,1,0:T(8,128)(2,1)S(1)} %bitcast.48, bf16[4,192,512]{2,1,0:T(8,128)(2,1)} %collective-permute-done.2.a_oth, ...), custom_call_target="tpu_custom_call" | custom-call | flops 575000000 | bytes 1 | tf_op jit(solution)/shard_map/grad_expand/pallas_call | solution.py:41
  88.8 2.0 %collective-permute-start.11 = (bf16[2,4,120,384]{3,2,1,0:T(8,128)(2,1)S(1)}, bf16[2,4,120,384]{3,2,1,0:T(8,128)(2,1)S(1)}, u32[]{:S(2)}, u32[]{:S(2)}) collective-permute-start(bf16[2,4,120,384]{3,2,1,0:T(8,128)(2,1)S(1)} %get-tuple-element.134), channel_id=1, source_target_pairs={{0,1},{1,0},{2,3},{3,2},{4,5},{5,4},{6,7},{7,6},{8,9},{9,8},{10,11... | collective-permute-start | bytes 2211848 | tf_op jit(solution)/shard_map/ppermute | solution.py:558
  91.4 2.1 %grad_reduce_add1.1 = (bf16[4,96,384]{2,1,0:T(8,128)(2,1)S(1)}, bf16[4,96,384]{2,1,0:T(8,128)(2,1)S(1)}) custom-call(s32[9]{0:T(128)S(1)} %copy-done.10, bf16[2,4,96,384]{3,2,1,0:T(8,128)(2,1)S(1)} %copy-done.24, bf16[2,4,96,384]{3,2,1,0:T(8,128)(2,1)} %collective-permute-done.8.xr, bf16[2,4,96,384]{3,2,1,0:T(8,128)(2,1)S(1)} %copy-done.26, ...), custom_call_target="tpu_custom_call" | custom-call | flops 1150000000 | bytes 1 | tf_op jit(solution)/shard_map/grad_reduce_add1/pallas_call | solution.py:41
  93.5 1.6 collective-permute-start.13
  95.2 13.9 %attention_back.1 = (bf16[9,512,128]{2,1,0:T(8,128)(2,1)S(1)}, bf16[9,512,128]{2,1,0:T(8,128)(2,1)S(1)}, f32[3,8,768]{2,1,0:T(8,128)S(1)}) custom-call(s32[9]{0:T(128)S(1)} %copy-done.10, bf16[512,768]{1,0:T(8,128)(2,1)S(1)} %copy-done.52, bf16[512,768]{1,0:T(8,128)(2,1)S(1)} %copy-done.36, bf16[512,768]{1,0:T(8,128)(2,1)S(1)} %copy-done.38, ...), custom_call_target="tpu_custom_call" | custom-call | flops 16099999744 | bytes 1 | tf_op jit(solution)/shard_map/attention_back/pallas_call | solution.py:41
  109.3 0.9 collective-permute-done.12.yr
  111.5 5.0 %collective-permute-done.13.xm = bf16[4,96,384]{2,1,0:T(8,128)(2,1)S(1)} collective-permute-done((bf16[4,96,384]{2,1,0:T(8,128)(2,1)S(1)}, bf16[4,96,384]{2,1,0:T(8,128)(2,1)S(1)}, u32[]{:S(2)}, u32[]{:S(2)}) %collective-permute-start.13) | collective-permute-done | bytes 294944 | tf_op jit(solution)/shard_map/ppermute | solution.py:558
  116.5 1.8 grad_reduce_add2.1
  118.4 1.6 collective-permute-start.18
  120.0 2.6 %collective-permute-start.19 = (bf16[2,96,384]{2,1,0:T(8,128)(2,1)S(1)}, bf16[2,96,384]{2,1,0:T(8,128)(2,1)S(1)}, u32[]{:S(2)}, u32[]{:S(2)}) collective-permute-start(bf16[2,96,384]{2,1,0:T(8,128)(2,1)S(1)} %get-tuple-element.168), channel_id=1, source_target_pairs={{0,16},{1,17},{2,18},{3,19},{4,20},{5,21},{6,22},{7,23},{8,24},{9,... | collective-permute-start | bytes 442376 | tf_op jit(solution)/shard_map/ppermute | solution.py:558
  122.9 5.1 %grad_heads.1 = (bf16[2,4,80,384]{3,2,1,0:T(8,128)(2,1)S(1)}, bf16[2,4,80,384]{3,2,1,0:T(8,128)(2,1)S(1)}, bf16[2,4,80,384]{3,2,1,0:T(8,128)(2,1)S(1)}, bf16[2,4,80,384]{3,2,1,0:T(8,128)(2,1)S(1)}) custom-call(s32[9]{0:T(128)S(1)} %copy-done.10, bf16[4,192,512]{2,1,0:T(8,128)(2,1)S(1)} %bitcast.53, bf16[4,192,512]{2,1,0:T(8,128)(2,1)S(1)} %copy-done.19, ...), custom_call_target="tpu_custom_call" | custom-call | flops 5750000128 | bytes 1 | tf_op jit(solution)/shard_map/grad_heads/pallas_call | solution.py:41
  127.9 2.0 %collective-permute-start.21 = (bf16[2,4,80,384]{3,2,1,0:T(8,128)(2,1)S(1)}, bf16[2,4,80,384]{3,2,1,0:T(8,128)(2,1)S(1)}, u32[]{:S(2)}, u32[]{:S(2)}) collective-permute-start(bf16[2,4,80,384]{3,2,1,0:T(8,128)(2,1)S(1)} %get-tuple-element.160), channel_id=1, source_target_pairs={{0,1},{1,0},{2,3},{3,2},{4,5},{5,4},{6,7},{7,6},{8,9},{9,8},{10,11... | collective-permute-start | bytes 1474568 | tf_op jit(solution)/shard_map/ppermute | solution.py:558
  130.5 5.2 %input_grad.1 = f32[512,768]{1,0:T(8,128)} custom-call(s32[9]{0:T(128)S(1)} %copy-done.10, f32[512,768]{1,0:T(8,128)S(1)} %copy-done.34, bf16[9,512,128]{2,1,0:T(8,128)(2,1)S(1)} %get-tuple-element.154.b_own.keep, bf16[9,512,128]{2,1,0:T(8,128)(2,1)S(1)} %get-tuple-element.144.send, bf16[768,2304]{1,0:T(8,128)(2,1)S(1)} %copy-done.14, ...), custom_call_target="tpu_custom_call" | custom-call | flops 6095000064 | bytes 1 | tf_op jit(solution)/shard_map/input_grad/pallas_call | solution.py:41
  137.3 3.5 %collective-permute-start.24 = (bf16[2,120,384]{2,1,0:T(8,128)(2,1)S(1)}, bf16[2,120,384]{2,1,0:T(8,128)(2,1)S(1)}, u32[]{:S(2)}, u32[]{:S(2)}) collective-permute-start(bf16[2,120,384]{2,1,0:T(8,128)(2,1)S(1)} %get-tuple-element.178), channel_id=1, source_target_pairs={{0,16},{1,17},{2,18},{3,19},{4,20},{5,21},{6,22},{7,23},{8,24},{9,... | collective-permute-start | bytes 552968 | tf_op jit(solution)/shard_map/ppermute | solution.py:558
  142.3 2.4 %collective-permute-done.23.z1 = bf16[2,120,384]{2,1,0:T(8,128)(2,1)S(1)} collective-permute-done((bf16[2,120,384]{2,1,0:T(8,128)(2,1)S(1)}, bf16[2,120,384]{2,1,0:T(8,128)(2,1)S(1)}, u32[]{:S(2)}, u32[]{:S(2)}) %collective-permute-start.23) | collective-permute-done | bytes 184352 | tf_op jit(solution)/shard_map/ppermute | solution.py:558
  144.7 6.8 %collective-permute-done.24.z2 = bf16[2,120,384]{2,1,0:T(8,128)(2,1)S(1)} collective-permute-done((bf16[2,120,384]{2,1,0:T(8,128)(2,1)S(1)}, bf16[2,120,384]{2,1,0:T(8,128)(2,1)S(1)}, u32[]{:S(2)}, u32[]{:S(2)}) %collective-permute-start.24) | collective-permute-done | bytes 184352 | tf_op jit(solution)/shard_map/ppermute | solution.py:558
  152.7 1.5 collective-permute-start.26
  155.7 4.9 %collective-permute-done.26.xm = bf16[4,80,384]{2,1,0:T(8,128)(2,1)S(1)} collective-permute-done((bf16[4,80,384]{2,1,0:T(8,128)(2,1)S(1)}, bf16[4,80,384]{2,1,0:T(8,128)(2,1)S(1)}, u32[]{:S(2)}, u32[]{:S(2)}) %collective-permute-start.26) | collective-permute-done | bytes 245792 | tf_op jit(solution)/shard_map/ppermute | solution.py:558
  160.7 1.3 collective-permute-done.27.ym
  162.7 2.6 %collective-permute-start.28 = (bf16[2,80,384]{2,1,0:T(8,128)(2,1)S(1)}, bf16[2,80,384]{2,1,0:T(8,128)(2,1)S(1)}, u32[]{:S(2)}, u32[]{:S(2)}) collective-permute-start(bf16[2,80,384]{2,1,0:T(8,128)(2,1)S(1)} %get-tuple-element.184), channel_id=1, source_target_pairs={{0,8},{1,9},{2,10},{3,11},{4,12},{5,13},{6,14},{7,15},{8,0},{9,1},... | collective-permute-start | bytes 368648 | tf_op jit(solution)/shard_map/ppermute | solution.py:558
  165.3 1.1 collective-permute-start.29
  166.4 1.4 collective-permute-start.30
  167.8 1.6 collective-permute-done.28.z1
  169.3 7.3 %collective-permute-done.29.z2 = bf16[2,80,384]{2,1,0:T(8,128)(2,1)S(1)} collective-permute-done((bf16[2,80,384]{2,1,0:T(8,128)(2,1)S(1)}, bf16[2,80,384]{2,1,0:T(8,128)(2,1)S(1)}, u32[]{:S(2)}, u32[]{:S(2)}) %collective-permute-start.29) | collective-permute-done | bytes 122912 | tf_op jit(solution)/shard_map/ppermute | solution.py:558
  (229 shorter events, 23.1 us)
Async XLA Ops:
  2.2 17.1 %collective-permute-start = (bf16[4,192,512]{2,1,0:T(8,128)(2,1)S(1)}, bf16[4,192,512]{2,1,0:T(8,128)(2,1)S(1)}, u32[]{:S(2)}, u32[]{:S(2)}) collective-permute-start(bf16[4,192,512]{2,1,0:T(8,128)(2,1)S(1)} %bitcast.52), channel_id=1, source_target_pairs={{0,2},{1,3},{2,0},{3,1},{4,6},{5,7},{6,4},{7,5},{8,10},{9,11},{10,... | collective-permute-start | bytes 2359304 | tf_op jit(solution)/shard_map/ppermute | solution.py:558
  4.8 40.9 %copy-start.8 = (s32[9]{0:T(128)}, s32[9]{0:T(128)S(1)}, u32[]{:S(2)}) copy-start(s32[9]{0:T(128)S(1)} %concatenate.37.scal) | copy-start | bytes 112
  4.8 15.3 %slice-start = ((s8[4718592]{0:T(1024)(128)(4,1)}), s8[4194304]{0:T(1024)(128)(4,1)S(1)}, s32[]{:S(2)}) async-start(s8[4718592]{0:T(1024)(128)(4,1)} %bitcast.56), calls=%async_computation | async-start | bytes 8388608
  4.8 15.3 %slice-start.2 = ((s8[4718592]{0:T(1024)(128)(4,1)}), s8[4194304]{0:T(1024)(128)(4,1)S(1)}, s32[]{:S(2)}) async-start(s8[4718592]{0:T(1024)(128)(4,1)} %bitcast.58), calls=%async_computation.2 | async-start | bytes 8388608
  8.8 11.4 %collective-permute-start.1 = (bf16[7,128,128]{2,1,0:T(8,128)(2,1)S(1)}, bf16[7,128,128]{2,1,0:T(8,128)(2,1)S(1)}, u32[]{:S(2)}, u32[]{:S(2)}) collective-permute-start(bf16[7,128,128]{2,1,0:T(8,128)(2,1)S(1)} %get-tuple-element.111), channel_id=1, source_target_pairs={{0,1},{2,3},{4,5},{6,7},{8,9},{10,11},{12,13},{14,15},{16,17},{18,... | collective-permute-start | bytes 688136 | tf_op jit(solution)/shard_map/ppermute | solution.py:701
  20.2 13.8 %copy-start.71 = (bf16[768]{0:T(1024)(128)(2,1)S(1)}, bf16[768]{0:T(1024)(128)(2,1)}, u32[]{:S(2)}) copy-start(bf16[768]{0:T(1024)(128)(2,1)} %param.26) | copy-start | bytes 4612
  20.2 13.8 %copy-start.72 = (bf16[768]{0:T(1024)(128)(2,1)S(1)}, bf16[768]{0:T(1024)(128)(2,1)}, u32[]{:S(2)}) copy-start(bf16[768]{0:T(1024)(128)(2,1)} %param.27) | copy-start | bytes 4612
  20.2 13.8 %copy-start.17 = (bf16[512,768]{1,0:T(8,128)(2,1)S(1)}, bf16[512,768]{1,0:T(8,128)(2,1)}, u32[]{:S(2)}) copy-start(bf16[512,768]{1,0:T(8,128)(2,1)} %cot.1) | copy-start | bytes 2359300
  33.8 11.9 %collective-permute-start.3 = (bf16[512,3072]{1,0:T(8,128)(2,1)}, bf16[512,3072]{1,0:T(8,128)(2,1)}, u32[]{:S(2)}, u32[]{:S(2)}) collective-permute-start(bf16[512,3072]{1,0:T(8,128)(2,1)} %get-tuple-element.120.a_own), channel_id=1, source_target_pairs={{0,2},{1,3},{2,0},{3,1},{4,6},{5,7},{6,4},{7,5},{8,10},{9,11},{10,... | collective-permute-start | bytes 9437192 | tf_op jit(solution)/shard_map/ppermute | solution.py:558
  37.2 8.5 %collective-permute-start.4 = (bf16[512,384]{1,0:T(8,128)(2,1)}, bf16[512,384]{1,0:T(8,128)(2,1)}, u32[]{:S(2)}, u32[]{:S(2)}) collective-permute-start(bf16[512,384]{1,0:T(8,128)(2,1)} %get-tuple-element.122), channel_id=1, source_target_pairs={{0,2},{1,3},{2,0},{3,1},{4,6},{5,7},{6,4},{7,5},{8,10},{9,11},{10,... | collective-permute-start | bytes 1179656 | tf_op jit(solution)/shard_map/ppermute | solution.py:558
  43.0 37.1 %collective-permute-start.5 = (bf16[2,512,768]{2,1,0:T(8,128)(2,1)}, bf16[2,512,768]{2,1,0:T(8,128)(2,1)S(1)}, u32[]{:S(2)}, u32[]{:S(2)}) collective-permute-start(bf16[2,512,768]{2,1,0:T(8,128)(2,1)} %get-tuple-element.130), channel_id=1, source_target_pairs={{0,2},{1,3},{2,0},{3,1},{4,6},{5,7},{6,4},{7,5},{8,10},{9,11},{10,... | collective-permute-start | bytes 4718600 | tf_op jit(solution)/shard_map/ppermute | solution.py:558
  43.6 34.5 %collective-permute-start.2 = (bf16[4,192,512]{2,1,0:T(8,128)(2,1)S(1)}, bf16[4,192,512]{2,1,0:T(8,128)(2,1)}, u32[]{:S(2)}, u32[]{:S(2)}) collective-permute-start(bf16[4,192,512]{2,1,0:T(8,128)(2,1)S(1)} %bitcast.47), channel_id=1, source_target_pairs={{0,2},{1,3},{2,0},{3,1},{4,6},{5,7},{6,4},{7,5},{8,10},{9,11},{10,... | collective-permute-start | bytes 2359304 | tf_op jit(solution)/shard_map/ppermute | solution.py:558
  45.3 33.5 %collective-permute-start.6 = (bf16[4,192,512]{2,1,0:T(8,128)(2,1)S(1)}, bf16[4,192,512]{2,1,0:T(8,128)(2,1)}, u32[]{:S(2)}, u32[]{:S(2)}) collective-permute-start(bf16[4,192,512]{2,1,0:T(8,128)(2,1)S(1)} %bitcast.49), channel_id=1, source_target_pairs={{0,2},{1,3},{2,0},{3,1},{4,6},{5,7},{6,4},{7,5},{8,10},{9,11},{10,... | collective-permute-start | bytes 2359304 | tf_op jit(solution)/shard_map/ppermute | solution.py:558
  46.7 13.0 %copy-start.16 = (bf16[768,768]{1,0:T(8,128)(2,1)S(1)}, bf16[768,768]{1,0:T(8,128)(2,1)}, u32[]{:S(2)}) copy-start(bf16[768,768]{1,0:T(8,128)(2,1)} %w_merge.1) | copy-start | bytes 3538948
  46.7 13.0 %copy-start.28 = (bf16[512,3072]{1,0:T(8,128)(2,1)S(1)}, bf16[512,3072]{1,0:T(8,128)(2,1)}, u32[]{:S(2)}) copy-start(bf16[512,3072]{1,0:T(8,128)(2,1)} %copy-done.27) | copy-start | bytes 9437188
  46.7 13.0 %copy-start.30 = (f32[512,768]{1,0:T(8,128)S(1)}, f32[512,768]{1,0:T(8,128)}, u32[]{:S(2)}) copy-start(f32[512,768]{1,0:T(8,128)} %copy-done.29) | copy-start | bytes 4718596
  46.7 13.0 %copy-start.32 = (bf16[512,768]{1,0:T(8,128)(2,1)S(1)}, bf16[512,768]{1,0:T(8,128)(2,1)}, u32[]{:S(2)}) copy-start(bf16[512,768]{1,0:T(8,128)(2,1)} %copy-done.31) | copy-start | bytes 2359300
  46.7 13.0 %copy-start.40 = (f32[512,768]{1,0:T(8,128)S(1)}, f32[512,768]{1,0:T(8,128)}, u32[]{:S(2)}) copy-start(f32[512,768]{1,0:T(8,128)} %copy-done.39) | copy-start | bytes 4718596
  46.7 13.0 %copy-start.42 = (f32[512,768]{1,0:T(8,128)S(1)}, f32[512,768]{1,0:T(8,128)}, u32[]{:S(2)}) copy-start(f32[512,768]{1,0:T(8,128)} %copy-done.41) | copy-start | bytes 4718596
  46.7 13.0 %copy-start.44 = (f32[512,768]{1,0:T(8,128)S(1)}, f32[512,768]{1,0:T(8,128)}, u32[]{:S(2)}) copy-start(f32[512,768]{1,0:T(8,128)} %copy-done.43) | copy-start | bytes 4718596
  46.7 13.0 %copy-start.48 = (f32[512,128]{1,0:T(8,128)S(1)}, f32[512,128]{1,0:T(8,128)}, u32[]{:S(2)}) copy-start(f32[512,128]{1,0:T(8,128)} %copy-done.47) | copy-start | bytes 786436
  57.1 34.2 %collective-permute-start.8 = (bf16[2,4,96,384]{3,2,1,0:T(8,128)(2,1)}, bf16[2,4,96,384]{3,2,1,0:T(8,128)(2,1)}, u32[]{:S(2)}, u32[]{:S(2)}) collective-permute-start(bf16[2,4,96,384]{3,2,1,0:T(8,128)(2,1)} %get-tuple-element.123), channel_id=1, source_target_pairs={{0,1},{1,0},{2,3},{3,2},{4,5},{5,4},{6,7},{7,6},{8,9},{9,8},{10,11... | collective-permute-start | bytes 1769480 | tf_op jit(solution)/shard_map/ppermute | solution.py:558
  58.1 33.2 %collective-permute-start.9 = (bf16[2,4,96,384]{3,2,1,0:T(8,128)(2,1)}, bf16[2,4,96,384]{3,2,1,0:T(8,128)(2,1)}, u32[]{:S(2)}, u32[]{:S(2)}) collective-permute-start(bf16[2,4,96,384]{3,2,1,0:T(8,128)(2,1)} %get-tuple-element.138), channel_id=1, source_target_pairs={{0,4},{1,5},{2,6},{3,7},{4,0},{5,1},{6,2},{7,3},{8,12},{9,13},{10,... | collective-permute-start | bytes 1769480 | tf_op jit(solution)/shard_map/ppermute | solution.py:558
  78.8 2.1 %collective-permute-start.7 = (bf16[512,384]{1,0:T(8,128)(2,1)}, bf16[512,384]{1,0:T(8,128)(2,1)}, u32[]{:S(2)}, u32[]{:S(2)}) collective-permute-start(bf16[512,384]{1,0:T(8,128)(2,1)} %get-tuple-element.133), channel_id=1, source_target_pairs={{0,2},{1,3},{2,0},{3,1},{4,6},{5,7},{6,4},{7,5},{8,10},{9,11},{10,... | collective-permute-start | bytes 1179656 | tf_op jit(solution)/shard_map/ppermute | solution.py:558
  78.8 16.4 %collective-permute-start.10 = (bf16[7,128,128]{2,1,0:T(8,128)(2,1)}, bf16[7,128,128]{2,1,0:T(8,128)(2,1)S(1)}, u32[]{:S(2)}, u32[]{:S(2)}) collective-permute-start(bf16[7,128,128]{2,1,0:T(8,128)(2,1)} %copy-done.22), channel_id=1, source_target_pairs={{1,0},{3,2},{5,4},{7,6},{9,8},{11,10},{13,12},{15,14},{17,16},{19,... | collective-permute-start | bytes 688136 | tf_op jit(solution)/shard_map/ppermute | solution.py:818
  88.8 20.4 %collective-permute-start.11 = (bf16[2,4,120,384]{3,2,1,0:T(8,128)(2,1)S(1)}, bf16[2,4,120,384]{3,2,1,0:T(8,128)(2,1)S(1)}, u32[]{:S(2)}, u32[]{:S(2)}) collective-permute-start(bf16[2,4,120,384]{3,2,1,0:T(8,128)(2,1)S(1)} %get-tuple-element.134), channel_id=1, source_target_pairs={{0,1},{1,0},{2,3},{3,2},{4,5},{5,4},{6,7},{7,6},{8,9},{9,8},{10,11... | collective-permute-start | bytes 2211848 | tf_op jit(solution)/shard_map/ppermute | solution.py:558
  90.8 19.4 %collective-permute-start.12 = (bf16[2,4,120,384]{3,2,1,0:T(8,128)(2,1)S(1)}, bf16[2,4,120,384]{3,2,1,0:T(8,128)(2,1)S(1)}, u32[]{:S(2)}, u32[]{:S(2)}) collective-permute-start(bf16[2,4,120,384]{3,2,1,0:T(8,128)(2,1)S(1)} %get-tuple-element.148), channel_id=1, source_target_pairs={{0,4},{1,5},{2,6},{3,7},{4,0},{5,1},{6,2},{7,3},{8,12},{9,13},{10,... | collective-permute-start | bytes 2211848 | tf_op jit(solution)/shard_map/ppermute | solution.py:558
  93.5 23.0 %collective-permute-start.13 = (bf16[4,96,384]{2,1,0:T(8,128)(2,1)S(1)}, bf16[4,96,384]{2,1,0:T(8,128)(2,1)S(1)}, u32[]{:S(2)}, u32[]{:S(2)}) collective-permute-start(bf16[4,96,384]{2,1,0:T(8,128)(2,1)S(1)} %get-tuple-element.139), channel_id=1, source_target_pairs={{0,4},{1,5},{2,6},{3,7},{4,0},{5,1},{6,2},{7,3},{8,12},{9,13},{10,... | collective-permute-start | bytes 884744 | tf_op jit(solution)/shard_map/ppermute | solution.py:558
  95.1 21.4 %collective-permute-start.14 = (bf16[4,96,384]{2,1,0:T(8,128)(2,1)S(1)}, bf16[4,96,384]{2,1,0:T(8,128)(2,1)S(1)}, u32[]{:S(2)}, u32[]{:S(2)}) collective-permute-start(bf16[4,96,384]{2,1,0:T(8,128)(2,1)S(1)} %get-tuple-element.151), channel_id=1, source_target_pairs={{0,1},{1,0},{2,3},{3,2},{4,5},{5,4},{6,7},{7,6},{8,9},{9,8},{10,11... | collective-permute-start | bytes 884744 | tf_op jit(solution)/shard_map/ppermute | solution.py:558
  109.2 13.4 %collective-permute-start.15 = (bf16[9,512,128]{2,1,0:T(8,128)(2,1)S(1)}, bf16[9,512,128]{2,1,0:T(8,128)(2,1)S(1)}, u32[]{:S(2)}, u32[]{:S(2)}) collective-permute-start(bf16[9,512,128]{2,1,0:T(8,128)(2,1)S(1)} %get-tuple-element.144.send), channel_id=1, source_target_pairs={{0,2},{1,3},{2,0},{3,1},{4,6},{5,7},{6,4},{7,5},{8,10},{9,11},{10,... | collective-permute-start | bytes 3538952 | tf_op jit(solution)/shard_map/ppermute | solution.py:558
  110.9 17.0 %collective-permute-start.16 = (bf16[4,120,384]{2,1,0:T(8,128)(2,1)S(1)}, bf16[4,120,384]{2,1,0:T(8,128)(2,1)S(1)}, u32[]{:S(2)}, u32[]{:S(2)}) collective-permute-start(bf16[4,120,384]{2,1,0:T(8,128)(2,1)S(1)} %get-tuple-element.149), channel_id=1, source_target_pairs={{0,4},{1,5},{2,6},{3,7},{4,0},{5,1},{6,2},{7,3},{8,12},{9,13},{10,... | collective-permute-start | bytes 1105928 | tf_op jit(solution)/shard_map/ppermute | solution.py:558
  118.3 11.7 %collective-permute-start.17 = (bf16[4,120,384]{2,1,0:T(8,128)(2,1)S(1)}, bf16[4,120,384]{2,1,0:T(8,128)(2,1)S(1)}, u32[]{:S(2)}, u32[]{:S(2)}) collective-permute-start(bf16[4,120,384]{2,1,0:T(8,128)(2,1)S(1)} %get-tuple-element.164), channel_id=1, source_target_pairs={{0,1},{1,0},{2,3},{3,2},{4,5},{5,4},{6,7},{7,6},{8,9},{9,8},{10,11... | collective-permute-start | bytes 1105928 | tf_op jit(solution)/shard_map/ppermute | solution.py:558
  118.4 18.1 %collective-permute-start.18 = (bf16[2,96,384]{2,1,0:T(8,128)(2,1)S(1)}, bf16[2,96,384]{2,1,0:T(8,128)(2,1)S(1)}, u32[]{:S(2)}, u32[]{:S(2)}) collective-permute-start(bf16[2,96,384]{2,1,0:T(8,128)(2,1)S(1)} %get-tuple-element.167), channel_id=1, source_target_pairs={{0,8},{1,9},{2,10},{3,11},{4,12},{5,13},{6,14},{7,15},{8,0},{9,1},... | collective-permute-start | bytes 442376 | tf_op jit(solution)/shard_map/ppermute | solution.py:558
  120.0 17.2 %collective-permute-start.19 = (bf16[2,96,384]{2,1,0:T(8,128)(2,1)S(1)}, bf16[2,96,384]{2,1,0:T(8,128)(2,1)S(1)}, u32[]{:S(2)}, u32[]{:S(2)}) collective-permute-start(bf16[2,96,384]{2,1,0:T(8,128)(2,1)S(1)} %get-tuple-element.168), channel_id=1, source_target_pairs={{0,16},{1,17},{2,18},{3,19},{4,20},{5,21},{6,22},{7,23},{8,24},{9,... | collective-permute-start | bytes 442376 | tf_op jit(solution)/shard_map/ppermute | solution.py:558
  122.6 18.1 %collective-permute-start.20 = (bf16[2,96,384]{2,1,0:T(8,128)(2,1)S(1)}, bf16[2,96,384]{2,1,0:T(8,128)(2,1)S(1)}, u32[]{:S(2)}, u32[]{:S(2)}) collective-permute-start(bf16[2,96,384]{2,1,0:T(8,128)(2,1)S(1)} %get-tuple-element.169), channel_id=1, source_target_pairs={{0,24},{1,25},{2,26},{3,27},{4,28},{5,29},{6,30},{7,31},{8,16},{9,... | collective-permute-start | bytes 442376 | tf_op jit(solution)/shard_map/ppermute | solution.py:558
  127.9 13.7 %collective-permute-start.21 = (bf16[2,4,80,384]{3,2,1,0:T(8,128)(2,1)S(1)}, bf16[2,4,80,384]{3,2,1,0:T(8,128)(2,1)S(1)}, u32[]{:S(2)}, u32[]{:S(2)}) collective-permute-start(bf16[2,4,80,384]{3,2,1,0:T(8,128)(2,1)S(1)} %get-tuple-element.160), channel_id=1, source_target_pairs={{0,1},{1,0},{2,3},{3,2},{4,5},{5,4},{6,7},{7,6},{8,9},{9,8},{10,11... | collective-permute-start | bytes 1474568 | tf_op jit(solution)/shard_map/ppermute | solution.py:558
  129.9 11.7 %collective-permute-start.22 = (bf16[2,4,80,384]{3,2,1,0:T(8,128)(2,1)S(1)}, bf16[2,4,80,384]{3,2,1,0:T(8,128)(2,1)S(1)}, u32[]{:S(2)}, u32[]{:S(2)}) collective-permute-start(bf16[2,4,80,384]{3,2,1,0:T(8,128)(2,1)S(1)} %get-tuple-element.174), channel_id=1, source_target_pairs={{0,4},{1,5},{2,6},{3,7},{4,0},{5,1},{6,2},{7,3},{8,12},{9,13},{10,... | collective-permute-start | bytes 1474568 | tf_op jit(solution)/shard_map/ppermute | solution.py:558
  136.5 8.2 %collective-permute-start.23 = (bf16[2,120,384]{2,1,0:T(8,128)(2,1)S(1)}, bf16[2,120,384]{2,1,0:T(8,128)(2,1)S(1)}, u32[]{:S(2)}, u32[]{:S(2)}) collective-permute-start(bf16[2,120,384]{2,1,0:T(8,128)(2,1)S(1)} %get-tuple-element.177), channel_id=1, source_target_pairs={{0,8},{1,9},{2,10},{3,11},{4,12},{5,13},{6,14},{7,15},{8,0},{9,1},... | collective-permute-start | bytes 552968 | tf_op jit(solution)/shard_map/ppermute | solution.py:558
  137.3 14.3 %collective-permute-start.24 = (bf16[2,120,384]{2,1,0:T(8,128)(2,1)S(1)}, bf16[2,120,384]{2,1,0:T(8,128)(2,1)S(1)}, u32[]{:S(2)}, u32[]{:S(2)}) collective-permute-start(bf16[2,120,384]{2,1,0:T(8,128)(2,1)S(1)} %get-tuple-element.178), channel_id=1, source_target_pairs={{0,16},{1,17},{2,18},{3,19},{4,20},{5,21},{6,22},{7,23},{8,24},{9,... | collective-permute-start | bytes 552968 | tf_op jit(solution)/shard_map/ppermute | solution.py:558
  140.7 10.8 %collective-permute-start.25 = (bf16[2,120,384]{2,1,0:T(8,128)(2,1)S(1)}, bf16[2,120,384]{2,1,0:T(8,128)(2,1)S(1)}, u32[]{:S(2)}, u32[]{:S(2)}) collective-permute-start(bf16[2,120,384]{2,1,0:T(8,128)(2,1)S(1)} %get-tuple-element.179), channel_id=1, source_target_pairs={{0,24},{1,25},{2,26},{3,27},{4,28},{5,29},{6,30},{7,31},{8,16},{9,... | collective-permute-start | bytes 552968 | tf_op jit(solution)/shard_map/ppermute | solution.py:558
  152.2 2.8 %collective-permute-start.32 = (f32[120,384]{1,0:T(8,128)S(1)}, f32[120,384]{1,0:T(8,128)S(1)}, u32[]{:S(2)}, u32[]{:S(2)}) collective-permute-start(f32[120,384]{1,0:T(8,128)S(1)} %get-tuple-element.189), channel_id=1, source_target_pairs={{0,2},{1,3},{2,0},{3,1},{4,6},{5,7},{6,4},{7,5},{8,10},{9,11},{10,... | collective-permute-start | bytes 552968 | tf_op jit(solution)/shard_map/ppermute | solution.py:558
  152.2 2.7 %collective-permute-start.33 = (f32[96,384]{1,0:T(8,128)S(1)}, f32[96,384]{1,0:T(8,128)S(1)}, u32[]{:S(2)}, u32[]{:S(2)}) collective-permute-start(f32[96,384]{1,0:T(8,128)S(1)} %get-tuple-element.190), channel_id=1, source_target_pairs={{0,2},{1,3},{2,0},{3,1},{4,6},{5,7},{6,4},{7,5},{8,10},{9,11},{10,... | collective-permute-start | bytes 442376 | tf_op jit(solution)/shard_map/ppermute | solution.py:558
  152.7 7.9 %collective-permute-start.26 = (bf16[4,80,384]{2,1,0:T(8,128)(2,1)S(1)}, bf16[4,80,384]{2,1,0:T(8,128)(2,1)S(1)}, u32[]{:S(2)}, u32[]{:S(2)}) collective-permute-start(bf16[4,80,384]{2,1,0:T(8,128)(2,1)S(1)} %get-tuple-element.175), channel_id=1, source_target_pairs={{0,4},{1,5},{2,6},{3,7},{4,0},{5,1},{6,2},{7,3},{8,12},{9,13},{10,... | collective-permute-start | bytes 737288 | tf_op jit(solution)/shard_map/ppermute | solution.py:558
  154.3 7.7 %collective-permute-start.27 = (bf16[4,80,384]{2,1,0:T(8,128)(2,1)S(1)}, bf16[4,80,384]{2,1,0:T(8,128)(2,1)S(1)}, u32[]{:S(2)}, u32[]{:S(2)}) collective-permute-start(bf16[4,80,384]{2,1,0:T(8,128)(2,1)S(1)} %get-tuple-element.182), channel_id=1, source_target_pairs={{0,1},{1,0},{2,3},{3,2},{4,5},{5,4},{6,7},{7,6},{8,9},{9,8},{10,11... | collective-permute-start | bytes 737288 | tf_op jit(solution)/shard_map/ppermute | solution.py:558
  162.7 6.7 %collective-permute-start.28 = (bf16[2,80,384]{2,1,0:T(8,128)(2,1)S(1)}, bf16[2,80,384]{2,1,0:T(8,128)(2,1)S(1)}, u32[]{:S(2)}, u32[]{:S(2)}) collective-permute-start(bf16[2,80,384]{2,1,0:T(8,128)(2,1)S(1)} %get-tuple-element.184), channel_id=1, source_target_pairs={{0,8},{1,9},{2,10},{3,11},{4,12},{5,13},{6,14},{7,15},{8,0},{9,1},... | collective-permute-start | bytes 368648 | tf_op jit(solution)/shard_map/ppermute | solution.py:558
  165.3 11.4 %collective-permute-start.29 = (bf16[2,80,384]{2,1,0:T(8,128)(2,1)S(1)}, bf16[2,80,384]{2,1,0:T(8,128)(2,1)S(1)}, u32[]{:S(2)}, u32[]{:S(2)}) collective-permute-start(bf16[2,80,384]{2,1,0:T(8,128)(2,1)S(1)} %get-tuple-element.185), channel_id=1, source_target_pairs={{0,16},{1,17},{2,18},{3,19},{4,20},{5,21},{6,22},{7,23},{8,24},{9,... | collective-permute-start | bytes 368648 | tf_op jit(solution)/shard_map/ppermute | solution.py:558
  166.4 10.3 %collective-permute-start.30 = (bf16[2,80,384]{2,1,0:T(8,128)(2,1)S(1)}, bf16[2,80,384]{2,1,0:T(8,128)(2,1)S(1)}, u32[]{:S(2)}, u32[]{:S(2)}) collective-permute-start(bf16[2,80,384]{2,1,0:T(8,128)(2,1)S(1)} %get-tuple-element.186), channel_id=1, source_target_pairs={{0,24},{1,25},{2,26},{3,27},{4,28},{5,29},{6,30},{7,31},{8,16},{9,... | collective-permute-start | bytes 368648 | tf_op jit(solution)/shard_map/ppermute | solution.py:558
  177.3 1.5 collective-permute-start.31
  (64 other events, 331.1 us)

commit v3 on v2

--- a/solution.py
+++ b/solution.py
@@ -16,9 +16,16 @@
 BF = jnp.bfloat16
 F32 = jnp.float32
 AXES = ("dp", "head")
-VMEM_LIMIT = 20 * 1024 * 1024
+VMEM_LIMIT = 8 << 20
+VMEM_FFN = 11 << 20
 FF_BLOCK = 768
 MATMUL_PER_US = 1.15e9
+COST_EXPAND = 1
+VMEM_BACK = 16 << 20
+COST_KEPT = 5
+COST_SENT = 0.5
+COST_HEADS = 0.1
+COST_INPUT = 0.1
 FF_STEPS = FF // FF_BLOCK
 
 
@@ -35,7 +42,11 @@
 
 
 def call(kernel, name, scal, grid, ins, outs, scratch=(), us=1, vmem=VMEM_LIMIT):
-    spec = lambda b, m: pl.BlockSpec(memory_space=pltpu.VMEM) if b is None else pl.BlockSpec(b, m)
+    def spec(b, m):
+        if b is None:
+            return pl.BlockSpec(memory_space=pltpu.VMEM if m is None else m)
+        return pl.BlockSpec(b, m)
+
     in_specs = [spec(b, m) for _, b, m in ins]
     out_specs = [spec(b, m) for _, _, b, m in outs]
     return pl.pallas_call(
@@ -133,7 +144,14 @@
     return of_cos, of_sin, pick(0), pick(2)
 
 
-def kv_kernel(seqs, scal, tok, wk, wv, bk, bv, rk_o, v_o, st_o, tcol, trow, norms):
+def turn(value, out):
+    turned = value.T
+    share = out.shape[1]
+    for n in range(out.shape[0]):
+        out[n] = turned[n * share : (n + 1) * share]
+
+
+def kv_kernel(seqs, scal, tok, wk, wv, bk, bv, rk_o, v_o, st_o, tcol, trow, turned_o, norms):
     step = pl.program_id(0)
     rows = tok.shape[0]
 
@@ -141,6 +159,7 @@
     def _():
         tables(scal, rows, seqs, tcol, trow)
         norms[...] = jnp.zeros_like(norms)
+        turn(tok[...], turned_o)
 
     rk = jnp.maximum(dot(tok[...], wk[...]) + bk[...].astype(F32), 0.0).astype(BF)
     v = (dot(tok[...], wv[...]) + bv[...].astype(F32)).astype(BF)
@@ -212,7 +231,7 @@
 
 def merge_heads(
     head_at, scal, rq, num, den, st, tcol, tok, w_merge, b_merge, gain, bias, b_red,
-    att_o, inv_o, mixed_o, xhat_o, scale_o, normed_o, acc_o,
+    att_o, inv_o, mixed_o, xhat_o, scale_o, normed_o, acc_o, turned_o,
 ):
     cross = (scal[head_at] == 1).astype(F32)
     cos_b, sin_b = tcol[:, 3:4] * cross, tcol[:, 4:5] * cross
@@ -238,6 +257,8 @@
     scale_o[...] = jnp.broadcast_to(scale, scale_o.shape)
     normed_o[...] = normed.astype(BF)
     acc_o[...] = normed + b_red[...].astype(F32)
+    turn(mixed_o[...], turned_o.at[0])
+    turn(normed_o[...], turned_o.at[1])
 
 
 def expand_reduce(normed, w_exp, b_exp, w_red, act_o, slope_o):
@@ -252,11 +273,12 @@
 
 def ffn_kernel(head_at, scal, *refs):
     w_exp, b_exp, w_red = refs[11:14]
-    normed_o, acc_o, act_o, slope_o = refs[19:]
+    normed_o, acc_o = refs[19:21]
+    act_o, slope_o = refs[22:]
 
     @pl.when(pl.program_id(0) == 0)
     def _():
-        merge_heads(head_at, scal, *refs[:11], *refs[14:21])
+        merge_heads(head_at, scal, *refs[:11], *refs[14:22])
 
     acc_o[...] += expand_reduce(normed_o, w_exp, b_exp, w_red, act_o, slope_o)
 
@@ -288,88 +310,114 @@
     return (lane == at) | (lane == at + 1)
 
 
-def back_step(full, slope, w_exp, w_red, out_o, bexp_o):
-    pre_grad = (dot_r(full[...], w_red[...]) * slope[...].astype(F32)).astype(BF)
-    bexp_o[...] = jnp.sum(pre_grad.astype(F32), axis=0, keepdims=True)
-    out_o[0] = pre_grad
-    return dot_r(pre_grad, w_exp[...])
-
-
-def back_sent_kernel(scal, full, slope, w_exp, w_red, grad2, sent_o, bexp_o, acc):
-    @pl.when(pl.program_id(0) == 0)
-    def _():
-        acc[...] = grad2[...]
-
-    acc[...] += back_step(full, slope, w_exp, w_red, sent_o, bexp_o)
+def weight_copies(half, w_exp, w_red, exp_buf, red_buf, sems, n):
+    at = pl.ds(pl.multiple_of((half * exp_buf.shape[0] + n) * FF_BLOCK, FF_BLOCK), FF_BLOCK)
+    return (
+        pltpu.make_async_copy(w_red.at[at, :], red_buf.at[n], sems.at[0, n]),
+        pltpu.make_async_copy(w_exp.at[:, at], exp_buf.at[n], sems.at[1, n]),
+    )
+
+
+def back_steps(half, full, slope, w_exp, w_red, out_o, bexp_o, exp_buf, red_buf, sems):
+    blocks = exp_buf.shape[0]
+    copies = [weight_copies(half, w_exp, w_red, exp_buf, red_buf, sems, n) for n in range(blocks)]
+    for pair in copies:
+        for copy in pair:
+            copy.start()
+    total = None
+    for n, (of_red, of_exp) in enumerate(copies):
+        cols = slice(n * FF_BLOCK, (n + 1) * FF_BLOCK)
+        at = pl.ds(pl.multiple_of((half * blocks + n) * FF_BLOCK, FF_BLOCK), FF_BLOCK)
+        of_red.wait()
+        pre_grad = (dot_r(full[...], red_buf[n]) * slope[:, at].astype(F32)).astype(BF)
+        bexp_o[:, cols] = jnp.sum(pre_grad.astype(F32), axis=0, keepdims=True)
+        out_o[n] = pre_grad
+        of_exp.wait()
+        part = dot_r(pre_grad, exp_buf[n])
+        total = part if total is None else total + part
+    return total
+
+
+def back_sent_kernel(core_at, scal, full, slope, w_exp, w_red, grad2, sent_o, bexp_o, acc, exp_buf, red_buf, sems):
+    half = 1 - scal[core_at]
+    acc[...] = grad2[...] + back_steps(half, full, slope, w_exp, w_red, sent_o, bexp_o, exp_buf, red_buf, sems)
 
 
 def back_kernel(
     core_at, scal, full, slope, w_exp, w_red, acc_in, gain, xhat, scale, w_merge, att, inv, rq, tcol,
     kept_o, first_o, mk_o, ms_o, w_o, e_o, st_o, bexp_o, sums_o,
-    acc,
+    acc, exp_buf, red_buf, sems,
 ):
-    step = pl.program_id(0)
-
-    @pl.when(step == 0)
-    def _():
-        acc[...] = acc_in[...]
-
-    acc[...] += back_step(full, slope, w_exp, w_red, kept_o, bexp_o)
-
-    @pl.when(step == pl.num_programs(0) - 1)
-    def _():
-        grad_normed = acc[...]
-        xh = xhat[...]
-        t = grad_normed * gain[...].astype(F32)
-        first = scale[:, 0:1] * (
-            t - jnp.mean(t, axis=1, keepdims=True) - xh * jnp.mean(t * xh, axis=1, keepdims=True)
-        )
-        low = first.astype(BF)
-        first_o[...] = first
-        sums_o[0:1] = jnp.sum(grad_normed * xh, axis=0, keepdims=True)
-        sums_o[1:2] = jnp.sum(grad_normed, axis=0, keepdims=True)
-        sums_o[2:3] = jnp.sum(low.astype(F32), axis=0, keepdims=True)
-        is_first = scal[core_at] == 0
-        left, right = first[:, : D // 2], first[:, D // 2 :]
-        mk_o[...] = jnp.where(is_first, left, right).astype(BF)
-        ms_o[...] = jnp.where(is_first, right, left).astype(BF)
-        cos_b, sin_b = tcol[:, 3:4], tcol[:, 4:5]
-        w = (dot_r(low, w_merge[...]).astype(BF).astype(F32) * inv[...]).astype(BF)
-        w_o[...] = w
-        high, rest = high_low(w.astype(F32) * att[...])
-        column = lax.broadcasted_iota(jnp.int32, (D, LANES), 0)
-        target = lax.broadcasted_iota(jnp.int32, (D, LANES), 1)
-        picks = (target == 2 * (column // HALF)).astype(F32).astype(BF)
-        e_high, e_low = high_low(-(dot(high.astype(BF), picks) + dot(rest.astype(BF), picks)))
-        e = (e_high + pltpu.roll(e_low, 1, 1)).astype(BF)
-        e_o[...] = e
-        norms = jnp.zeros((LANES, LANES), F32)
-        sq_lane, upper, diag = square_masks()
-        for pair in range(PAIRS):
-            cols = slice(pair * LANES, (pair + 1) * LANES)
-            qp = rq[:, cols].astype(F32)
-            left = jnp.concatenate([(qp * cos_b).astype(BF), (qp * sin_b).astype(BF)], axis=1)
-            both = dot_t(left, jnp.concatenate([w[:, cols], e], axis=1))
-            mine = head_lanes(pair, sq_lane, upper)
-            norm = lambda part: jnp.sum(jnp.where(mine, part, 0.0), axis=1, keepdims=True)
-            packed, norms = pack_state(both, norm(both[:LANES, LANES:]), norm(both[LANES:, LANES:]), pair, norms)
-            st_o[pair] = packed
-        st_o[PAIRS] = norms.astype(BF)
-
-
-def attn_back_kernel(
-    head_at, core_at, scal, rq, rk, v, w, e, prior, later, tcol, trow,
-    pk_o, ps_o, sums_o,
-    weights, weights_t,
+    half = scal[core_at]
+    acc[...] = acc_in[...] + back_steps(half, full, slope, w_exp, w_red, kept_o, bexp_o, exp_buf, red_buf, sems)
+    back_rest(
+        core_at, scal, acc, gain, xhat, scale, w_merge, att, inv, rq, tcol,
+        first_o, mk_o, ms_o, w_o, e_o, st_o, sums_o,
+    )
+
+
+def back_rest(
+    core_at, scal, acc, gain, xhat, scale, w_merge, att, inv, rq, tcol,
+    first_o, mk_o, ms_o, w_o, e_o, st_o, sums_o,
 ):
-    pair = pl.program_id(0)
-    rows = rq.shape[0]
-    mid = rows // 2
-
-    @pl.when(pair == 0)
+    grad_normed = acc[...]
+    xh = xhat[...]
+    t = grad_normed * gain[...].astype(F32)
+    first = scale[:, 0:1] * (
+        t - jnp.mean(t, axis=1, keepdims=True) - xh * jnp.mean(t * xh, axis=1, keepdims=True)
+    )
+    low = first.astype(BF)
+    first_o[...] = first
+    sums_o[0:1] = jnp.sum(grad_normed * xh, axis=0, keepdims=True)
+    sums_o[1:2] = jnp.sum(grad_normed, axis=0, keepdims=True)
+    sums_o[2:3] = jnp.sum(low.astype(F32), axis=0, keepdims=True)
+    is_first = scal[core_at] == 0
+    left, right = first[:, : D // 2], first[:, D // 2 :]
+    mk_o[...] = jnp.where(is_first, left, right).astype(BF)
+    ms_o[...] = jnp.where(is_first, right, left).astype(BF)
+    cos_b, sin_b = tcol[:, 3:4], tcol[:, 4:5]
+    w = (dot_r(low, w_merge[...]).astype(BF).astype(F32) * inv[...]).astype(BF)
+    w_o[...] = w
+    high, rest = high_low(w.astype(F32) * att[...])
+    column = lax.broadcasted_iota(jnp.int32, (D, LANES), 0)
+    target = lax.broadcasted_iota(jnp.int32, (D, LANES), 1)
+    picks = (target == 2 * (column // HALF)).astype(F32).astype(BF)
+    e_high, e_low = high_low(-(dot(high.astype(BF), picks) + dot(rest.astype(BF), picks)))
+    e = (e_high + pltpu.roll(e_low, 1, 1)).astype(BF)
+    e_o[...] = e
+    norms = jnp.zeros((LANES, LANES), F32)
+    sq_lane, upper, diag = square_masks()
+    for pair in range(PAIRS):
+        cols = slice(pair * LANES, (pair + 1) * LANES)
+        qp = rq[:, cols].astype(F32)
+        left = jnp.concatenate([(qp * cos_b).astype(BF), (qp * sin_b).astype(BF)], axis=1)
+        both = dot_t(left, jnp.concatenate([w[:, cols], e], axis=1))
+        mine = head_lanes(pair, sq_lane, upper)
+        norm = lambda part: jnp.sum(jnp.where(mine, part, 0.0), axis=1, keepdims=True)
+        packed, norms = pack_state(both, norm(both[:LANES, LANES:]), norm(both[LANES:, LANES:]), pair, norms)
+        st_o[pair] = packed
+    st_o[PAIRS] = norms.astype(BF)
+
+
+def attn_sent_kernel(head_at, core_at, scal, rq, rk, v, w, e, prior, later, tcol, trow, out_o, sums_o, weights, weights_t):
+    @pl.when(pl.program_id(0) == 0)
     def _():
         weights[...] = weights_block(tcol, trow, False)
         weights_t[...] = weights_block(tcol, trow, True)
+
+    first = (1 - scal[core_at]) * pl.num_programs(0)
+    attn_back(head_at, first, scal, rq, rk, v, w, e, prior, later, tcol, weights, weights_t, out_o, sums_o)
+
+
+def attn_kept_kernel(head_at, core_at, scal, rq, rk, v, w, e, prior, later, tcol, weights, weights_t, out_o, sums_o):
+    first = scal[core_at] * pl.num_programs(0)
+    attn_back(head_at, first, scal, rq, rk, v, w, e, prior, later, tcol, weights, weights_t, out_o, sums_o)
+
+
+def attn_back(head_at, first, scal, rq, rk, v, w, e, prior, later, tcol, weights, weights_t, out_o, sums_o):
+    pair = first + pl.program_id(0)
+    rows = rq.shape[0]
+    mid = rows // 2
 
     qp, kp, vp, wp = rq[...], rk[...], v[...], w[...]
     lane, even, odd = lane_masks()
@@ -423,20 +471,9 @@
     dq = jnp.where(qp.astype(F32) > 0, dq, 0.0).astype(BF)
     dk = jnp.where(kw > 0, dk, 0.0).astype(BF)
     dv = dv.astype(BF)
-    blocks = 3 * PAIRS // 2
     for n, part in enumerate((dq, dk, dv)):
         sums_o[n] = jnp.broadcast_to(jnp.sum(part.astype(F32), axis=0, keepdims=True), sums_o.shape[1:])
-        at = n * PAIRS + pair
-        mine = (at >= blocks) == (scal[core_at] == 1)
-        slot = lax.rem(at, blocks)
-
-        @pl.when(mine)
-        def _():
-            pk_o[slot] = part
-
-        @pl.when(jnp.logical_not(mine))
-        def _():
-            ps_o[slot] = part
+        out_o[n] = part
 
 
 def input_kernel(scal, first, keep, send, w_keep, w_send, out_o):
@@ -444,8 +481,7 @@
     def _():
         out_o[...] = first[...]
 
-    left = lambda ref: jnp.concatenate([ref[n] for n in range(ref.shape[0])], axis=1)
-    out_o[...] += dot_r(left(keep), w_keep[...]) + dot_r(left(send), w_send[...])
+    out_o[...] += dot_r(keep[0], w_keep[...]) + dot_r(send[0], w_send[...])
 
 
 def place(values, piece_rows, tz, tys, x, y, z, extra, outs):
@@ -493,9 +529,9 @@
 def expand_grad_kernel(pos_at, scal, a_own, a_oth, b_own, b_oth, m_own, m_oth, c_own, c_oth, *outs):
     tz = pl.program_id(0)
     x, y, z = (scal[pos_at + n] for n in range(3))
-    an, ao = a_own[0], a_oth[0]
+    an, ao = a_own[0, 0], a_oth[0, 0]
     parts = [dot(an, b_own[n]) + dot(ao, b_oth[n]) for n in range(b_own.shape[0])]
-    parts.append(dot(m_own[0], c_own[...]) + dot(m_oth[0], c_oth[...]))
+    parts.append(dot(m_own[0, 0], c_own[...]) + dot(m_oth[0, 0], c_oth[...]))
     values = jnp.concatenate(parts, axis=1)
     pieces = place(values, values.shape[0] // 8, tz, (0, 1), x, y, z, None, outs)
     place_y(pieces, tz, (0, 1), x, y, z, outs)
@@ -517,7 +553,7 @@
 
 
 def heads_grad_kernel(
-    pos_at, scal, a_own, a_oth, b_own, b_oth, sums_q, sums_k, sums_v, sums_1, sums_e, sums_2, *refs, devices
+    pos_at, scal, a_own, a_oth, b_own, b_oth, kept_h, sent_h, sums_1, kept_e, sent_e, sums_2, *refs, devices
 ):
     outs, table = refs[:-1], refs[-1]
     tz = pl.program_id(0)
@@ -526,12 +562,15 @@
 
     @pl.when(tz == 0)
     def _():
-        scores = jnp.concatenate([sums_q[0, 0:1], sums_k[0, 0:1]], axis=1)
+        first_core = scal[pos_at - 1] == 0
+        ordered = lambda kept, sent: [jnp.where(first_core, kept, sent), jnp.where(first_core, sent, kept)]
+        sums_e = jnp.concatenate(ordered(kept_e[...], sent_e[...]), axis=1)
+        of_heads = [part for n in range(3) for part in ordered(kept_h[n, 0:1], sent_h[n, 0:1])]
         total = jnp.zeros((devices, width), F32)
         at = 0
         for entries in (
-            scores, sums_v[0, 0:1], sums_1[2:3], sums_1[0:1], sums_1[1:2],
-            sums_e[...], sums_2[2:3], sums_2[0:1], sums_2[1:2],
+            jnp.concatenate(of_heads[:4], axis=1), jnp.concatenate(of_heads[4:], axis=1), sums_1[2:3], sums_1[0:1], sums_1[1:2],
+            sums_e, sums_2[2:3], sums_2[0:1], sums_2[1:2],
         ):
             total = total + share_lanes(entries, devices, at, width)
             at += entries.shape[1] // devices
@@ -597,23 +636,23 @@
         self.ring, self.core_at, self.name = ring, core_at, name
         self.xk, self.xs, self.yk, self.ys = sent
 
-    def send(self):
-        self.xr, self.yr = self.ring.x(self.xs), self.ring.y(self.ys)
-
-    def first(self, scal):
+    def send(self, *others):
+        self.xr, self.yr = self.ring.x(after(self.xs, *others)), self.ring.y(after(self.ys, *others))
+
+    def first(self, scal, us=1):
         shape = self.xk.shape[1:]
         part = lambda a: (a, (1,) + shape, lambda j, s: (1, 0, 0, 0))
         xn, yn = call(
             add_first_kernel, self.name + "_add1", scal, (1,), [part(a) for a in (self.xk, self.xr, self.yk, self.yr)],
-            [(shape, BF, None, None)] * 2,
+            [(shape, BF, None, None)] * 2, us=us,
         )
         self.xn, self.yn = xn, yn
         return xn
 
-    def send_first(self):
-        self.xm, self.ym = self.ring.y(self.xn), self.ring.x(self.yn)
-
-    def second(self, scal, us=1):
+    def send_first(self, *others):
+        self.xm, self.ym = self.ring.y(after(self.xn, *others)), self.ring.x(after(self.yn, *others))
+
+    def second(self, scal):
         shape = self.xk.shape[1:]
         piece = (2,) + shape[1:]
         part = lambda a: (a, (1,) + shape, lambda j, s: (0, 0, 0, 0))
@@ -621,12 +660,12 @@
         self.own, *self.sends = call(
             add_second_kernel, self.name + "_add2", scal, (1,),
             [part(self.xk), part(self.xr), whole(self.xm), part(self.yk), part(self.yr), whole(self.ym)],
-            [(piece, F32, None, None)] + [(piece, BF, None, None)] * 3, us=us,
+            [(piece, F32, None, None)] + [(piece, BF, None, None)] * 3,
         )
         return self.own
 
-    def send_second(self):
-        self.arrived = [self.ring.z(v, k + 1) for k, v in enumerate(self.sends)]
+    def send_second(self, *others):
+        self.arrived = [self.ring.z(after(v, *others), k + 1) for k, v in enumerate(self.sends)]
 
     def last(self, scal):
         piece = self.own.shape[1:]
@@ -638,21 +677,44 @@
 
 
 def after(value, *others):
+    if not others:
+        return value
     return lax.optimization_barrier((value,) + others)[0]
 
 
-def halves(first_core, own, other):
-    left = jnp.where(first_core, own, other)
-    right = jnp.where(first_core, other, own)
-    return jnp.concatenate([left, right], axis=1)
-
-
-def columns(part, rows, blocks):
-    return part.reshape(blocks, rows, part.shape[-1]).transpose(1, 0, 2).reshape(rows, -1)
-
-
-def transposed_pieces(value):
-    return value.T.reshape(4, D // 4, value.shape[0])
+def side_by_side(core_at, scal, own, got):
+    first = scal[core_at] == 0
+    return [jnp.where(first, own, got), jnp.where(first, got, own)]
+
+
+def finish_first_kernel(core_at, scal, reduce_own, reduce_got, expand_own, expand_got, reduce_o, expand_o, merge_o):
+    width = reduce_own.shape[1]
+    for n, part in enumerate(side_by_side(core_at, scal, reduce_own[...], reduce_got[...])):
+        reduce_o[:, n * width : (n + 1) * width] = part
+    rows = merge_o.shape[0]
+    blocks = expand_own.shape[0] // rows - 1
+    for n, part in enumerate(side_by_side(core_at, scal, expand_own[...], expand_got[...])):
+        for k in range(blocks):
+            at = (n * blocks + k) * width
+            expand_o[:, at : at + width] = part[k * rows : (k + 1) * rows]
+        merge_o[:, n * width : (n + 1) * width] = part[blocks * rows :]
+
+
+def finish_last_kernel(core_at, scal, own, got, heads_o, *shares_o):
+    width = own.shape[1]
+    rows = heads_o.shape[0]
+    for n, part in enumerate(side_by_side(core_at, scal, own[...], got[...])):
+        for k in range(3):
+            at = (2 * k + n) * width
+            heads_o[:, at : at + width] = part[k * rows : (k + 1) * rows]
+    entries = own[3 * rows :] + got[3 * rows :]
+    entries = entries[0:1] + entries[1:2]
+    at = 0
+    for share in shares_o:
+        n = share.shape[1]
+        moved = entries if at == 0 else pltpu.roll(entries, width - at, 1)
+        share[...] = moved[:, :n]
+        at += n
 
 
 def per_device(
@@ -677,7 +739,8 @@
     wide_shape = (rows, D)
     quarter = 256
 
-    rk, v, state, tcol, trow = call(
+    turned = ((4, D // 4, rows), BF, None, None)
+    rk, v, state, tcol, trow, tokens_t = call(
         functools.partial(kv_kernel, seqs), "keys_values", scal, (3,),
         [
             (tokens, None, None),
@@ -691,19 +754,16 @@
             (wide_shape, BF, (rows, quarter), lambda j, s: (0, j)),
             ((PAIRS + 1, LANES, LANES), BF, None, None),
             ((rows, LANES), F32, None, None),
-            ((8, rows), F32, None, None),
+            ((8, rows), F32, None, None), turned,
         ],
         [pltpu.VMEM((LANES, LANES), F32)],
         us=4,
     )
-    forward = [(i, i + 1) for i in range(0, 2 * n_dp, 2)]
-    backward = [(b, a) for a, b in forward]
-    prior = lax.ppermute(state, AXES, forward)
+    prior = ring.x(state)
 
     fast = n_dp == 16
     order = scal
     if fast:
-        tokens_t = transposed_pieces(tokens)
         tokens_o = ring.core(tokens_t)
     rq, num, den = call(
         local_kernel, "local_attention", scal, (3,),
@@ -727,7 +787,7 @@
 
     if fast:
         order = after(scal, tokens_o)
-    att, inv, mixed, xhat, scale, normed, second, act, slope = call(
+    att, inv, mixed, xhat, scale, normed, second, turned_own, act, slope = call(
         functools.partial(ffn_kernel, head_at), "feed_forward", order, (FF_STEPS,),
         [
             (rq, None, None), (num, None, None), (den, None, None), (prior, None, None),
@@ -740,14 +800,13 @@
         [
             (wide_shape, F32, None, None), (wide_shape, F32, None, None), (wide_shape, BF, None, None),
             (wide_shape, F32, None, None), ((rows, LANES), F32, None, None), (wide_shape, BF, None, None),
-            (wide_shape, F32, None, None),
+            (wide_shape, F32, None, None), ((2, 4, D // 4, rows), BF, None, None),
             ((rows, FF), BF, (rows, FF_BLOCK), lambda j, s: (0, j)),
             ((rows, FF), BF, (rows, FF_BLOCK), lambda j, s: (0, j)),
         ],
-        us=11,
-    )
-
-    normed_t, mixed_t = map(transposed_pieces, (normed, mixed))
+        us=11, vmem=VMEM_FFN,
+    )
+
     half_shape = (rows, D // 2)
     result, grad_second, branch, bg_keep, bg_send, sums_second = call(
         functools.partial(second_kernel, core_at), "second_norm", scal, (1,),
@@ -762,6 +821,7 @@
     devices = ring.devices
     small, large = D // devices, FF // devices
     whole = lambda a: (a, None, None)
+    part = lambda a, n: (a, (1, 1, D // 4, rows), lambda j, s: (n, j, 0, 0))
     by_z = lambda a: (a, (1, D // 4, rows), lambda j, s: (j, 0, 0))
     by_col = lambda a: (a, (rows, FF // 4), lambda j, s: (0, j))
 
@@ -773,34 +833,35 @@
         return Scatter(ring, core_at, name, sent)
 
     ff_half = FF_STEPS // 2
-    half_of = lambda core_of: [
-        (slope, (rows, FF_BLOCK), lambda j, s: (0, core_of(s) * ff_half + j)),
-        (w_expand, (D, FF_BLOCK), lambda j, s: (0, core_of(s) * ff_half + j)),
-        (w_reduce, (FF_BLOCK, D), lambda j, s: (core_of(s) * ff_half + j, 0)),
+    in_hbm = lambda a: (a, None, pltpu.HBM)
+    hidden = ((ff_half, rows, FF_BLOCK), BF, None, None)
+    hidden_sums = ((1, FF // 2), F32, None, None)
+    buffers = [
+        pltpu.VMEM((ff_half, D, FF_BLOCK), BF), pltpu.VMEM((ff_half, FF_BLOCK, D), BF),
+        pltpu.SemaphoreType.DMA((2, ff_half)),
     ]
-    hidden = ((ff_half, rows, FF_BLOCK), BF, (1, rows, FF_BLOCK), lambda j, s: (j, 0, 0))
-    hidden_sums = ((1, FF // 2), F32, (1, FF_BLOCK), lambda j, s: (0, j))
+    hidden_in = [whole(branch), whole(slope), in_hbm(w_expand), in_hbm(w_reduce)]
     pg_send, sum_sent, partial = call(
-        back_sent_kernel, "feed_forward_back_sent", scal, (ff_half,),
-        [(branch, None, None), *half_of(lambda s: 1 - s[core_at]), (grad_second, None, None)],
-        [hidden, hidden_sums, (wide_shape, F32, None, None)],
-        us=5,
+        functools.partial(back_sent_kernel, core_at), "feed_forward_back_sent", scal, (),
+        [*hidden_in, whole(grad_second)],
+        [hidden, hidden_sums, (wide_shape, F32, None, None)], buffers,
+        us=5, vmem=VMEM_BACK,
     )
     order = scal
     if fast:
         pg_o = ring.core(pg_send)
-        act_o, normed_o, mixed_o, bg_o = map(ring.core, (act, normed_t, mixed_t, bg_send))
+        act_o, turned_other, bg_o = map(ring.core, (act, turned_own, bg_send))
         reduced = group(
-            reduce_grad_kernel, "grad_reduce", after(scal, partial),
+            reduce_grad_kernel, "grad_reduce", after(scal, partial, turned_other),
             [by_col(act), by_col(act_o), whole(bg_keep), whole(bg_o)], large, 6,
         )
         order = after(scal, reduced.xs)
         reduced.send()
 
     pg_keep, grad_first, mg_keep, mg_send, w_att, e_att, later, sum_kept, sums_first = call(
-        functools.partial(back_kernel, core_at), "feed_forward_back", order, (ff_half,),
+        functools.partial(back_kernel, core_at), "feed_forward_back", order, (),
         [
-            (branch, None, None), *half_of(lambda s: s[core_at]),
+            *hidden_in,
             (partial, None, None), (gain_first, None, None), (xhat, None, None), (scale, None, None),
             (w_merge, None, None), (att, None, None), (inv, None, None), (rq, None, None), (tcol, None, None),
         ],
@@ -809,103 +870,95 @@
             (wide_shape, BF, None, None), ((rows, LANES), BF, None, None),
             ((PAIRS + 1, LANES, LANES), BF, None, None), hidden_sums, ((8, D), F32, None, None),
         ],
-        [pltpu.VMEM(wide_shape, F32)],
-        us=9,
-    )
-    sum_expand = jnp.where(
-        first_core, jnp.concatenate([sum_kept, sum_sent], axis=1), jnp.concatenate([sum_sent, sum_kept], axis=1)
-    )
-    later = lax.ppermute(later, AXES, backward)
+        [pltpu.VMEM(wide_shape, F32), *buffers],
+        us=9, vmem=VMEM_BACK,
+    )
+    later = ring.x(later)
 
     if fast:
         mg_o = ring.core(mg_send)
         expanded = group(
             expand_grad_kernel, "grad_expand", scal,
             [
-                by_z(normed_t), by_z(normed_o), whole(pg_keep), whole(pg_o),
-                by_z(mixed_t), by_z(mixed_o), whole(mg_keep), whole(mg_o),
+                part(turned_own, 1), part(turned_other, 1), whole(pg_keep), whole(pg_o),
+                part(turned_own, 0), part(turned_other, 0), whole(mg_keep), whole(mg_o),
             ],
-            5 * small, 0.5,
-        )
-        expanded.send()
-        order = after(scal, reduced.first(after(scal, expanded.xs)))
+            5 * small, COST_EXPAND,
+        )
+        order = after(scal, reduced.first(after(scal, expanded.xs, later)))
         reduced.send_first()
 
-    blocks = 3 * PAIRS // 2
-    pair_block = lambda a: (a, (rows, LANES), lambda j, s: (0, j))
-    pj_keep, pj_send, sum_heads = call(
-        functools.partial(attn_back_kernel, head_at, core_at), "attention_back", order, (PAIRS,),
-        [
-            pair_block(rq), pair_block(rk), pair_block(v), pair_block(w_att), whole(e_att),
-            (prior, None, None), (later, None, None), (tcol, None, None), (trow, None, None),
-        ],
-        [
-            ((blocks, rows, LANES), BF, None, None), ((blocks, rows, LANES), BF, None, None),
-            ((3, 8, D), F32, (3, 8, LANES), lambda j, s: (0, 0, j)),
-        ],
-        [pltpu.VMEM((rows, rows), F32), pltpu.VMEM((rows, rows), F32)],
-        us=14,
-    )
-
+    half_pairs = PAIRS // 2
+    pair_blocks = lambda core_of: [
+        (a, (rows, LANES), lambda j, s: (0, core_of(s) * half_pairs + j)) for a in (rq, rk, v, w_att)
+    ]
+    both_states = [whole(e_att), whole(prior), whole(later), whole(tcol)]
+    pj_out = ((3, rows, D // 2), BF, (3, rows, LANES), lambda j, s: (0, 0, j))
+    pj_sums = ((3, 8, D // 2), F32, (3, 8, LANES), lambda j, s: (0, 0, j))
+    table = ((rows, rows), F32, None, None)
+    pj_send, sum_heads_sent, weights, weights_t = call(
+        functools.partial(attn_sent_kernel, head_at, core_at), "attention_back_sent", order, (half_pairs,),
+        [*pair_blocks(lambda s: 1 - s[core_at]), *both_states, whole(trow)], [pj_out, pj_sums, table, table], us=COST_SENT,
+    )
+    order = scal
     if fast:
         pj_o = ring.core(pj_send)
-        order = expanded.first(after(scal, pj_send))
-        expanded.send_first()
-        order = reduced.second(after(scal, order), us=12)
+        order = after(scal, reduced.second(after(scal, pj_send)))
+        expanded.send()
+    pj_keep, sum_heads_kept = call(
+        functools.partial(attn_kept_kernel, head_at, core_at), "attention_back_kept", order, (half_pairs,),
+        [*pair_blocks(lambda s: s[core_at]), *both_states, whole(weights), whole(weights_t)], [pj_out, pj_sums], us=COST_KEPT,
+    )
+
+    if fast:
+        order = after(scal, expanded.first(after(scal, pj_keep), us=20))
+        expanded.send_first(pj_o)
         reduced.send_second()
         heads = group(
-            functools.partial(heads_grad_kernel, devices=devices), "grad_heads", after(scal, order),
+            functools.partial(heads_grad_kernel, devices=devices), "grad_heads", order,
             [
                 by_z(tokens_t), by_z(tokens_o), whole(pj_keep), whole(pj_o),
-                *((sum_heads, (1, 8, D), lambda j, s, n=n: (n, 0, 0)) for n in range(3)),
-                whole(sums_first), whole(sum_expand), whole(sums_second),
+                *map(whole, (sum_heads_kept, sum_heads_sent, sums_first, sum_kept, sum_sent, sums_second)),
             ],
-            3 * small + 8, 5, [pltpu.VMEM((devices, D // 2), F32)],
-        )
-        heads.send()
+            3 * small + 8, COST_HEADS, [pltpu.VMEM((devices, D // 2), F32)],
+        )
+        heads.send(expanded.xm, expanded.ym)
         order = after(scal, heads.xs)
 
-    third = blocks // 3
-    wide_block = third * LANES
+    of_part = lambda a: (a, (1, rows, D // 2), lambda j, s: (j, 0, 0))
     (input_grad,) = call(
         input_kernel, "input_grad", order, (3,),
         [
-            (grad_first, None, None),
-            (pj_keep, (third, rows, LANES), lambda j, s: (j, 0, 0)),
-            (pj_send, (third, rows, LANES), lambda j, s: (j, 0, 0)),
-            (w_heads, (D, wide_block), lambda j, s: (0, 3 * s[core_at] + j)),
-            (w_heads, (D, wide_block), lambda j, s: (0, 3 * (1 - s[core_at]) + j)),
+            whole(grad_first), of_part(pj_keep), of_part(pj_send),
+            (w_heads, (D, D // 2), lambda j, s: (0, 2 * j + s[core_at])),
+            (w_heads, (D, D // 2), lambda j, s: (0, 2 * j + 1 - s[core_at])),
         ],
         [(wide_shape, F32, None, None)],
-        us=5.3,
+        us=COST_INPUT,
     )
 
     if fast:
-        order = expanded.second(after(scal, input_grad))
+        reduce_own, reduce_got = reduced.last(after(scal, input_grad))
+        order = expanded.second(after(scal, reduce_own))
         expanded.send_second()
-        reduce_own, reduce_got = reduced.last(after(scal, order))
-        order = heads.first(after(scal, reduce_own))
+        order = heads.first(after(scal, order))
         heads.send_first()
+        order = heads.second(after(scal, order))
+        heads.send_second()
         expand_own, expand_got = expanded.last(after(scal, order))
-        heads.second(after(scal, expand_own))
-        heads.send_second()
-        heads_own, heads_got = heads.last(scal)
-        w_reduce_grad = halves(first_core, reduce_own, reduce_got)
-        split = 4 * small
-        w_expand_grad = halves(
-            first_core, columns(expand_own[:split], small, 4), columns(expand_got[:split], small, 4)
-        )
-        w_merge_grad = halves(first_core, expand_own[split:], expand_got[split:])
-        split = 3 * small
-        w_heads_grad = halves(
-            first_core, columns(heads_own[:split], small, 3), columns(heads_got[:split], small, 3)
-        )
-        entries = heads_own[split:] + heads_got[split:]
-        entries = entries[0] + entries[1]
-        shares, at = [], 0
-        for n in (2 * small, small, small, small, small, large, small, small, small):
-            shares.append(entries[at : at + n])
-            at += n
+        heads_own, heads_got = heads.last(after(scal, expand_own))
+        out = lambda n, m: ((n, m), F32, None, None)
+        w_reduce_grad, w_expand_grad, w_merge_grad = call(
+            functools.partial(finish_first_kernel, core_at), "finish_first", after(scal, heads_own), (),
+            [*map(whole, (reduce_own, reduce_got, expand_own, expand_got))],
+            [out(large, D), out(small, FF), out(small, D)],
+        )
+        counts = (2 * small, small, small, small, small, large, small, small, small)
+        w_heads_grad, *shares = call(
+            functools.partial(finish_last_kernel, core_at), "finish_last", scal, (),
+            [whole(heads_own), whole(heads_got)], [out(small, 3 * D), *(out(1, n) for n in counts)],
+        )
+        shares = [share.reshape(-1) for share in shares]
         grads = (
             w_heads_grad, *shares[:2], w_merge_grad, *shares[2:5], w_expand_grad, shares[5], w_reduce_grad,
             *shares[6:],
@@ -915,14 +968,18 @@
             [jnp.where(first_core, keep, send), jnp.where(first_core, send, keep)], axis=1
         )
         flat = lambda v: v.transpose(1, 0, 2).reshape(rows, -1)
+        by_heads = lambda keep, send: jnp.concatenate(
+            [by_core(keep[n], send[n]) for n in range(3)], axis=1
+        )
+        sum_heads = by_heads(sum_heads_kept, sum_heads_sent)[0]
         scatter = lambda v: lax.psum_scatter(v, AXES, scatter_dimension=0, tiled=True)
         grads = (
-            scatter(dot_t(tokens, by_core(flat(pj_keep), flat(pj_send)))),
-            scatter(jnp.concatenate([sum_heads[0, 0], sum_heads[1, 0]])), scatter(sum_heads[2, 0]),
+            scatter(dot_t(tokens, by_heads(pj_keep, pj_send))),
+            scatter(sum_heads[: 2 * D]), scatter(sum_heads[2 * D :]),
             scatter(dot_t(mixed, by_core(mg_keep, mg_send))),
             scatter(sums_first[2]), scatter(sums_first[0]), scatter(sums_first[1]),
             scatter(dot_t(normed, by_core(flat(pg_keep), flat(pg_send)))),
-            scatter(sum_expand[0]),
+            scatter(by_core(sum_kept, sum_sent)[0]),
             scatter(dot_t(act, branch)),
             scatter(sums_second[2]), scatter(sums_second[0]), scatter(sums_second[1]),
         )

time: 182 us -> 153 us (0.84)
  local copies, waits for them, and re-layouts: 26.7 us -> 5.92 us
  other arithmetic: 2.9 us -> 0.01 us
  Pallas kernels: 84.4 us -> 82.1 us
  waiting for transfers between devices: 31 us -> 28.9 us
    unnamed x158 -> x50, local copies, waits for them, and re-layouts: 21.6 us -> 4.45 us
    ppermute x2 -> x0, starting transfers between devices: 5.75 us -> none  [the longest x1 4.47 us: per_device(): prior = lax.ppermute(state, AXES, forward)]
    ppermute x32 -> x33, starting transfers between devices: 28.8 us -> 34.3 us  [swap(): lax.ppermute(value, AXES, [(i, i ^ bits) for i in range(self.devices)])]
    transpose x3 -> x0, local copies, waits for them, and re-layouts: 3.17 us -> none  [transposed_pieces(): return value.T.reshape(4, D // 4, value.shape[0])]
    concatenate x4 -> x0, other arithmetic: 2.81 us -> none  [halves(): return jnp.concatenate([left, right], axis=1)]
    pallas_call x20 -> x23, Pallas kernels: 84.4 us -> 82.1 us  [call(): pl.pallas_call(kernel, name=name, grid_spec=pltpu.PrefetchScalarGridSpec(...]
    ppermute x32 -> x33, waiting for transfers between devices: 31 us -> 28.9 us  [swap(): lax.ppermute(value, AXES, [(i, i ^ bits) for i in range(self.devices)])]
  transfers between devices with their start and end apart: 34 -> 33, of which waited for: 9 -> 12; matrix products, arithmetic and copies ran while one was open for 2% -> 0% of each run, Pallas kernels for 39% -> 42%
where the time goes in v3:
time: 153 us; the launch traced here: 152 us
  Pallas kernels  82.1 us (54%)
  starting transfers between devices  34.3 us (22%)
  waiting for transfers between devices  28.9 us (19%)
  local copies, waits for them, and re-layouts  5.92 us (4%)
    pallas_call x23, Pallas kernels, call(): pl.pallas_call(kernel, name=name, grid_spec=pltpu.PrefetchScalarGridSpec(...  82.1 us
    ppermute x33, starting transfers between devices, swap(): lax.ppermute(value, AXES, [(i, i ^ bits) for i in range(self.devices)])  34.3 us
    ppermute x33, waiting for transfers between devices, swap(): lax.ppermute(value, AXES, [(i, i ^ bits) for i in range(self.devices)])  28.9 us
    unnamed x50, local copies, waits for them, and re-layouts  4.45 us
  transfers between devices with their start and end apart: 33, of which 12 were waited for; matrix products, arithmetic and copies ran while one was open for 0% of the time, Pallas kernels for 42%

profile of v3, /device:TPU:0, one launch (start us, length us, event | category | flops | bytes accessed | tf_op | source)
XLA Modules:
  0.0 152.4 jit_solution(14338048415690918332)
XLA Ops:
  0.7 0.7 reshape.81.bk.bv.bq
  1.4 0.7 concatenate.3.scal
  2.1 2.0 %copy-done = bf16[768,2304]{1,0:T(8,128)(2,1)S(1)} copy-done((bf16[768,2304]{1,0:T(8,128)(2,1)S(1)}, bf16[768,2304]{1,0:T(8,128)(2,1)}, u32[]{:S(2)}) %copy-start) | copy-done | bytes 3538968
  4.1 1.1 copy-done.3
  5.3 4.1 %keys_values.1 = (bf16[512,768]{1,0:T(8,128)(2,1)S(1)}, bf16[512,768]{1,0:T(8,128)(2,1)S(1)}, bf16[7,128,128]{2,1,0:T(8,128)(2,1)S(1)}, f32[512,128]{1,0:T(8,128...) custom-call(s32[9]{0:T(128)S(1)} %concatenate.3.scal, bf16[512,768]{1,0:T(8,128)(2,1)S(1)} %copy-done.3, ...), custom_call_target="tpu_custom_call" | custom-call | flops 4600000000 | bytes 1 | tf_op jit(solution)/shard_map/keys_values/pallas_call | solution.py:52
  9.9 2.6 %collective-permute-start.1 = (bf16[7,128,128]{2,1,0:T(8,128)(2,1)S(1)}, bf16[7,128,128]{2,1,0:T(8,128)(2,1)S(1)}, u32[]{:S(2)}, u32[]{:S(2)}) collective-permute-start(bf16[7,128,128]{2,1,0:T(8,128)(2,1)S(1)} %get-tuple-element.135), channel_id=1, source_target_pairs={{0,1},{1,0},{2,3},{3,2},{4,5},{5,4},{6,7},{7,6},{8,9},{9,8},{10,11... | collective-permute-start | bytes 688136 | tf_op jit(solution)/shard_map/ppermute | solution.py:597
  12.5 5.7 %local_attention.1 = (bf16[512,768]{1,0:T(8,128)(2,1)S(1)}, f32[512,768]{1,0:T(8,128)S(1)}, f32[512,768]{1,0:T(8,128)S(1)}) custom-call(s32[9]{0:T(128)S(1)} %concatenate.3.scal, bf16[512,768]{1,0:T(8,128)(2,1)S(1)} %copy-done.4, bf16[768,2304]{1,0:T(8,128)(2,1)S(1)} %copy-done, bf16[1,2304]{1,0:T(2,128)(2,1)S(1)} %reshape.81.bk.bv.bq, ...), custom_call_target="tpu_custom_call" | custom-call | flops 6899999744 | bytes 1 | tf_op jit(solution)/shard_map/local_attention/pallas_call | solution.py:52
  18.7 11.9 %feed_forward.1 = (f32[512,768]{1,0:T(8,128)S(1)}, f32[512,768]{1,0:T(8,128)S(1)}, bf16[512,768]{1,0:T(8,128)(2,1)}, f32[512,768]{1,0:T(8,128)S(1)}, f32[512,128...) custom-call(s32[9]{0:T(128)S(1)} %concatenate.3.scal, ...), custom_call_target="tpu_custom_call" | custom-call | flops 12650000384 | bytes 1 | tf_op jit(solution)/shard_map/feed_forward/pallas_call | solution.py:52
  30.6 1.2 copy-done.8
  32.4 2.6 %second_norm.1 = (bf16[512,768]{1,0:T(8,128)(2,1)}, f32[512,768]{1,0:T(8,128)S(1)}, bf16[512,768]{1,0:T(8,128)(2,1)S(1)}, bf16[512,384]{1,0:T(8,128)(2,1)S(1)}, ...) custom-call(s32[9]{0:T(128)S(1)} %concatenate.3.scal, f32[512,768]{1,0:T(8,128)S(1)} %get-tuple-element.136.second, ...), custom_call_target="tpu_custom_call" | custom-call | flops 2990000128 | bytes 1 | tf_op jit(solution)/shard_map/second_norm/pallas_call | solution.py:52
  35.1 5.4 %feed_forward_back_sent.1 = (bf16[2,512,768]{2,1,0:T(8,128)(2,1)S(1)}, f32[1,1536]{1,0:T(1,128)S(1)}, f32[512,768]{1,0:T(8,128)S(1)}) custom-call(s32[9]{0:T(128)S(1)} %concatenate.3.scal, bf16[512,768]{1,0:T(8,128)(2,1)S(1)} %get-tuple-element.139.full, bf16[512,3072]{1,0:T(8,128)(2,1)S(1)} %get-tuple-element.140.slope, bf16[768,3072]{1,0:T(8,128)(2,1)S(1)} %bitcast.15, ...), custom_call_target="tpu_custom_call" | custom-call | flops 5750000128 | bytes 1 | tf_op jit(solution)/shard_map/feed_forward_back_sent/pallas_call | solution.py:52
  41.0 5.3 %grad_reduce.1 = (bf16[2,4,96,384]{3,2,1,0:T(8,128)(2,1)S(1)}, bf16[2,4,96,384]{3,2,1,0:T(8,128)(2,1)S(1)}, bf16[2,4,96,384]{3,2,1,0:T(8,128)(2,1)S(1)}, bf16[2,4,96,384]{3,2,1,0:T(8,128)(2,1)S(1)}) custom-call(s32[9]{0:T(128)S(1)} %concatenate.3.scal, bf16[512,3072]{1,0:T(8,128)(2,1)S(1)} %get-tuple-element.144.a_own, ...), custom_call_target="tpu_custom_call" | custom-call | flops 6899999744 | bytes 1 | tf_op jit(solution)/shard_map/grad_reduce/pallas_call | solution.py:52
  46.3 1.8 %collective-permute-start.8 = (bf16[2,4,96,384]{3,2,1,0:T(8,128)(2,1)S(1)}, bf16[2,4,96,384]{3,2,1,0:T(8,128)(2,1)S(1)}, u32[]{:S(2)}, u32[]{:S(2)}) collective-permute-start(bf16[2,4,96,384]{3,2,1,0:T(8,128)(2,1)S(1)} %get-tuple-element.147), channel_id=1, source_target_pairs={{0,1},{1,0},{2,3},{3,2},{4,5},{5,4},{6,7},{7,6},{8,9},{9,8},{10,11... | collective-permute-start | bytes 1769480 | tf_op jit(solution)/shard_map/ppermute | solution.py:597
  48.2 1.5 %collective-permute-start.9 = (bf16[2,4,96,384]{3,2,1,0:T(8,128)(2,1)S(1)}, bf16[2,4,96,384]{3,2,1,0:T(8,128)(2,1)S(1)}, u32[]{:S(2)}, u32[]{:S(2)}) collective-permute-start(bf16[2,4,96,384]{3,2,1,0:T(8,128)(2,1)S(1)} %get-tuple-element.162), channel_id=1, source_target_pairs={{0,4},{1,5},{2,6},{3,7},{4,0},{5,1},{6,2},{7,3},{8,12},{9,13},{10,... | collective-permute-start | bytes 1769480 | tf_op jit(solution)/shard_map/ppermute | solution.py:597
  49.7 8.7 %feed_forward_back.1 = (bf16[2,512,768]{2,1,0:T(8,128)(2,1)S(1)}, f32[512,768]{1,0:T(8,128)S(1)}, bf16[512,384]{1,0:T(8,128)(2,1)S(1)}, bf16[512,384]{1,0:T(8,12...) custom-call(s32[9]{0:T(128)S(1)} %concatenate.3.scal, ...), custom_call_target="tpu_custom_call" | custom-call | flops 10350000128 | bytes 1 | tf_op jit(solution)/shard_map/feed_forward_back/pallas_call | solution.py:52
  59.0 1.2 collective-permute-done.6.c_oth
  60.2 4.6 %grad_expand.1 = (bf16[2,4,120,384]{3,2,1,0:T(8,128)(2,1)S(1)}, bf16[2,4,120,384]{3,2,1,0:T(8,128)(2,1)S(1)}, bf16[2,4,120,384]{3,2,1,0:T(8,128)(2,1)S(1)}, bf16[2,4,120,384]{3,2,1,0:T(8,128)(2,1)S(1)}) custom-call(s32[9]{0:T(128)S(1)} %concatenate.3.scal, bf16[2,4,192,512]{3,2,1,0:T(8,128)(2,1)S(1)} %get-tuple-element.138.a_own.m_own, ...), custom_call_target="tpu_custom_call" | custom-call | flops 1150000000 | bytes 1 | tf_op jit(solution)/shard_map/grad_expand/pallas_call | solution.py:52
  64.9 1.8 %collective-permute-done.7.later = bf16[7,128,128]{2,1,0:T(8,128)(2,1)S(1)} collective-permute-done((bf16[7,128,128]{2,1,0:T(8,128)(2,1)S(1)}, bf16[7,128,128]{2,1,0:T(8,128)(2,1)S(1)}, u32[]{:S(2)}, u32[]{:S(2)}) %collective-permute-start.7) | collective-permute-done | bytes 229408 | tf_op jit(solution)/shard_map/ppermute | solution.py:597
  66.7 0.7 grad_reduce_add1.1
  67.4 1.8 %collective-permute-start.11 = (bf16[4,96,384]{2,1,0:T(8,128)(2,1)S(1)}, bf16[4,96,384]{2,1,0:T(8,128)(2,1)S(1)}, u32[]{:S(2)}, u32[]{:S(2)}) collective-permute-start(bf16[4,96,384]{2,1,0:T(8,128)(2,1)S(1)} %get-tuple-element.169), channel_id=1, source_target_pairs={{0,1},{1,0},{2,3},{3,2},{4,5},{5,4},{6,7},{7,6},{8,9},{9,8},{10,11... | collective-permute-start | bytes 884744 | tf_op jit(solution)/shard_map/ppermute | solution.py:597
  69.2 1.5 %collective-permute-start.10 = (bf16[4,96,384]{2,1,0:T(8,128)(2,1)S(1)}, bf16[4,96,384]{2,1,0:T(8,128)(2,1)S(1)}, u32[]{:S(2)}, u32[]{:S(2)}) collective-permute-start(bf16[4,96,384]{2,1,0:T(8,128)(2,1)S(1)} %get-tuple-element.163), channel_id=1, source_target_pairs={{0,4},{1,5},{2,6},{3,7},{4,0},{5,1},{6,2},{7,3},{8,12},{9,13},{10,... | collective-permute-start | bytes 884744 | tf_op jit(solution)/shard_map/ppermute | solution.py:597
  71.5 7.4 %attention_back_sent.1 = (bf16[3,512,384]{2,1,0:T(8,128)(2,1)S(1)}, f32[3,8,384]{2,1,0:T(8,128)S(1)}, f32[512,512]{1,0:T(8,128)S(1)}, f32[512,512]{1,0:T(8,128)S(1)}) custom-call(s32[9]{0:T(128)S(1)} %concatenate.3.scal, bf16[512,768]{1,0:T(8,128)(2,1)S(1)} %get-tuple-element.132.refs_0_.rq, bf16[512,768]{1,0:T(8,128)(2,1)S(1)} %get-tuple-element.128.rk, ...), custom_call_target="tpu_custom_call" | custom-call | flops 575000000 | bytes 1 | tf_op jit(solution)/shard_map/attention_back_sent/pallas_call | solution.py:52
  79.1 0.8 grad_reduce_add2.1
  79.9 7.0 %attention_back_kept.1 = (bf16[3,512,384]{2,1,0:T(8,128)(2,1)S(1)}, f32[3,8,384]{2,1,0:T(8,128)S(1)}) custom-call(s32[9]{0:T(128)S(1)} %concatenate.3.scal, bf16[512,768]{1,0:T(8,128)(2,1)S(1)} %get-tuple-element.132.refs_0_.rq, bf16[512,768]{1,0:T(8,128)(2,1)S(1)} %get-tuple-element.128.rk, bf16[512,768]{1,0:T(8,128)(2,1)S(1)} %get-tuple-element.129.v, ...), custom_call_target="tpu_custom_call" | custom-call | flops 5750000128 | bytes 1 | tf_op jit(solution)/shard_map/attention_back_kept/pallas_call | solution.py:52
  86.9 6.0 %collective-permute-done.13.yr = bf16[2,4,120,384]{3,2,1,0:T(8,128)(2,1)S(1)} collective-permute-done((bf16[2,4,120,384]{3,2,1,0:T(8,128)(2,1)S(1)}, bf16[2,4,120,384]{3,2,1,0:T(8,128)(2,1)S(1)}, u32[]{:S(2)}, u32[]{:S(2)}) %collective-permute-start.13) | collective-permute-done | bytes 737312 | tf_op jit(solution)/shard_map/ppermute | solution.py:597
  92.8 0.7 grad_expand_add1.1
  93.6 1.6 %collective-permute-start.18 = (bf16[4,120,384]{2,1,0:T(8,128)(2,1)S(1)}, bf16[4,120,384]{2,1,0:T(8,128)(2,1)S(1)}, u32[]{:S(2)}, u32[]{:S(2)}) collective-permute-start(bf16[4,120,384]{2,1,0:T(8,128)(2,1)S(1)} %get-tuple-element.196), channel_id=1, source_target_pairs={{0,4},{1,5},{2,6},{3,7},{4,0},{5,1},{6,2},{7,3},{8,12},{9,13},{10,... | collective-permute-start | bytes 1105928 | tf_op jit(solution)/shard_map/ppermute | solution.py:597
  95.7 5.1 %grad_heads.1 = (bf16[2,4,80,384]{3,2,1,0:T(8,128)(2,1)S(1)}, bf16[2,4,80,384]{3,2,1,0:T(8,128)(2,1)S(1)}, bf16[2,4,80,384]{3,2,1,0:T(8,128)(2,1)S(1)}, bf16[2,4,80,384]{3,2,1,0:T(8,128)(2,1)S(1)}) custom-call(s32[9]{0:T(128)S(1)} %concatenate.3.scal, bf16[4,192,512]{2,1,0:T(8,128)(2,1)S(1)} %get-tuple-element.126.a_own, ...), custom_call_target="tpu_custom_call" | custom-call | flops 115000000 | bytes 1 | tf_op jit(solution)/shard_map/grad_heads/pallas_call | solution.py:52
  100.8 1.4 collective-permute-done.18.xm
  102.2 1.7 %collective-permute-done.19.ym = bf16[4,120,384]{2,1,0:T(8,128)(2,1)S(1)} collective-permute-done((bf16[4,120,384]{2,1,0:T(8,128)(2,1)S(1)}, bf16[4,120,384]{2,1,0:T(8,128)(2,1)S(1)}, u32[]{:S(2)}, u32[]{:S(2)}) %collective-permute-start.19) | collective-permute-done | bytes 368672 | tf_op jit(solution)/shard_map/ppermute | solution.py:597
  104.0 1.3 collective-permute-start.21
  105.3 1.8 %collective-permute-start.15 = (bf16[2,96,384]{2,1,0:T(8,128)(2,1)S(1)}, bf16[2,96,384]{2,1,0:T(8,128)(2,1)S(1)}, u32[]{:S(2)}, u32[]{:S(2)}) collective-permute-start(bf16[2,96,384]{2,1,0:T(8,128)(2,1)S(1)} %get-tuple-element.191), channel_id=1, source_target_pairs={{0,8},{1,9},{2,10},{3,11},{4,12},{5,13},{6,14},{7,15},{8,0},{9,1},... | collective-permute-start | bytes 442376 | tf_op jit(solution)/shard_map/ppermute | solution.py:597
  107.1 2.6 %collective-permute-start.16 = (bf16[2,96,384]{2,1,0:T(8,128)(2,1)S(1)}, bf16[2,96,384]{2,1,0:T(8,128)(2,1)S(1)}, u32[]{:S(2)}, u32[]{:S(2)}) collective-permute-start(bf16[2,96,384]{2,1,0:T(8,128)(2,1)S(1)} %get-tuple-element.192), channel_id=1, source_target_pairs={{0,16},{1,17},{2,18},{3,19},{4,20},{5,21},{6,22},{7,23},{8,24},{9,... | collective-permute-start | bytes 442376 | tf_op jit(solution)/shard_map/ppermute | solution.py:597
  109.7 5.3 %input_grad.1 = f32[512,768]{1,0:T(8,128)} custom-call(s32[9]{0:T(128)S(1)} %concatenate.3.scal, f32[512,768]{1,0:T(8,128)S(1)} %get-tuple-element.189.first, bf16[3,512,384]{2,1,0:T(8,128)(2,1)S(1)} %get-tuple-element.174.b_own.keep, bf16[3,512,384]{2,1,0:T(8,128)(2,1)S(1)} %get-tuple-element.167.send, bf16[768,2304]{1,0:T(8,128)(2,1)S(1)} %copy-done.1, ...), custom_call_target="tpu_custom_call" | custom-call | flops 115000000 | bytes 1 | tf_op jit(solution)/shard_map/input_grad/pallas_call | solution.py:52
  115.0 3.2 %collective-permute-done.16.z2 = bf16[2,96,384]{2,1,0:T(8,128)(2,1)S(1)} collective-permute-done((bf16[2,96,384]{2,1,0:T(8,128)(2,1)S(1)}, bf16[2,96,384]{2,1,0:T(8,128)(2,1)S(1)}, u32[]{:S(2)}, u32[]{:S(2)}) %collective-permute-start.16) | collective-permute-done | bytes 147488 | tf_op jit(solution)/shard_map/ppermute | solution.py:597
  118.8 0.8 grad_expand_add2.1
  120.7 1.1 collective-permute-start.22
  121.8 2.1 %collective-permute-start.24 = (bf16[2,120,384]{2,1,0:T(8,128)(2,1)S(1)}, bf16[2,120,384]{2,1,0:T(8,128)(2,1)S(1)}, u32[]{:S(2)}, u32[]{:S(2)}) collective-permute-start(bf16[2,120,384]{2,1,0:T(8,128)(2,1)S(1)} %get-tuple-element.211), channel_id=1, source_target_pairs={{0,8},{1,9},{2,10},{3,11},{4,12},{5,13},{6,14},{7,15},{8,0},{9,1},... | collective-permute-start | bytes 552968 | tf_op jit(solution)/shard_map/ppermute | solution.py:597
  124.0 1.1 collective-permute-start.25
  125.0 1.5 collective-permute-start.26
  126.9 0.7 grad_heads_add2.1
  127.6 2.2 %collective-permute-start.27 = (bf16[2,80,384]{2,1,0:T(8,128)(2,1)S(1)}, bf16[2,80,384]{2,1,0:T(8,128)(2,1)S(1)}, u32[]{:S(2)}, u32[]{:S(2)}) collective-permute-start(bf16[2,80,384]{2,1,0:T(8,128)(2,1)S(1)} %get-tuple-element.216), channel_id=1, source_target_pairs={{0,8},{1,9},{2,10},{3,11},{4,12},{5,13},{6,14},{7,15},{8,0},{9,1},... | collective-permute-start | bytes 368648 | tf_op jit(solution)/shard_map/ppermute | solution.py:597
  129.8 1.1 collective-permute-start.28
  130.9 4.0 %collective-permute-start.29 = (bf16[2,80,384]{2,1,0:T(8,128)(2,1)S(1)}, bf16[2,80,384]{2,1,0:T(8,128)(2,1)S(1)}, u32[]{:S(2)}, u32[]{:S(2)}) collective-permute-start(bf16[2,80,384]{2,1,0:T(8,128)(2,1)S(1)} %get-tuple-element.218), channel_id=1, source_target_pairs={{0,24},{1,25},{2,26},{3,27},{4,28},{5,29},{6,30},{7,31},{8,16},{9,... | collective-permute-start | bytes 368648 | tf_op jit(solution)/shard_map/ppermute | solution.py:597
  134.9 5.8 %collective-permute-done.25.z2 = bf16[2,120,384]{2,1,0:T(8,128)(2,1)S(1)} collective-permute-done((bf16[2,120,384]{2,1,0:T(8,128)(2,1)S(1)}, bf16[2,120,384]{2,1,0:T(8,128)(2,1)S(1)}, u32[]{:S(2)}, u32[]{:S(2)}) %collective-permute-start.25) | collective-permute-done | bytes 184352 | tf_op jit(solution)/shard_map/ppermute | solution.py:597
  142.0 7.1 %collective-permute-done.28.z2 = bf16[2,80,384]{2,1,0:T(8,128)(2,1)S(1)} collective-permute-done((bf16[2,80,384]{2,1,0:T(8,128)(2,1)S(1)}, bf16[2,80,384]{2,1,0:T(8,128)(2,1)S(1)}, u32[]{:S(2)}, u32[]{:S(2)}) %collective-permute-start.28) | collective-permute-done | bytes 122912 | tf_op jit(solution)/shard_map/ppermute | solution.py:597
  149.7 1.4 finish_first.1
  151.2 1.3 finish_last.1
  (102 shorter events, 8.3 us)
Async XLA Ops:
  5.3 7.2 %copy-start.4 = (bf16[512,768]{1,0:T(8,128)(2,1)S(1)}, bf16[512,768]{1,0:T(8,128)(2,1)}, u32[]{:S(2)}) copy-start(bf16[512,768]{1,0:T(8,128)(2,1)} %refs_5_.1) | copy-start | bytes 2359300
  5.3 13.4 %slice-start = ((s8[4718592]{0:T(1024)(128)(4,1)}), s8[4194304]{0:T(1024)(128)(4,1)S(1)}, s32[]{:S(2)}) async-start(s8[4718592]{0:T(1024)(128)(4,1)} %bitcast.14), calls=%async_computation | async-start | bytes 8388608
  5.3 13.4 %slice-start.2 = ((s8[4718592]{0:T(1024)(128)(4,1)}), s8[4194304]{0:T(1024)(128)(4,1)S(1)}, s32[]{:S(2)}) async-start(s8[4718592]{0:T(1024)(128)(4,1)} %bitcast.16), calls=%async_computation.2 | async-start | bytes 8388608
  9.4 9.0 %collective-permute-start = (bf16[4,192,512]{2,1,0:T(8,128)(2,1)S(1)}, bf16[4,192,512]{2,1,0:T(8,128)(2,1)S(1)}, u32[]{:S(2)}, u32[]{:S(2)}) collective-permute-start(bf16[4,192,512]{2,1,0:T(8,128)(2,1)S(1)} %get-tuple-element.126.a_own), channel_id=1, source_target_pairs={{0,2},{1,3},{2,0},{3,1},{4,6},{5,7},{6,4},{7,5},{8,10},{9,11},{10,... | collective-permute-start | bytes 2359304 | tf_op jit(solution)/shard_map/ppermute | solution.py:597
  9.9 8.8 %collective-permute-start.1 = (bf16[7,128,128]{2,1,0:T(8,128)(2,1)S(1)}, bf16[7,128,128]{2,1,0:T(8,128)(2,1)S(1)}, u32[]{:S(2)}, u32[]{:S(2)}) collective-permute-start(bf16[7,128,128]{2,1,0:T(8,128)(2,1)S(1)} %get-tuple-element.135), channel_id=1, source_target_pairs={{0,1},{1,0},{2,3},{3,2},{4,5},{5,4},{6,7},{7,6},{8,9},{9,8},{10,11... | collective-permute-start | bytes 688136 | tf_op jit(solution)/shard_map/ppermute | solution.py:597
  12.5 5.9 %copy-start.14 = (bf16[3072]{0:T(1024)(128)(2,1)S(1)}, bf16[3072]{0:T(1024)(128)(2,1)}, u32[]{:S(2)}) copy-start(bf16[3072]{0:T(1024)(128)(2,1)} %param.23) | copy-start | bytes 18436
  12.5 6.2 %slice-start.1 = ((s8[4718592]{0:T(1024)(128)(4,1)}), s8[524288]{0:T(1024)(128)(4,1)S(1)}, s32[]{:S(2)}) async-start(s8[4718592]{0:T(1024)(128)(4,1)} %bitcast.14), calls=%async_computation.1 | async-start | bytes 1048576
  12.5 6.2 %slice-start.3 = ((s8[4718592]{0:T(1024)(128)(4,1)}), s8[524288]{0:T(1024)(128)(4,1)S(1)}, s32[]{:S(2)}) async-start(s8[4718592]{0:T(1024)(128)(4,1)} %bitcast.16), calls=%async_computation.3 | async-start | bytes 1048576
  12.5 6.2 %copy-start.2 = (bf16[768,768]{1,0:T(8,128)(2,1)S(1)}, bf16[768,768]{1,0:T(8,128)(2,1)}, u32[]{:S(2)}) copy-start(bf16[768,768]{1,0:T(8,128)(2,1)} %w_merge.1) | copy-start | bytes 3538948
  18.7 13.7 %copy-start.19 = (bf16[768]{0:T(1024)(128)(2,1)S(1)}, bf16[768]{0:T(1024)(128)(2,1)}, u32[]{:S(2)}) copy-start(bf16[768]{0:T(1024)(128)(2,1)} %param.26) | copy-start | bytes 4612
  18.7 13.7 %copy-start.20 = (bf16[768]{0:T(1024)(128)(2,1)S(1)}, bf16[768]{0:T(1024)(128)(2,1)}, u32[]{:S(2)}) copy-start(bf16[768]{0:T(1024)(128)(2,1)} %param.27) | copy-start | bytes 4612
  18.7 13.7 %copy-start.5 = (bf16[512,768]{1,0:T(8,128)(2,1)S(1)}, bf16[512,768]{1,0:T(8,128)(2,1)}, u32[]{:S(2)}) copy-start(bf16[512,768]{1,0:T(8,128)(2,1)} %cot.1) | copy-start | bytes 2359300
  31.8 9.2 %collective-permute-start.3 = (bf16[512,3072]{1,0:T(8,128)(2,1)S(1)}, bf16[512,3072]{1,0:T(8,128)(2,1)S(1)}, u32[]{:S(2)}, u32[]{:S(2)}) collective-permute-start(bf16[512,3072]{1,0:T(8,128)(2,1)S(1)} %get-tuple-element.144.a_own), channel_id=1, source_target_pairs={{0,2},{1,3},{2,0},{3,1},{4,6},{5,7},{6,4},{7,5},{8,10},{9,11},{10,... | collective-permute-start | bytes 9437192 | tf_op jit(solution)/shard_map/ppermute | solution.py:597
  31.9 9.1 %collective-permute-start.2 = (bf16[2,4,192,512]{3,2,1,0:T(8,128)(2,1)S(1)}, bf16[2,4,192,512]{3,2,1,0:T(8,128)(2,1)S(1)}, u32[]{:S(2)}, u32[]{:S(2)}) collective-permute-start(bf16[2,4,192,512]{3,2,1,0:T(8,128)(2,1)S(1)} %get-tuple-element.138.a_own.m_own), channel_id=1, source_target_pairs={{0,2},{1,3},{2,0},{3,1},{4,6},{5,7},{6,4},{7,5},{8,10},{9,11},{10,... | collective-permute-start | bytes 4718600 | tf_op jit(solution)/shard_map/ppermute | solution.py:597
  35.0 6.0 %collective-permute-start.4 = (bf16[512,384]{1,0:T(8,128)(2,1)S(1)}, bf16[512,384]{1,0:T(8,128)(2,1)S(1)}, u32[]{:S(2)}, u32[]{:S(2)}) collective-permute-start(bf16[512,384]{1,0:T(8,128)(2,1)S(1)} %get-tuple-element.146), channel_id=1, source_target_pairs={{0,2},{1,3},{2,0},{3,1},{4,6},{5,7},{6,4},{7,5},{8,10},{9,11},{10,... | collective-permute-start | bytes 1179656 | tf_op jit(solution)/shard_map/ppermute | solution.py:597
  40.5 18.5 %collective-permute-start.5 = (bf16[2,512,768]{2,1,0:T(8,128)(2,1)S(1)}, bf16[2,512,768]{2,1,0:T(8,128)(2,1)S(1)}, u32[]{:S(2)}, u32[]{:S(2)}) collective-permute-start(bf16[2,512,768]{2,1,0:T(8,128)(2,1)S(1)} %get-tuple-element.154), channel_id=1, source_target_pairs={{0,2},{1,3},{2,0},{3,1},{4,6},{5,7},{6,4},{7,5},{8,10},{9,11},{10,... | collective-permute-start | bytes 4718600 | tf_op jit(solution)/shard_map/ppermute | solution.py:597
  41.0 8.7 %copy-start.7 = (bf16[512,3072]{1,0:T(8,128)(2,1)S(1)}, bf16[512,3072]{1,0:T(8,128)(2,1)}, u32[]{:S(2)}) copy-start(bf16[512,3072]{1,0:T(8,128)(2,1)} %copy-done.6) | copy-start | bytes 9437188
  41.0 8.7 %copy-start.9 = (f32[512,768]{1,0:T(8,128)S(1)}, f32[512,768]{1,0:T(8,128)}, u32[]{:S(2)}) copy-start(f32[512,768]{1,0:T(8,128)} %copy-done.8) | copy-start | bytes 4718596
  41.0 8.7 %copy-start.11 = (f32[512,768]{1,0:T(8,128)S(1)}, f32[512,768]{1,0:T(8,128)}, u32[]{:S(2)}) copy-start(f32[512,768]{1,0:T(8,128)} %copy-done.10) | copy-start | bytes 4718596
  41.0 8.7 %copy-start.13 = (f32[512,768]{1,0:T(8,128)S(1)}, f32[512,768]{1,0:T(8,128)}, u32[]{:S(2)}) copy-start(f32[512,768]{1,0:T(8,128)} %copy-done.12) | copy-start | bytes 4718596
  46.3 20.3 %collective-permute-start.8 = (bf16[2,4,96,384]{3,2,1,0:T(8,128)(2,1)S(1)}, bf16[2,4,96,384]{3,2,1,0:T(8,128)(2,1)S(1)}, u32[]{:S(2)}, u32[]{:S(2)}) collective-permute-start(bf16[2,4,96,384]{3,2,1,0:T(8,128)(2,1)S(1)} %get-tuple-element.147), channel_id=1, source_target_pairs={{0,1},{1,0},{2,3},{3,2},{4,5},{5,4},{6,7},{7,6},{8,9},{9,8},{10,11... | collective-permute-start | bytes 1769480 | tf_op jit(solution)/shard_map/ppermute | solution.py:597
  48.2 18.5 %collective-permute-start.9 = (bf16[2,4,96,384]{3,2,1,0:T(8,128)(2,1)S(1)}, bf16[2,4,96,384]{3,2,1,0:T(8,128)(2,1)S(1)}, u32[]{:S(2)}, u32[]{:S(2)}) collective-permute-start(bf16[2,4,96,384]{3,2,1,0:T(8,128)(2,1)S(1)} %get-tuple-element.162), channel_id=1, source_target_pairs={{0,4},{1,5},{2,6},{3,7},{4,0},{5,1},{6,2},{7,3},{8,12},{9,13},{10,... | collective-permute-start | bytes 1769480 | tf_op jit(solution)/shard_map/ppermute | solution.py:597
  58.4 1.8 %collective-permute-start.6 = (bf16[512,384]{1,0:T(8,128)(2,1)S(1)}, bf16[512,384]{1,0:T(8,128)(2,1)S(1)}, u32[]{:S(2)}, u32[]{:S(2)}) collective-permute-start(bf16[512,384]{1,0:T(8,128)(2,1)S(1)} %get-tuple-element.156), channel_id=1, source_target_pairs={{0,2},{1,3},{2,0},{3,1},{4,6},{5,7},{6,4},{7,5},{8,10},{9,11},{10,... | collective-permute-start | bytes 1179656 | tf_op jit(solution)/shard_map/ppermute | solution.py:597
  58.5 8.2 %collective-permute-start.7 = (bf16[7,128,128]{2,1,0:T(8,128)(2,1)S(1)}, bf16[7,128,128]{2,1,0:T(8,128)(2,1)S(1)}, u32[]{:S(2)}, u32[]{:S(2)}) collective-permute-start(bf16[7,128,128]{2,1,0:T(8,128)(2,1)S(1)} %get-tuple-element.158), channel_id=1, source_target_pairs={{0,1},{1,0},{2,3},{3,2},{4,5},{5,4},{6,7},{7,6},{8,9},{9,8},{10,11... | collective-permute-start | bytes 688136 | tf_op jit(solution)/shard_map/ppermute | solution.py:597
  67.4 11.6 %collective-permute-start.11 = (bf16[4,96,384]{2,1,0:T(8,128)(2,1)S(1)}, bf16[4,96,384]{2,1,0:T(8,128)(2,1)S(1)}, u32[]{:S(2)}, u32[]{:S(2)}) collective-permute-start(bf16[4,96,384]{2,1,0:T(8,128)(2,1)S(1)} %get-tuple-element.169), channel_id=1, source_target_pairs={{0,1},{1,0},{2,3},{3,2},{4,5},{5,4},{6,7},{7,6},{8,9},{9,8},{10,11... | collective-permute-start | bytes 884744 | tf_op jit(solution)/shard_map/ppermute | solution.py:597
  69.2 9.9 %collective-permute-start.10 = (bf16[4,96,384]{2,1,0:T(8,128)(2,1)S(1)}, bf16[4,96,384]{2,1,0:T(8,128)(2,1)S(1)}, u32[]{:S(2)}, u32[]{:S(2)}) collective-permute-start(bf16[4,96,384]{2,1,0:T(8,128)(2,1)S(1)} %get-tuple-element.163), channel_id=1, source_target_pairs={{0,4},{1,5},{2,6},{3,7},{4,0},{5,1},{6,2},{7,3},{8,12},{9,13},{10,... | collective-permute-start | bytes 884744 | tf_op jit(solution)/shard_map/ppermute | solution.py:597
  70.7 22.2 %collective-permute-start.13 = (bf16[2,4,120,384]{3,2,1,0:T(8,128)(2,1)S(1)}, bf16[2,4,120,384]{3,2,1,0:T(8,128)(2,1)S(1)}, u32[]{:S(2)}, u32[]{:S(2)}) collective-permute-start(bf16[2,4,120,384]{3,2,1,0:T(8,128)(2,1)S(1)} %get-tuple-element.178), channel_id=1, source_target_pairs={{0,4},{1,5},{2,6},{3,7},{4,0},{5,1},{6,2},{7,3},{8,12},{9,13},{10,... | collective-permute-start | bytes 2211848 | tf_op jit(solution)/shard_map/ppermute | solution.py:597
  71.2 21.7 %collective-permute-start.12 = (bf16[2,4,120,384]{3,2,1,0:T(8,128)(2,1)S(1)}, bf16[2,4,120,384]{3,2,1,0:T(8,128)(2,1)S(1)}, u32[]{:S(2)}, u32[]{:S(2)}) collective-permute-start(bf16[2,4,120,384]{3,2,1,0:T(8,128)(2,1)S(1)} %get-tuple-element.157), channel_id=1, source_target_pairs={{0,1},{1,0},{2,3},{3,2},{4,5},{5,4},{6,7},{7,6},{8,9},{9,8},{10,11... | collective-permute-start | bytes 2211848 | tf_op jit(solution)/shard_map/ppermute | solution.py:597
  78.9 14.7 %collective-permute-start.14 = (bf16[3,512,384]{2,1,0:T(8,128)(2,1)S(1)}, bf16[3,512,384]{2,1,0:T(8,128)(2,1)S(1)}, u32[]{:S(2)}, u32[]{:S(2)}) collective-permute-start(bf16[3,512,384]{2,1,0:T(8,128)(2,1)S(1)} %get-tuple-element.167.send), channel_id=1, source_target_pairs={{0,2},{1,3},{2,0},{3,1},{4,6},{5,7},{6,4},{7,5},{8,10},{9,11},{10,... | collective-permute-start | bytes 3538952 | tf_op jit(solution)/shard_map/ppermute | solution.py:597
  93.6 8.6 %collective-permute-start.18 = (bf16[4,120,384]{2,1,0:T(8,128)(2,1)S(1)}, bf16[4,120,384]{2,1,0:T(8,128)(2,1)S(1)}, u32[]{:S(2)}, u32[]{:S(2)}) collective-permute-start(bf16[4,120,384]{2,1,0:T(8,128)(2,1)S(1)} %get-tuple-element.196), channel_id=1, source_target_pairs={{0,4},{1,5},{2,6},{3,7},{4,0},{5,1},{6,2},{7,3},{8,12},{9,13},{10,... | collective-permute-start | bytes 1105928 | tf_op jit(solution)/shard_map/ppermute | solution.py:597
  95.2 8.8 %collective-permute-start.19 = (bf16[4,120,384]{2,1,0:T(8,128)(2,1)S(1)}, bf16[4,120,384]{2,1,0:T(8,128)(2,1)S(1)}, u32[]{:S(2)}, u32[]{:S(2)}) collective-permute-start(bf16[4,120,384]{2,1,0:T(8,128)(2,1)S(1)} %get-tuple-element.198), channel_id=1, source_target_pairs={{0,1},{1,0},{2,3},{3,2},{4,5},{5,4},{6,7},{7,6},{8,9},{9,8},{10,11... | collective-permute-start | bytes 1105928 | tf_op jit(solution)/shard_map/ppermute | solution.py:597
  95.7 14.0 %copy-start.1 = (bf16[768,2304]{1,0:T(8,128)(2,1)S(1)}, bf16[768,2304]{1,0:T(8,128)(2,1)}, u32[]{:S(2)}) copy-start(bf16[768,2304]{1,0:T(8,128)(2,1)} %w_send.1) | copy-start | bytes 10616836
  103.9 15.7 %collective-permute-start.20 = (bf16[2,4,80,384]{3,2,1,0:T(8,128)(2,1)S(1)}, bf16[2,4,80,384]{3,2,1,0:T(8,128)(2,1)S(1)}, u32[]{:S(2)}, u32[]{:S(2)}) collective-permute-start(bf16[2,4,80,384]{3,2,1,0:T(8,128)(2,1)S(1)} %get-tuple-element.202), channel_id=1, source_target_pairs={{0,1},{1,0},{2,3},{3,2},{4,5},{5,4},{6,7},{7,6},{8,9},{9,8},{10,11... | collective-permute-start | bytes 1474568 | tf_op jit(solution)/shard_map/ppermute | solution.py:597
  104.0 15.6 %collective-permute-start.21 = (bf16[2,4,80,384]{3,2,1,0:T(8,128)(2,1)S(1)}, bf16[2,4,80,384]{3,2,1,0:T(8,128)(2,1)S(1)}, u32[]{:S(2)}, u32[]{:S(2)}) collective-permute-start(bf16[2,4,80,384]{3,2,1,0:T(8,128)(2,1)S(1)} %get-tuple-element.205), channel_id=1, source_target_pairs={{0,4},{1,5},{2,6},{3,7},{4,0},{5,1},{6,2},{7,3},{8,12},{9,13},{10,... | collective-permute-start | bytes 1474568 | tf_op jit(solution)/shard_map/ppermute | solution.py:597
  105.3 9.7 %collective-permute-start.15 = (bf16[2,96,384]{2,1,0:T(8,128)(2,1)S(1)}, bf16[2,96,384]{2,1,0:T(8,128)(2,1)S(1)}, u32[]{:S(2)}, u32[]{:S(2)}) collective-permute-start(bf16[2,96,384]{2,1,0:T(8,128)(2,1)S(1)} %get-tuple-element.191), channel_id=1, source_target_pairs={{0,8},{1,9},{2,10},{3,11},{4,12},{5,13},{6,14},{7,15},{8,0},{9,1},... | collective-permute-start | bytes 442376 | tf_op jit(solution)/shard_map/ppermute | solution.py:597
  107.1 11.1 %collective-permute-start.16 = (bf16[2,96,384]{2,1,0:T(8,128)(2,1)S(1)}, bf16[2,96,384]{2,1,0:T(8,128)(2,1)S(1)}, u32[]{:S(2)}, u32[]{:S(2)}) collective-permute-start(bf16[2,96,384]{2,1,0:T(8,128)(2,1)S(1)} %get-tuple-element.192), channel_id=1, source_target_pairs={{0,16},{1,17},{2,18},{3,19},{4,20},{5,21},{6,22},{7,23},{8,24},{9,... | collective-permute-start | bytes 442376 | tf_op jit(solution)/shard_map/ppermute | solution.py:597
  109.7 8.5 %collective-permute-start.17 = (bf16[2,96,384]{2,1,0:T(8,128)(2,1)S(1)}, bf16[2,96,384]{2,1,0:T(8,128)(2,1)S(1)}, u32[]{:S(2)}, u32[]{:S(2)}) collective-permute-start(bf16[2,96,384]{2,1,0:T(8,128)(2,1)S(1)} %get-tuple-element.193), channel_id=1, source_target_pairs={{0,24},{1,25},{2,26},{3,27},{4,28},{5,29},{6,30},{7,31},{8,16},{9,... | collective-permute-start | bytes 442376 | tf_op jit(solution)/shard_map/ppermute | solution.py:597
  120.3 6.3 %collective-permute-start.23 = (bf16[4,80,384]{2,1,0:T(8,128)(2,1)S(1)}, bf16[4,80,384]{2,1,0:T(8,128)(2,1)S(1)}, u32[]{:S(2)}, u32[]{:S(2)}) collective-permute-start(bf16[4,80,384]{2,1,0:T(8,128)(2,1)S(1)} %get-tuple-element.208), channel_id=1, source_target_pairs={{0,1},{1,0},{2,3},{3,2},{4,5},{5,4},{6,7},{7,6},{8,9},{9,8},{10,11... | collective-permute-start | bytes 737288 | tf_op jit(solution)/shard_map/ppermute | solution.py:597
  120.7 6.2 %collective-permute-start.22 = (bf16[4,80,384]{2,1,0:T(8,128)(2,1)S(1)}, bf16[4,80,384]{2,1,0:T(8,128)(2,1)S(1)}, u32[]{:S(2)}, u32[]{:S(2)}) collective-permute-start(bf16[4,80,384]{2,1,0:T(8,128)(2,1)S(1)} %get-tuple-element.206), channel_id=1, source_target_pairs={{0,4},{1,5},{2,6},{3,7},{4,0},{5,1},{6,2},{7,3},{8,12},{9,13},{10,... | collective-permute-start | bytes 737288 | tf_op jit(solution)/shard_map/ppermute | solution.py:597
  121.8 9.1 %collective-permute-start.24 = (bf16[2,120,384]{2,1,0:T(8,128)(2,1)S(1)}, bf16[2,120,384]{2,1,0:T(8,128)(2,1)S(1)}, u32[]{:S(2)}, u32[]{:S(2)}) collective-permute-start(bf16[2,120,384]{2,1,0:T(8,128)(2,1)S(1)} %get-tuple-element.211), channel_id=1, source_target_pairs={{0,8},{1,9},{2,10},{3,11},{4,12},{5,13},{6,14},{7,15},{8,0},{9,1},... | collective-permute-start | bytes 552968 | tf_op jit(solution)/shard_map/ppermute | solution.py:597
  124.0 16.8 %collective-permute-start.25 = (bf16[2,120,384]{2,1,0:T(8,128)(2,1)S(1)}, bf16[2,120,384]{2,1,0:T(8,128)(2,1)S(1)}, u32[]{:S(2)}, u32[]{:S(2)}) collective-permute-start(bf16[2,120,384]{2,1,0:T(8,128)(2,1)S(1)} %get-tuple-element.212), channel_id=1, source_target_pairs={{0,16},{1,17},{2,18},{3,19},{4,20},{5,21},{6,22},{7,23},{8,24},{9,... | collective-permute-start | bytes 552968 | tf_op jit(solution)/shard_map/ppermute | solution.py:597
  125.0 15.7 %collective-permute-start.26 = (bf16[2,120,384]{2,1,0:T(8,128)(2,1)S(1)}, bf16[2,120,384]{2,1,0:T(8,128)(2,1)S(1)}, u32[]{:S(2)}, u32[]{:S(2)}) collective-permute-start(bf16[2,120,384]{2,1,0:T(8,128)(2,1)S(1)} %get-tuple-element.213), channel_id=1, source_target_pairs={{0,24},{1,25},{2,26},{3,27},{4,28},{5,29},{6,30},{7,31},{8,16},{9,... | collective-permute-start | bytes 552968 | tf_op jit(solution)/shard_map/ppermute | solution.py:597
  127.6 14.4 %collective-permute-start.27 = (bf16[2,80,384]{2,1,0:T(8,128)(2,1)S(1)}, bf16[2,80,384]{2,1,0:T(8,128)(2,1)S(1)}, u32[]{:S(2)}, u32[]{:S(2)}) collective-permute-start(bf16[2,80,384]{2,1,0:T(8,128)(2,1)S(1)} %get-tuple-element.216), channel_id=1, source_target_pairs={{0,8},{1,9},{2,10},{3,11},{4,12},{5,13},{6,14},{7,15},{8,0},{9,1},... | collective-permute-start | bytes 368648 | tf_op jit(solution)/shard_map/ppermute | solution.py:597
  129.8 19.2 %collective-permute-start.28 = (bf16[2,80,384]{2,1,0:T(8,128)(2,1)S(1)}, bf16[2,80,384]{2,1,0:T(8,128)(2,1)S(1)}, u32[]{:S(2)}, u32[]{:S(2)}) collective-permute-start(bf16[2,80,384]{2,1,0:T(8,128)(2,1)S(1)} %get-tuple-element.217), channel_id=1, source_target_pairs={{0,16},{1,17},{2,18},{3,19},{4,20},{5,21},{6,22},{7,23},{8,24},{9,... | collective-permute-start | bytes 368648 | tf_op jit(solution)/shard_map/ppermute | solution.py:597
  130.9 18.1 %collective-permute-start.29 = (bf16[2,80,384]{2,1,0:T(8,128)(2,1)S(1)}, bf16[2,80,384]{2,1,0:T(8,128)(2,1)S(1)}, u32[]{:S(2)}, u32[]{:S(2)}) collective-permute-start(bf16[2,80,384]{2,1,0:T(8,128)(2,1)S(1)} %get-tuple-element.218), channel_id=1, source_target_pairs={{0,24},{1,25},{2,26},{3,27},{4,28},{5,29},{6,30},{7,31},{8,16},{9,... | collective-permute-start | bytes 368648 | tf_op jit(solution)/shard_map/ppermute | solution.py:597
  141.4 8.4 %collective-permute-start.32 = (f32[120,384]{1,0:T(8,128)S(1)}, f32[120,384]{1,0:T(8,128)S(1)}, u32[]{:S(2)}, u32[]{:S(2)}) collective-permute-start(f32[120,384]{1,0:T(8,128)S(1)} %get-tuple-element.226), channel_id=1, source_target_pairs={{0,2},{1,3},{2,0},{3,1},{4,6},{5,7},{6,4},{7,5},{8,10},{9,11},{10,... | collective-permute-start | bytes 552968 | tf_op jit(solution)/shard_map/ppermute | solution.py:597
  141.5 8.3 %collective-permute-start.31 = (f32[96,384]{1,0:T(8,128)S(1)}, f32[96,384]{1,0:T(8,128)S(1)}, u32[]{:S(2)}, u32[]{:S(2)}) collective-permute-start(f32[96,384]{1,0:T(8,128)S(1)} %get-tuple-element.225), channel_id=1, source_target_pairs={{0,2},{1,3},{2,0},{3,1},{4,6},{5,7},{6,4},{7,5},{8,10},{9,11},{10,... | collective-permute-start | bytes 442376 | tf_op jit(solution)/shard_map/ppermute | solution.py:597
  149.6 1.5 %collective-permute-start.30 = (f32[80,384]{1,0:T(8,128)S(1)}, f32[80,384]{1,0:T(8,128)S(1)}, u32[]{:S(2)}, u32[]{:S(2)}) collective-permute-start(f32[80,384]{1,0:T(8,128)S(1)} %get-tuple-element.220), channel_id=1, source_target_pairs={{0,2},{1,3},{2,0},{3,1},{4,6},{5,7},{6,4},{7,5},{8,10},{9,11},{10,... | collective-permute-start | bytes 368648 | tf_op jit(solution)/shard_map/ppermute | solution.py:597
  (10 other events, 37.1 us)

commit v4 on v3

--- a/solution.py
+++ b/solution.py
@@ -17,12 +17,15 @@
 F32 = jnp.float32
 AXES = ("dp", "head")
 VMEM_LIMIT = 8 << 20
-VMEM_FFN = 11 << 20
+VMEM_FFN = 16 << 20
 FF_BLOCK = 768
+FFN_BLOCK = 1024
+FFN_STEPS = FF // FFN_BLOCK
 MATMUL_PER_US = 1.15e9
 COST_EXPAND = 1
 VMEM_BACK = 16 << 20
-COST_KEPT = 5
+COST_KEPT = 0.5
+COST_BACK = 3
 COST_SENT = 0.5
 COST_HEADS = 0.1
 COST_INPUT = 0.1
@@ -41,7 +44,7 @@
     return lax.dot_general(a, b, (((1,), (1,)), ((), ())), preferred_element_type=F32)
 
 
-def call(kernel, name, scal, grid, ins, outs, scratch=(), us=1, vmem=VMEM_LIMIT):
+def call(kernel, name, scal, grid, ins, outs, scratch=(), us=0.1, vmem=VMEM_LIMIT):
     def spec(b, m):
         if b is None:
             return pl.BlockSpec(memory_space=pltpu.VMEM if m is None else m)
@@ -261,14 +264,17 @@
     turn(normed_o[...], turned_o.at[1])
 
 
-def expand_reduce(normed, w_exp, b_exp, w_red, act_o, slope_o):
-    pre = dot(normed[...], w_exp[...]) + b_exp[...].astype(F32)
-    cdf = 0.5 + 0.5 * lax.erf(pre * (2.0**-0.5))
-    pdf = jnp.exp(-0.5 * pre * pre) * (1.0 / math.sqrt(2.0 * math.pi))
-    act = (pre * cdf).astype(BF)
-    act_o[...] = act
-    slope_o[...] = (cdf + pre * pdf).astype(BF)
-    return dot(act, w_red[...])
+def expand_reduce(normed, w_exp, b_exp, w_red, act_o, slope_o, acc_o):
+    rows = normed.shape[0]
+    pre = [dot(normed[at : at + rows // 2], w_exp[...]) + b_exp[...].astype(F32) for at in (0, rows // 2)]
+    for at, x in zip((0, rows // 2), pre):
+        part = slice(at, at + rows // 2)
+        cdf = 0.5 + 0.5 * lax.erf(x * (2.0**-0.5))
+        pdf = jnp.exp(-0.5 * x * x) * (1.0 / math.sqrt(2.0 * math.pi))
+        act = (x * cdf).astype(BF)
+        act_o[part] = act
+        slope_o[part] = (cdf + x * pdf).astype(BF)
+        acc_o[part] += dot(act, w_red[...])
 
 
 def ffn_kernel(head_at, scal, *refs):
@@ -280,7 +286,7 @@
     def _():
         merge_heads(head_at, scal, *refs[:11], *refs[14:22])
 
-    acc_o[...] += expand_reduce(normed_o, w_exp, b_exp, w_red, act_o, slope_o)
+    expand_reduce(normed_o, w_exp, b_exp, w_red, act_o, slope_o, acc_o)
 
 
 def second_kernel(core_at, scal, second, cot, gain, bias, out_o, grad_o, full_o, keep_o, send_o, sums_o):
@@ -399,22 +405,22 @@
     st_o[PAIRS] = norms.astype(BF)
 
 
-def attn_sent_kernel(head_at, core_at, scal, rq, rk, v, w, e, prior, later, tcol, trow, out_o, sums_o, weights, weights_t):
+def attn_sent_kernel(head_at, core_at, scal, rq, rk, v, w, e, prior, later, tcol, trow, early_o, late_o, sums_o, weights, weights_t):
     @pl.when(pl.program_id(0) == 0)
     def _():
         weights[...] = weights_block(tcol, trow, False)
         weights_t[...] = weights_block(tcol, trow, True)
 
     first = (1 - scal[core_at]) * pl.num_programs(0)
-    attn_back(head_at, first, scal, rq, rk, v, w, e, prior, later, tcol, weights, weights_t, out_o, sums_o)
-
-
-def attn_kept_kernel(head_at, core_at, scal, rq, rk, v, w, e, prior, later, tcol, weights, weights_t, out_o, sums_o):
+    attn_back(head_at, first, scal, rq, rk, v, w, e, prior, later, tcol, weights, weights_t, early_o, late_o, sums_o)
+
+
+def attn_kept_kernel(head_at, core_at, scal, rq, rk, v, w, e, prior, later, tcol, weights, weights_t, early_o, late_o, sums_o):
     first = scal[core_at] * pl.num_programs(0)
-    attn_back(head_at, first, scal, rq, rk, v, w, e, prior, later, tcol, weights, weights_t, out_o, sums_o)
-
-
-def attn_back(head_at, first, scal, rq, rk, v, w, e, prior, later, tcol, weights, weights_t, out_o, sums_o):
+    attn_back(head_at, first, scal, rq, rk, v, w, e, prior, later, tcol, weights, weights_t, early_o, late_o, sums_o)
+
+
+def attn_back(head_at, first, scal, rq, rk, v, w, e, prior, later, tcol, weights, weights_t, early_o, late_o, sums_o):
     pair = first + pl.program_id(0)
     rows = rq.shape[0]
     mid = rows // 2
@@ -473,15 +479,17 @@
     dv = dv.astype(BF)
     for n, part in enumerate((dq, dk, dv)):
         sums_o[n] = jnp.broadcast_to(jnp.sum(part.astype(F32), axis=0, keepdims=True), sums_o.shape[1:])
-        out_o[n] = part
-
-
-def input_kernel(scal, first, keep, send, w_keep, w_send, out_o):
+        early_o[n] = part[:mid]
+        late_o[n] = part[mid:]
+
+
+def input_kernel(scal, first, keep_early, keep_late, send_early, send_late, w_keep, w_send, out_o):
     @pl.when(pl.program_id(0) == 0)
     def _():
         out_o[...] = first[...]
 
-    out_o[...] += dot_r(keep[0], w_keep[...]) + dot_r(send[0], w_send[...])
+    rows = lambda early, late: jnp.concatenate([early[0], late[0]], axis=0)
+    out_o[...] += dot_r(rows(keep_early, keep_late), w_keep[...]) + dot_r(rows(send_early, send_late), w_send[...])
 
 
 def place(values, piece_rows, tz, tys, x, y, z, extra, outs):
@@ -517,13 +525,25 @@
         ys[slot, slot_z] = jnp.where(y == 0, b, a).astype(BF)
 
 
-def reduce_grad_kernel(pos_at, scal, a_own, a_oth, b_own, b_oth, *outs):
+def reduce_grad_kernel(pos_at, scal, a_own, a_oth, b_own, b_oth, kept, near):
     tz = pl.program_id(0)
     x, y, z = (scal[pos_at + n] for n in range(3))
     values = dot_t(a_own[...], b_own[...]) + dot_t(a_oth[...], b_oth[...])
-    piece_rows = values.shape[0] // 8
-    pieces = place(values, piece_rows, tz, (0, 1), x, y, z, None, outs)
-    place_y(pieces, tz, (0, 1), x, y, z, outs)
+    rows = values.shape[0] // 8
+    slot = tz ^ z
+
+    def put(out):
+        for n in range(8):
+            ty, tc, tx = n // 4, n // 2 % 2, n % 2
+            out[slot // 2, tc, tx ^ x, ty ^ y] = values[n * rows : (n + 1) * rows].astype(BF)
+
+    @pl.when(slot % 2 == 0)
+    def _():
+        put(kept)
+
+    @pl.when(slot % 2 == 1)
+    def _():
+        put(near)
 
 
 def expand_grad_kernel(pos_at, scal, a_own, a_oth, b_own, b_oth, m_own, m_oth, c_own, c_oth, *outs):
@@ -553,7 +573,7 @@
 
 
 def heads_grad_kernel(
-    pos_at, scal, a_own, a_oth, b_own, b_oth, kept_h, sent_h, sums_1, kept_e, sent_e, sums_2, *refs, devices
+    pos_at, scal, a_own, a_oth, own_early, own_late, oth_early, oth_late, kept_h, sent_h, sums_1, kept_e, sent_e, sums_2, *refs, devices
 ):
     outs, table = refs[:-1], refs[-1]
     tz = pl.program_id(0)
@@ -576,8 +596,10 @@
             at += entries.shape[1] // devices
         table[...] = total
 
-    join = lambda ref: jnp.concatenate([ref[n] for n in range(ref.shape[0])], axis=1)
-    values = dot(a_own[0], join(b_own)) + dot(a_oth[0], join(b_oth))
+    join = lambda early, late: jnp.concatenate(
+        [jnp.concatenate([early[n], late[n]], axis=0) for n in range(early.shape[0])], axis=1
+    )
+    values = dot(a_own[0], join(own_early, own_late)) + dot(a_oth[0], join(oth_early, oth_late))
     line = lax.broadcasted_iota(jnp.int32, (8, width), 0)
     rows8 = table[pl.ds(pl.multiple_of(tz * 8, 8), 8)]
     extra = []
@@ -631,6 +653,54 @@
     send[...] = jnp.where(first, of_second, of_first)
 
 
+def add_second_half_kernel(scal, xk, xr, xm, yk, yr, ym, kept, sent):
+    for n, (keep, got, more) in enumerate(((xk, xr, xm), (yk, yr, ym))):
+        total = lambda k: keep[0, k].astype(F32) + got[0, k].astype(F32) + more[k].astype(F32)
+        for k in range(2):
+            kept[k, n] = total(2 * k)
+            sent[k, n] = total(2 * k + 1).astype(BF)
+
+
+def add_third_half_kernel(scal, kept, got, own, sent):
+    own[...] = kept[0] + got[0].astype(F32)
+    sent[...] = (kept[1] + got[1].astype(F32)).astype(BF)
+
+
+def add_last_half_kernel(core_at, scal, own, got, keep, send):
+    first = scal[core_at] == 0
+    of_first, of_second = (own[n] + got[n].astype(F32) for n in range(2))
+    keep[...] = jnp.where(first, of_first, of_second)
+    send[...] = jnp.where(first, of_second, of_first)
+
+
+def add_near_kernel(scal, kept, got, own, far):
+    own[...] = kept[0].astype(F32) + got[0].astype(F32)
+    far[...] = (kept[1].astype(F32) + got[1].astype(F32)).astype(BF)
+
+
+def add_far_kernel(scal, own, got, xk, xs, yk, ys):
+    total = lambda *at: own[at] + got[at].astype(F32)
+    for n in range(2):
+        xk[n] = total(0, 0, n)
+        xs[n] = total(0, 1, n).astype(BF)
+        yk[n] = total(1, n, 0)
+        ys[n] = total(1, n, 1).astype(BF)
+
+
+def add_side_kernel(scal, xk, xr, yk, yr, own, xn, yn):
+    own[0] = xk[0] + xr[0].astype(F32)
+    own[1] = yk[0] + yr[0].astype(F32)
+    xn[...] = (xk[1] + xr[1].astype(F32)).astype(BF)
+    yn[...] = (yk[1] + yr[1].astype(F32)).astype(BF)
+
+
+def add_end_kernel(core_at, scal, own, xm, ym, keep, send):
+    first = scal[core_at] == 0
+    of_first, of_second = own[0] + xm[...].astype(F32), own[1] + ym[...].astype(F32)
+    keep[...] = jnp.where(first, of_first, of_second)
+    send[...] = jnp.where(first, of_second, of_first)
+
+
 class Scatter:
     def __init__(self, ring, core_at, name, sent):
         self.ring, self.core_at, self.name = ring, core_at, name
@@ -639,7 +709,7 @@
     def send(self, *others):
         self.xr, self.yr = self.ring.x(after(self.xs, *others)), self.ring.y(after(self.ys, *others))
 
-    def first(self, scal, us=1):
+    def first(self, scal, us=0.1):
         shape = self.xk.shape[1:]
         part = lambda a: (a, (1,) + shape, lambda j, s: (1, 0, 0, 0))
         xn, yn = call(
@@ -676,6 +746,90 @@
         return keep, self.ring.core(send)
 
 
+class HalvingScatter(Scatter):
+    def second(self, scal):
+        shape = self.xk.shape[1:]
+        piece = (2, 2) + shape[1:]
+        part = lambda a: (a, (1,) + shape, lambda j, s: (0, 0, 0, 0))
+        whole = lambda a: (a, None, None)
+        self.kept, self.near = call(
+            add_second_half_kernel, self.name + "_add2", scal, (1,),
+            [part(self.xk), part(self.xr), whole(self.xm), part(self.yk), part(self.yr), whole(self.ym)],
+            [(piece, F32, None, None), (piece, BF, None, None)],
+        )
+        return self.kept
+
+    def send_second(self):
+        self.got = self.ring.z(self.near, 1)
+
+    def third(self, scal):
+        piece = self.kept.shape[1:]
+        self.own, self.far = call(
+            add_third_half_kernel, self.name + "_add3", scal, (1,),
+            [(a, None, None) for a in (self.kept, self.got)], [(piece, F32, None, None), (piece, BF, None, None)],
+        )
+        return self.own
+
+    def send_third(self):
+        self.arrived = self.ring.z(self.far, 2)
+
+    def last(self, scal):
+        piece = self.own.shape[1:]
+        keep, send = call(
+            functools.partial(add_last_half_kernel, self.core_at), self.name + "_add4", scal, (1,),
+            [(a, None, None) for a in (self.own, self.arrived)], [(piece, F32, None, None)] * 2,
+        )
+        return keep, self.ring.core(send)
+
+
+class DepthScatter:
+    def __init__(self, ring, core_at, name, sent):
+        self.ring, self.core_at, self.name = ring, core_at, name
+        self.kept, self.near = sent
+
+    def call(self, kernel, step, scal, ins, outs):
+        whole = lambda a: (a, None, None)
+        return call(kernel, self.name + step, scal, (), [*map(whole, ins)], [(s, d, None, None) for s, d in outs])
+
+    def send_near(self):
+        self.got = self.ring.z(self.near, 1)
+
+    def add_near(self, scal):
+        shape = self.kept.shape[1:]
+        self.own, self.far = self.call(add_near_kernel, "_add1", scal, (self.kept, self.got), [(shape, F32), (shape, BF)])
+        return self.own
+
+    def send_far(self):
+        self.got = self.ring.z(self.far, 2)
+
+    def add_far(self, scal):
+        shape = self.own.shape[2:]
+        self.xk, self.xs, self.yk, self.ys = self.call(
+            add_far_kernel, "_add2", scal, (self.own, self.got), [(shape, F32), (shape, BF)] * 2
+        )
+        return self.xk
+
+    def send_side(self):
+        self.xr, self.yr = self.ring.x(self.xs), self.ring.y(self.ys)
+
+    def add_side(self, scal):
+        shape = self.xk.shape
+        self.own, xn, yn = self.call(
+            add_side_kernel, "_add3", scal, (self.xk, self.xr, self.yk, self.yr),
+            [(shape, F32), (shape[1:], BF), (shape[1:], BF)],
+        )
+        self.xm, self.ym = self.ring.y(xn), self.ring.x(yn)
+        return self.own
+
+    def last(self, scal):
+        shape = self.own.shape[1:]
+        keep, send = self.call(
+            functools.partial(add_end_kernel, self.core_at), "_add4", scal, (self.own, self.xm, self.ym),
+            [(shape, F32)] * 2,
+        )
+        return keep, self.ring.core(send)
+
+
 def after(value, *others):
     if not others:
         return value
@@ -687,22 +841,20 @@
     return [jnp.where(first, own, got), jnp.where(first, got, own)]
 
 
-def finish_first_kernel(core_at, scal, reduce_own, reduce_got, expand_own, expand_got, reduce_o, expand_o, merge_o):
-    width = reduce_own.shape[1]
+def finish_kernel(
+    core_at, scal, own, got, reduce_own, reduce_got, expand_own, expand_got,
+    heads_o, reduce_o, expand_o, merge_o, *shares_o,
+):
+    width = own.shape[1]
+    rows = heads_o.shape[0]
     for n, part in enumerate(side_by_side(core_at, scal, reduce_own[...], reduce_got[...])):
         reduce_o[:, n * width : (n + 1) * width] = part
-    rows = merge_o.shape[0]
     blocks = expand_own.shape[0] // rows - 1
     for n, part in enumerate(side_by_side(core_at, scal, expand_own[...], expand_got[...])):
         for k in range(blocks):
             at = (n * blocks + k) * width
             expand_o[:, at : at + width] = part[k * rows : (k + 1) * rows]
         merge_o[:, n * width : (n + 1) * width] = part[blocks * rows :]
-
-
-def finish_last_kernel(core_at, scal, own, got, heads_o, *shares_o):
-    width = own.shape[1]
-    rows = heads_o.shape[0]
     for n, part in enumerate(side_by_side(core_at, scal, own[...], got[...])):
         for k in range(3):
             at = (2 * k + n) * width
@@ -788,21 +940,21 @@
     if fast:
         order = after(scal, tokens_o)
     att, inv, mixed, xhat, scale, normed, second, turned_own, act, slope = call(
-        functools.partial(ffn_kernel, head_at), "feed_forward", order, (FF_STEPS,),
+        functools.partial(ffn_kernel, head_at), "feed_forward", order, (FFN_STEPS,),
         [
             (rq, None, None), (num, None, None), (den, None, None), (prior, None, None),
             (tcol, None, None), (tokens, None, None), (w_merge, None, None), (b_merge, None, None),
             (gain_first, None, None), (bias_first, None, None), (b_reduce, None, None),
-            (w_expand, (D, FF_BLOCK), lambda j, s: (0, j)),
-            (b_expand, (1, FF_BLOCK), lambda j, s: (0, j)),
-            (w_reduce, (FF_BLOCK, D), lambda j, s: (j, 0)),
+            (w_expand, (D, FFN_BLOCK), lambda j, s: (0, j)),
+            (b_expand, (1, FFN_BLOCK), lambda j, s: (0, j)),
+            (w_reduce, (FFN_BLOCK, D), lambda j, s: (j, 0)),
         ],
         [
             (wide_shape, F32, None, None), (wide_shape, F32, None, None), (wide_shape, BF, None, None),
             (wide_shape, F32, None, None), ((rows, LANES), F32, None, None), (wide_shape, BF, None, None),
             (wide_shape, F32, None, None), ((2, 4, D // 4, rows), BF, None, None),
-            ((rows, FF), BF, (rows, FF_BLOCK), lambda j, s: (0, j)),
-            ((rows, FF), BF, (rows, FF_BLOCK), lambda j, s: (0, j)),
+            ((rows, FF), BF, (rows, FFN_BLOCK), lambda j, s: (0, j)),
+            ((rows, FF), BF, (rows, FFN_BLOCK), lambda j, s: (0, j)),
         ],
         us=11, vmem=VMEM_FFN,
     )
@@ -825,12 +977,12 @@
     by_z = lambda a: (a, (1, D // 4, rows), lambda j, s: (j, 0, 0))
     by_col = lambda a: (a, (rows, FF // 4), lambda j, s: (0, j))
 
-    def group(kernel, name, scal, ins, piece_rows, us, scratch=()):
+    def group(kernel, name, scal, ins, piece_rows, us, scratch=(), kind=Scatter):
         shape = (2, 4, piece_rows, D // 2)
         sent = call(
             functools.partial(kernel, pos_at), name, scal, (4,), ins, [(shape, BF, None, None)] * 4, scratch, us
         )
-        return Scatter(ring, core_at, name, sent)
+        return kind(ring, core_at, name, sent)
 
     ff_half = FF_STEPS // 2
     in_hbm = lambda a: (a, None, pltpu.HBM)
@@ -851,12 +1003,14 @@
     if fast:
         pg_o = ring.core(pg_send)
         act_o, turned_other, bg_o = map(ring.core, (act, turned_own, bg_send))
-        reduced = group(
-            reduce_grad_kernel, "grad_reduce", after(scal, partial, turned_other),
-            [by_col(act), by_col(act_o), whole(bg_keep), whole(bg_o)], large, 6,
-        )
-        order = after(scal, reduced.xs)
-        reduced.send()
+        pieces = ((2, 2, 2, 2, large, D // 2), BF, None, None)
+        sent = call(
+            functools.partial(reduce_grad_kernel, pos_at), "grad_reduce", after(scal, partial, turned_other), (4,),
+            [by_col(act), by_col(act_o), whole(bg_keep), whole(bg_o)], [pieces, pieces], us=6,
+        )
+        reduced = DepthScatter(ring, core_at, "grad_reduce", sent)
+        reduced.send_near()
+        order = after(scal, reduced.near)
 
     pg_keep, grad_first, mg_keep, mg_send, w_att, e_att, later, sum_kept, sums_first = call(
         functools.partial(back_kernel, core_at), "feed_forward_back", order, (),
@@ -871,7 +1025,7 @@
             ((PAIRS + 1, LANES, LANES), BF, None, None), hidden_sums, ((8, D), F32, None, None),
         ],
         [pltpu.VMEM(wide_shape, F32), *buffers],
-        us=9, vmem=VMEM_BACK,
+        us=COST_BACK, vmem=VMEM_BACK,
     )
     later = ring.x(later)
 
@@ -883,53 +1037,52 @@
                 part(turned_own, 1), part(turned_other, 1), whole(pg_keep), whole(pg_o),
                 part(turned_own, 0), part(turned_other, 0), whole(mg_keep), whole(mg_o),
             ],
-            5 * small, COST_EXPAND,
-        )
-        order = after(scal, reduced.first(after(scal, expanded.xs, later)))
-        reduced.send_first()
+            5 * small, COST_EXPAND, kind=HalvingScatter,
+        )
+        expanded.send(later)
+        order = after(scal, expanded.xs, later)
 
     half_pairs = PAIRS // 2
     pair_blocks = lambda core_of: [
         (a, (rows, LANES), lambda j, s: (0, core_of(s) * half_pairs + j)) for a in (rq, rk, v, w_att)
     ]
     both_states = [whole(e_att), whole(prior), whole(later), whole(tcol)]
-    pj_out = ((3, rows, D // 2), BF, (3, rows, LANES), lambda j, s: (0, 0, j))
+    pj_out = [((3, rows // 2, D // 2), BF, (3, rows // 2, LANES), lambda j, s: (0, 0, j))] * 2
     pj_sums = ((3, 8, D // 2), F32, (3, 8, LANES), lambda j, s: (0, 0, j))
     table = ((rows, rows), F32, None, None)
-    pj_send, sum_heads_sent, weights, weights_t = call(
+    *pj_send, sum_heads_sent, weights, weights_t = call(
         functools.partial(attn_sent_kernel, head_at, core_at), "attention_back_sent", order, (half_pairs,),
-        [*pair_blocks(lambda s: 1 - s[core_at]), *both_states, whole(trow)], [pj_out, pj_sums, table, table], us=COST_SENT,
+        [*pair_blocks(lambda s: 1 - s[core_at]), *both_states, whole(trow)], [*pj_out, pj_sums, table, table], us=COST_SENT,
     )
     order = scal
     if fast:
-        pj_o = ring.core(pj_send)
-        order = after(scal, reduced.second(after(scal, pj_send)))
-        expanded.send()
-    pj_keep, sum_heads_kept = call(
+        pj_o = [ring.core(v) for v in pj_send]
+        order = after(scal, reduced.add_near(after(scal, pj_send[0])))
+        reduced.send_far()
+    *pj_keep, sum_heads_kept = call(
         functools.partial(attn_kept_kernel, head_at, core_at), "attention_back_kept", order, (half_pairs,),
-        [*pair_blocks(lambda s: s[core_at]), *both_states, whole(weights), whole(weights_t)], [pj_out, pj_sums], us=COST_KEPT,
+        [*pair_blocks(lambda s: s[core_at]), *both_states, whole(weights), whole(weights_t)], [*pj_out, pj_sums], us=COST_KEPT,
     )
 
     if fast:
-        order = after(scal, expanded.first(after(scal, pj_keep), us=20))
-        expanded.send_first(pj_o)
-        reduced.send_second()
+        order = after(scal, expanded.first(after(scal, pj_keep[0])))
+        expanded.send_first()
         heads = group(
             functools.partial(heads_grad_kernel, devices=devices), "grad_heads", order,
             [
-                by_z(tokens_t), by_z(tokens_o), whole(pj_keep), whole(pj_o),
+                by_z(tokens_t), by_z(tokens_o), *map(whole, (*pj_keep, *pj_o)),
                 *map(whole, (sum_heads_kept, sum_heads_sent, sums_first, sum_kept, sum_sent, sums_second)),
             ],
             3 * small + 8, COST_HEADS, [pltpu.VMEM((devices, D // 2), F32)],
         )
-        heads.send(expanded.xm, expanded.ym)
+        heads.send()
         order = after(scal, heads.xs)
 
-    of_part = lambda a: (a, (1, rows, D // 2), lambda j, s: (j, 0, 0))
+    of_part = lambda a: (a, (1, rows // 2, D // 2), lambda j, s: (j, 0, 0))
     (input_grad,) = call(
         input_kernel, "input_grad", order, (3,),
         [
-            whole(grad_first), of_part(pj_keep), of_part(pj_send),
+            whole(grad_first), *map(of_part, (*pj_keep, *pj_send)),
             (w_heads, (D, D // 2), lambda j, s: (0, 2 * j + s[core_at])),
             (w_heads, (D, D // 2), lambda j, s: (0, 2 * j + 1 - s[core_at])),
         ],
@@ -938,25 +1091,26 @@
     )
 
     if fast:
-        reduce_own, reduce_got = reduced.last(after(scal, input_grad))
-        order = expanded.second(after(scal, reduce_own))
+        order = reduced.add_far(after(scal, input_grad))
+        order = expanded.second(after(scal, order))
         expanded.send_second()
+        reduced.send_side()
         order = heads.first(after(scal, order))
         heads.send_first()
+        order = expanded.third(after(scal, order))
+        expanded.send_third()
         order = heads.second(after(scal, order))
         heads.send_second()
+        order = reduced.add_side(after(scal, order))
         expand_own, expand_got = expanded.last(after(scal, order))
-        heads_own, heads_got = heads.last(after(scal, expand_own))
+        reduce_own, reduce_got = reduced.last(after(scal, expand_own))
+        heads_own, heads_got = heads.last(after(scal, reduce_own))
         out = lambda n, m: ((n, m), F32, None, None)
-        w_reduce_grad, w_expand_grad, w_merge_grad = call(
-            functools.partial(finish_first_kernel, core_at), "finish_first", after(scal, heads_own), (),
-            [*map(whole, (reduce_own, reduce_got, expand_own, expand_got))],
-            [out(large, D), out(small, FF), out(small, D)],
-        )
         counts = (2 * small, small, small, small, small, large, small, small, small)
-        w_heads_grad, *shares = call(
-            functools.partial(finish_last_kernel, core_at), "finish_last", scal, (),
-            [whole(heads_own), whole(heads_got)], [out(small, 3 * D), *(out(1, n) for n in counts)],
+        w_heads_grad, w_reduce_grad, w_expand_grad, w_merge_grad, *shares = call(
+            functools.partial(finish_kernel, core_at), "finish", scal, (),
+            [*map(whole, (heads_own, heads_got, reduce_own, reduce_got, expand_own, expand_got))],
+            [out(small, 3 * D), out(large, D), out(small, FF), out(small, D), *(out(1, n) for n in counts)],
         )
         shares = [share.reshape(-1) for share in shares]
         grads = (
@@ -971,6 +1125,7 @@
         by_heads = lambda keep, send: jnp.concatenate(
             [by_core(keep[n], send[n]) for n in range(3)], axis=1
         )
+        pj_keep, pj_send = (jnp.concatenate(v, axis=1) for v in (pj_keep, pj_send))
         sum_heads = by_heads(sum_heads_kept, sum_heads_sent)[0]
         scatter = lambda v: lax.psum_scatter(v, AXES, scatter_dimension=0, tiled=True)
         grads = (

time: 153 us -> 141 us (0.922)
  starting transfers between devices: 34.3 us -> 29 us
  waiting for transfers between devices: 28.9 us -> 25.3 us
    ppermute x33 -> x32, starting transfers between devices: 34.3 us -> 29 us  [swap(): lax.ppermute(value, AXES, [(i, i ^ bits) for i in range(self.devices)])]
    ppermute x33 -> x32, waiting for transfers between devices: 28.9 us -> 25.3 us  [swap(): lax.ppermute(value, AXES, [(i, i ^ bits) for i in range(self.devices)])]
    pallas_call x23 -> x24, Pallas kernels: 82.1 us -> 80.7 us  [call(): pl.pallas_call(kernel, name=name, grid_spec=pltpu.PrefetchScalarGridSpec(...]
    unnamed x50 -> x34, local copies, waits for them, and re-layouts: 4.45 us -> 3.21 us
  transfers between devices with their start and end apart: 33 -> 32, of which waited for: 12 -> 9; matrix products, arithmetic and copies ran while one was open for 0% -> 0% of each run, Pallas kernels for 42% -> 46%
where the time goes in v4:
time: 141 us
  Pallas kernels  80.7 us (57%)
  starting transfers between devices  29 us (21%)
  waiting for transfers between devices  25.3 us (18%)
  local copies, waits for them, and re-layouts  4.69 us (3%)
    pallas_call x24, Pallas kernels, call(): pl.pallas_call(kernel, name=name, grid_spec=pltpu.PrefetchScalarGridSpec(...  80.7 us
    ppermute x32, starting transfers between devices, swap(): lax.ppermute(value, AXES, [(i, i ^ bits) for i in range(self.devices)])  29 us
    ppermute x32, waiting for transfers between devices, swap(): lax.ppermute(value, AXES, [(i, i ^ bits) for i in range(self.devices)])  25.3 us
    unnamed x34, local copies, waits for them, and re-layouts  3.21 us
  transfers between devices with their start and end apart: 32, of which 9 were waited for; matrix products, arithmetic and copies ran while one was open for 0% of the time, Pallas kernels for 46%

profile of v4, /device:TPU:0, one launch (start us, length us, event | category | flops | bytes accessed | tf_op | source)
XLA Modules:
  0.0 141.0 jit_solution(10187091636997446175)
XLA Ops:
  0.7 0.7 reshape.81.bk.bv.bq
  1.4 0.7 concatenate.3.scal
  2.1 2.0 %copy-done = bf16[768,2304]{1,0:T(8,128)(2,1)S(1)} copy-done((bf16[768,2304]{1,0:T(8,128)(2,1)S(1)}, bf16[768,2304]{1,0:T(8,128)(2,1)}, u32[]{:S(2)}) %copy-start) | copy-done | bytes 3538968
  4.1 1.1 copy-done.3
  5.3 4.1 %keys_values.1 = (bf16[512,768]{1,0:T(8,128)(2,1)S(1)}, bf16[512,768]{1,0:T(8,128)(2,1)S(1)}, bf16[7,128,128]{2,1,0:T(8,128)(2,1)S(1)}, f32[512,128]{1,0:T(8,128...) custom-call(s32[9]{0:T(128)S(1)} %concatenate.3.scal, bf16[512,768]{1,0:T(8,128)(2,1)S(1)} %copy-done.3, ...), custom_call_target="tpu_custom_call" | custom-call | flops 4600000000 | bytes 1 | tf_op jit(solution)/shard_map/keys_values/pallas_call | solution.py:55
  9.9 2.6 %collective-permute-start.1 = (bf16[7,128,128]{2,1,0:T(8,128)(2,1)S(1)}, bf16[7,128,128]{2,1,0:T(8,128)(2,1)S(1)}, u32[]{:S(2)}, u32[]{:S(2)}) collective-permute-start(bf16[7,128,128]{2,1,0:T(8,128)(2,1)S(1)} %get-tuple-element.137), channel_id=1, source_target_pairs={{0,1},{1,0},{2,3},{3,2},{4,5},{5,4},{6,7},{7,6},{8,9},{9,8},{10,11... | collective-permute-start | bytes 688136 | tf_op jit(solution)/shard_map/ppermute | solution.py:619
  12.5 5.7 %local_attention.1 = (bf16[512,768]{1,0:T(8,128)(2,1)S(1)}, f32[512,768]{1,0:T(8,128)S(1)}, f32[512,768]{1,0:T(8,128)S(1)}) custom-call(s32[9]{0:T(128)S(1)} %concatenate.3.scal, bf16[512,768]{1,0:T(8,128)(2,1)S(1)} %copy-done.3, bf16[768,2304]{1,0:T(8,128)(2,1)S(1)} %copy-done, bf16[1,2304]{1,0:T(2,128)(2,1)S(1)} %reshape.81.bk.bv.bq, ...), custom_call_target="tpu_custom_call" | custom-call | flops 6899999744 | bytes 1 | tf_op jit(solution)/shard_map/local_attention/pallas_call | solution.py:55
  18.7 10.4 %feed_forward.1 = (f32[512,768]{1,0:T(8,128)S(1)}, f32[512,768]{1,0:T(8,128)S(1)}, bf16[512,768]{1,0:T(8,128)(2,1)}, f32[512,768]{1,0:T(8,128)S(1)}, f32[512,128...) custom-call(s32[9]{0:T(128)S(1)} %concatenate.3.scal, ...), custom_call_target="tpu_custom_call" | custom-call | flops 12650000384 | bytes 1 | tf_op jit(solution)/shard_map/feed_forward/pallas_call | solution.py:55
  29.7 2.6 %second_norm.1 = (bf16[512,768]{1,0:T(8,128)(2,1)}, f32[512,768]{1,0:T(8,128)S(1)}, bf16[512,768]{1,0:T(8,128)(2,1)S(1)}, bf16[512,384]{1,0:T(8,128)(2,1)S(1)}, ...) custom-call(s32[9]{0:T(128)S(1)} %concatenate.3.scal, f32[512,768]{1,0:T(8,128)S(1)} %get-tuple-element.138.second, ...), custom_call_target="tpu_custom_call" | custom-call | flops 2990000128 | bytes 1 | tf_op jit(solution)/shard_map/second_norm/pallas_call | solution.py:55
  32.3 5.6 %feed_forward_back_sent.1 = (bf16[2,512,768]{2,1,0:T(8,128)(2,1)S(1)}, f32[1,1536]{1,0:T(1,128)S(1)}, f32[512,768]{1,0:T(8,128)S(1)}) custom-call(s32[9]{0:T(128)S(1)} %concatenate.3.scal, bf16[512,768]{1,0:T(8,128)(2,1)S(1)} %get-tuple-element.141.full, bf16[512,3072]{1,0:T(8,128)(2,1)S(1)} %get-tuple-element.142.slope, bf16[768,3072]{1,0:T(8,128)(2,1)S(1)} %bitcast.15, ...), custom_call_target="tpu_custom_call" | custom-call | flops 5750000128 | bytes 1 | tf_op jit(solution)/shard_map/feed_forward_back_sent/pallas_call | solution.py:55
  38.5 5.3 %grad_reduce.1 = (bf16[2,2,2,2,96,384]{5,4,3,2,1,0:T(8,128)(2,1)S(1)}, bf16[2,2,2,2,96,384]{5,4,3,2,1,0:T(8,128)(2,1)S(1)}) custom-call(s32[9]{0:T(128)S(1)} %concatenate.3.scal, bf16[512,3072]{1,0:T(8,128)(2,1)S(1)} %get-tuple-element.146.a_own, bf16[512,3072]{1,0:T(8,128)(2,1)S(1)} %collective-permute-done.3.a_oth, ...), custom_call_target="tpu_custom_call" | custom-call | flops 6899999744 | bytes 1 | tf_op jit(solution)/shard_map/grad_reduce/pallas_call | solution.py:55
  43.8 1.9 %collective-permute-start.8 = (bf16[2,2,2,2,96,384]{5,4,3,2,1,0:T(8,128)(2,1)S(1)}, bf16[2,2,2,2,96,384]{5,4,3,2,1,0:T(8,128)(2,1)S(1)}, u32[]{:S(2)}, u32[]{:S(2)}) collective-permute-start(bf16[2,2,2,2,96,384]{5,4,3,2,1,0:T(8,128)(2,1)S(1)} %get-tuple-element.149), channel_id=1, source_target_pairs={{0,8},{1,9},{2,10},{3,11},{4,12},{5,13},{6,14},{7,15},{8,0},{9,1},... | collective-permute-start | bytes 3538952 | tf_op jit(solution)/shard_map/ppermute | solution.py:619
  45.8 8.7 %feed_forward_back.1 = (bf16[2,512,768]{2,1,0:T(8,128)(2,1)S(1)}, f32[512,768]{1,0:T(8,128)S(1)}, bf16[512,384]{1,0:T(8,128)(2,1)S(1)}, bf16[512,384]{1,0:T(8,12...) custom-call(s32[9]{0:T(128)S(1)} %concatenate.3.scal, ...), custom_call_target="tpu_custom_call" | custom-call | flops 3449999872 | bytes 1 | tf_op jit(solution)/shard_map/feed_forward_back/pallas_call | solution.py:55
  54.5 1.6 %collective-permute-start.7 = (bf16[7,128,128]{2,1,0:T(8,128)(2,1)S(1)}, bf16[7,128,128]{2,1,0:T(8,128)(2,1)S(1)}, u32[]{:S(2)}, u32[]{:S(2)}) collective-permute-start(bf16[7,128,128]{2,1,0:T(8,128)(2,1)S(1)} %get-tuple-element.160), channel_id=1, source_target_pairs={{0,1},{1,0},{2,3},{3,2},{4,5},{5,4},{6,7},{7,6},{8,9},{9,8},{10,11... | collective-permute-start | bytes 688136 | tf_op jit(solution)/shard_map/ppermute | solution.py:619
  56.2 4.6 %grad_expand.1 = (bf16[2,4,120,384]{3,2,1,0:T(8,128)(2,1)S(1)}, bf16[2,4,120,384]{3,2,1,0:T(8,128)(2,1)S(1)}, bf16[2,4,120,384]{3,2,1,0:T(8,128)(2,1)S(1)}, bf16[2,4,120,384]{3,2,1,0:T(8,128)(2,1)S(1)}) custom-call(s32[9]{0:T(128)S(1)} %concatenate.3.scal, bf16[2,4,192,512]{3,2,1,0:T(8,128)(2,1)S(1)} %get-tuple-element.140.a_own.m_own, ...), custom_call_target="tpu_custom_call" | custom-call | flops 1150000000 | bytes 1 | tf_op jit(solution)/shard_map/grad_expand/pallas_call | solution.py:55
  60.9 1.7 %collective-permute-done.7.later = bf16[7,128,128]{2,1,0:T(8,128)(2,1)S(1)} collective-permute-done((bf16[7,128,128]{2,1,0:T(8,128)(2,1)S(1)}, bf16[7,128,128]{2,1,0:T(8,128)(2,1)S(1)}, u32[]{:S(2)}, u32[]{:S(2)}) %collective-permute-start.7) | collective-permute-done | bytes 229408 | tf_op jit(solution)/shard_map/ppermute | solution.py:619
  62.5 1.5 %collective-permute-start.9 = (bf16[2,4,120,384]{3,2,1,0:T(8,128)(2,1)S(1)}, bf16[2,4,120,384]{3,2,1,0:T(8,128)(2,1)S(1)}, u32[]{:S(2)}, u32[]{:S(2)}) collective-permute-start(bf16[2,4,120,384]{3,2,1,0:T(8,128)(2,1)S(1)} %get-tuple-element.174), channel_id=1, source_target_pairs={{0,1},{1,0},{2,3},{3,2},{4,5},{5,4},{6,7},{7,6},{8,9},{9,8},{10,11... | collective-permute-start | bytes 2211848 | tf_op jit(solution)/shard_map/ppermute | solution.py:619
  64.0 1.5 %collective-permute-start.10 = (bf16[2,4,120,384]{3,2,1,0:T(8,128)(2,1)S(1)}, bf16[2,4,120,384]{3,2,1,0:T(8,128)(2,1)S(1)}, u32[]{:S(2)}, u32[]{:S(2)}) collective-permute-start(bf16[2,4,120,384]{3,2,1,0:T(8,128)(2,1)S(1)} %get-tuple-element.177), channel_id=1, source_target_pairs={{0,4},{1,5},{2,6},{3,7},{4,0},{5,1},{6,2},{7,3},{8,12},{9,13},{10,... | collective-permute-start | bytes 2211848 | tf_op jit(solution)/shard_map/ppermute | solution.py:619
  65.5 7.6 %attention_back_sent.1 = (bf16[3,256,384]{2,1,0:T(8,128)(2,1)S(1)}, bf16[3,256,384]{2,1,0:T(8,128)(2,1)S(1)}, f32[3,8,384]{2,1,0:T(8,128)S(1)}, f32[512,512]{1,0:T(8,128)S(1)}, f32[512,512]{1,0:T(8,128)S(1)}) custom-call(s32[9]{0:T(128)S(1)} %concatenate.3.scal, bf16[512,768]{1,0:T(8,128)(2,1)S(1)} %get-tuple-element.134.refs_0_.rq, ...), custom_call_target="tpu_custom_call" | custom-call | flops 575000000 | bytes 1 | tf_op jit(solution)/shard_map/attention_back_sent/pallas_call | solution.py:55
  73.7 0.8 grad_reduce_add1.1
  74.5 2.7 %collective-permute-start.13 = (bf16[2,2,2,96,384]{4,3,2,1,0:T(8,128)(2,1)S(1)}, bf16[2,2,2,96,384]{4,3,2,1,0:T(8,128)(2,1)S(1)}, u32[]{:S(2)}, u32[]{:S(2)}) collective-permute-start(bf16[2,2,2,96,384]{4,3,2,1,0:T(8,128)(2,1)S(1)} %get-tuple-element.192), channel_id=1, source_target_pairs={{0,16},{1,17},{2,18},{3,19},{4,20},{5,21},{6,22},{7,23},{8,24},{9,... | collective-permute-start | bytes 1769480 | tf_op jit(solution)/shard_map/ppermute | solution.py:619
  77.2 6.7 %attention_back_kept.1 = (bf16[3,256,384]{2,1,0:T(8,128)(2,1)S(1)}, bf16[3,256,384]{2,1,0:T(8,128)(2,1)S(1)}, f32[3,8,384]{2,1,0:T(8,128)S(1)}) custom-call(s32[9]{0:T(128)S(1)} %concatenate.3.scal, bf16[512,768]{1,0:T(8,128)(2,1)S(1)} %get-tuple-element.134.refs_0_.rq, bf16[512,768]{1,0:T(8,128)(2,1)S(1)} %get-tuple-element.130.rk, ...), custom_call_target="tpu_custom_call" | custom-call | flops 575000000 | bytes 1 | tf_op jit(solution)/shard_map/attention_back_kept/pallas_call | solution.py:55
  83.9 0.7 grad_expand_add1.1
  85.3 0.8 collective-permute-start.14
  86.1 5.1 %grad_heads.1 = (bf16[2,4,80,384]{3,2,1,0:T(8,128)(2,1)S(1)}, bf16[2,4,80,384]{3,2,1,0:T(8,128)(2,1)S(1)}, bf16[2,4,80,384]{3,2,1,0:T(8,128)(2,1)S(1)}, bf16[2,4,80,384]{3,2,1,0:T(8,128)(2,1)S(1)}) custom-call(s32[9]{0:T(128)S(1)} %concatenate.3.scal, bf16[4,192,512]{2,1,0:T(8,128)(2,1)S(1)} %get-tuple-element.128.a_own, ...), custom_call_target="tpu_custom_call" | custom-call | flops 115000000 | bytes 1 | tf_op jit(solution)/shard_map/grad_heads/pallas_call | solution.py:55
  91.2 1.2 collective-permute-start.17
  92.4 1.5 %collective-permute-start.16 = (bf16[2,4,80,384]{3,2,1,0:T(8,128)(2,1)S(1)}, bf16[2,4,80,384]{3,2,1,0:T(8,128)(2,1)S(1)}, u32[]{:S(2)}, u32[]{:S(2)}) collective-permute-start(bf16[2,4,80,384]{3,2,1,0:T(8,128)(2,1)S(1)} %get-tuple-element.188), channel_id=1, source_target_pairs={{0,1},{1,0},{2,3},{3,2},{4,5},{5,4},{6,7},{7,6},{8,9},{9,8},{10,11... | collective-permute-start | bytes 1474568 | tf_op jit(solution)/shard_map/ppermute | solution.py:619
  93.9 5.3 %input_grad.1 = f32[512,768]{1,0:T(8,128)} custom-call(s32[9]{0:T(128)S(1)} %concatenate.3.scal, f32[512,768]{1,0:T(8,128)S(1)} %get-tuple-element.190.first, bf16[3,256,384]{2,1,0:T(8,128)(2,1)S(1)} %get-tuple-element.171.own_early.keep_early, bf16[3,256,384]{2,1,0:T(8,128)(2,1)S(1)} %get-tuple-element.180.own_late.keep_late, ...), custom_call_target="tpu_custom_call" | custom-call | flops 115000000 | bytes 1 | tf_op jit(solution)/shard_map/input_grad/pallas_call | solution.py:55
  99.2 4.1 %collective-permute-done.13.got = bf16[2,2,2,96,384]{4,3,2,1,0:T(8,128)(2,1)S(1)} collective-permute-done((bf16[2,2,2,96,384]{4,3,2,1,0:T(8,128)(2,1)S(1)}, bf16[2,2,2,96,384]{4,3,2,1,0:T(8,128)(2,1)S(1)}, u32[]{:S(2)}, u32[]{:S(2)}) %collective-permute-start.13) | collective-permute-done | bytes 589856 | tf_op jit(solution)/shard_map/ppermute | solution.py:619
  103.3 0.7 grad_reduce_add2.1
  104.0 0.8 grad_expand_add2.1
  104.9 0.9 collective-permute-done.17.yr
  105.8 0.7 grad_heads_add1.1
  106.5 1.6 %collective-permute-start.20 = (bf16[4,80,384]{2,1,0:T(8,128)(2,1)S(1)}, bf16[4,80,384]{2,1,0:T(8,128)(2,1)S(1)}, u32[]{:S(2)}, u32[]{:S(2)}) collective-permute-start(bf16[4,80,384]{2,1,0:T(8,128)(2,1)S(1)} %get-tuple-element.206), channel_id=1, source_target_pairs={{0,1},{1,0},{2,3},{3,2},{4,5},{5,4},{6,7},{7,6},{8,9},{9,8},{10,11... | collective-permute-start | bytes 737288 | tf_op jit(solution)/shard_map/ppermute | solution.py:619
  109.1 1.5 %collective-permute-start.22 = (bf16[2,96,384]{2,1,0:T(8,128)(2,1)S(1)}, bf16[2,96,384]{2,1,0:T(8,128)(2,1)S(1)}, u32[]{:S(2)}, u32[]{:S(2)}) collective-permute-start(bf16[2,96,384]{2,1,0:T(8,128)(2,1)S(1)} %get-tuple-element.211), channel_id=1, source_target_pairs={{0,4},{1,5},{2,6},{3,7},{4,0},{5,1},{6,2},{7,3},{8,12},{9,13},{10,... | collective-permute-start | bytes 442376 | tf_op jit(solution)/shard_map/ppermute | solution.py:619
  110.6 4.9 %collective-permute-done.18.got = bf16[2,2,120,384]{3,2,1,0:T(8,128)(2,1)S(1)} collective-permute-done((bf16[2,2,120,384]{3,2,1,0:T(8,128)(2,1)S(1)}, bf16[2,2,120,384]{3,2,1,0:T(8,128)(2,1)S(1)}, u32[]{:S(2)}, u32[]{:S(2)}) %collective-permute-start.18) | collective-permute-done | bytes 368672 | tf_op jit(solution)/shard_map/ppermute | solution.py:619
  115.5 0.6 grad_expand_add3.1
  116.1 0.7 collective-permute-start.23
  116.8 0.7 grad_heads_add2.1
  117.5 0.6 grad_reduce_add3.1
  118.6 1.6 %collective-permute-start.26 = (bf16[2,80,384]{2,1,0:T(8,128)(2,1)S(1)}, bf16[2,80,384]{2,1,0:T(8,128)(2,1)S(1)}, u32[]{:S(2)}, u32[]{:S(2)}) collective-permute-start(bf16[2,80,384]{2,1,0:T(8,128)(2,1)S(1)} %get-tuple-element.221), channel_id=1, source_target_pairs={{0,8},{1,9},{2,10},{3,11},{4,12},{5,13},{6,14},{7,15},{8,0},{9,1},... | collective-permute-start | bytes 368648 | tf_op jit(solution)/shard_map/ppermute | solution.py:619
  120.2 1.2 collective-permute-start.27
  121.4 1.6 %collective-permute-start.28 = (bf16[2,80,384]{2,1,0:T(8,128)(2,1)S(1)}, bf16[2,80,384]{2,1,0:T(8,128)(2,1)S(1)}, u32[]{:S(2)}, u32[]{:S(2)}) collective-permute-start(bf16[2,80,384]{2,1,0:T(8,128)(2,1)S(1)} %get-tuple-element.223), channel_id=1, source_target_pairs={{0,24},{1,25},{2,26},{3,27},{4,28},{5,29},{6,30},{7,31},{8,16},{9,... | collective-permute-start | bytes 368648 | tf_op jit(solution)/shard_map/ppermute | solution.py:619
  122.9 9.2 %collective-permute-done.23.got = bf16[2,120,384]{2,1,0:T(8,128)(2,1)S(1)} collective-permute-done((bf16[2,120,384]{2,1,0:T(8,128)(2,1)S(1)}, bf16[2,120,384]{2,1,0:T(8,128)(2,1)S(1)}, u32[]{:S(2)}, u32[]{:S(2)}) %collective-permute-start.23) | collective-permute-done | bytes 184352 | tf_op jit(solution)/shard_map/ppermute | solution.py:619
  133.4 3.1 %collective-permute-done.25.ym = bf16[96,384]{1,0:T(8,128)(2,1)S(1)} collective-permute-done((bf16[96,384]{1,0:T(8,128)(2,1)S(1)}, bf16[96,384]{1,0:T(8,128)(2,1)S(1)}, u32[]{:S(2)}, u32[]{:S(2)}) %collective-permute-start.25) | collective-permute-done | bytes 73760 | tf_op jit(solution)/shard_map/ppermute | solution.py:619
  137.2 0.6 grad_heads_add3.1
  138.3 1.0 collective-permute-done.29.got
  139.3 1.5 %finish.1 = (f32[24,2304]{1,0:T(8,128)}, f32[96,768]{1,0:T(8,128)}, f32[24,3072]{1,0:T(8,128)}, f32[24,768]{1,0:T(8,128)}, f32[1,48]{1,0:T(1,128)}, /*index=5*/f...) custom-call(s32[9]{0:T(128)S(1)} %concatenate.3.scal, ...), custom_call_target="tpu_custom_call" | custom-call | flops 115000000 | bytes 1 | tf_op jit(solution)/shard_map/finish/pallas_call | solution.py:55
  (85 shorter events, 7.3 us)
Async XLA Ops:
  2.1 2.0 %copy-start = (bf16[768,2304]{1,0:T(8,128)(2,1)S(1)}, bf16[768,2304]{1,0:T(8,128)(2,1)}, u32[]{:S(2)}) copy-start(bf16[768,2304]{1,0:T(8,128)(2,1)} %w_send.1) | copy-start | bytes 10616836
  5.3 13.4 %slice-start = ((s8[4718592]{0:T(1024)(128)(4,1)}), s8[4194304]{0:T(1024)(128)(4,1)S(1)}, s32[]{:S(2)}) async-start(s8[4718592]{0:T(1024)(128)(4,1)} %bitcast.14), calls=%async_computation | async-start | bytes 8388608
  5.3 13.4 %slice-start.2 = ((s8[4718592]{0:T(1024)(128)(4,1)}), s8[4194304]{0:T(1024)(128)(4,1)S(1)}, s32[]{:S(2)}) async-start(s8[4718592]{0:T(1024)(128)(4,1)} %bitcast.16), calls=%async_computation.2 | async-start | bytes 8388608
  9.4 9.0 %collective-permute-start = (bf16[4,192,512]{2,1,0:T(8,128)(2,1)S(1)}, bf16[4,192,512]{2,1,0:T(8,128)(2,1)S(1)}, u32[]{:S(2)}, u32[]{:S(2)}) collective-permute-start(bf16[4,192,512]{2,1,0:T(8,128)(2,1)S(1)} %get-tuple-element.128.a_own), channel_id=1, source_target_pairs={{0,2},{1,3},{2,0},{3,1},{4,6},{5,7},{6,4},{7,5},{8,10},{9,11},{10,... | collective-permute-start | bytes 2359304 | tf_op jit(solution)/shard_map/ppermute | solution.py:619
  9.9 8.8 %collective-permute-start.1 = (bf16[7,128,128]{2,1,0:T(8,128)(2,1)S(1)}, bf16[7,128,128]{2,1,0:T(8,128)(2,1)S(1)}, u32[]{:S(2)}, u32[]{:S(2)}) collective-permute-start(bf16[7,128,128]{2,1,0:T(8,128)(2,1)S(1)} %get-tuple-element.137), channel_id=1, source_target_pairs={{0,1},{1,0},{2,3},{3,2},{4,5},{5,4},{6,7},{7,6},{8,9},{9,8},{10,11... | collective-permute-start | bytes 688136 | tf_op jit(solution)/shard_map/ppermute | solution.py:619
  12.4 5.8 %copy-start.7 = (bf16[768]{0:T(1024)(128)(2,1)S(1)}, bf16[768]{0:T(1024)(128)(2,1)}, u32[]{:S(2)}) copy-start(bf16[768]{0:T(1024)(128)(2,1)} %param.20) | copy-start | bytes 4612
  12.4 5.8 %copy-start.8 = (bf16[768]{0:T(1024)(128)(2,1)S(1)}, bf16[768]{0:T(1024)(128)(2,1)}, u32[]{:S(2)}) copy-start(bf16[768]{0:T(1024)(128)(2,1)} %param.19) | copy-start | bytes 4612
  12.4 5.8 %copy-start.9 = (bf16[768]{0:T(1024)(128)(2,1)S(1)}, bf16[768]{0:T(1024)(128)(2,1)}, u32[]{:S(2)}) copy-start(bf16[768]{0:T(1024)(128)(2,1)} %param.21) | copy-start | bytes 4612
  12.4 5.9 %copy-start.10 = (bf16[768]{0:T(1024)(128)(2,1)S(1)}, bf16[768]{0:T(1024)(128)(2,1)}, u32[]{:S(2)}) copy-start(bf16[768]{0:T(1024)(128)(2,1)} %param.25) | copy-start | bytes 4612
  12.5 5.9 %copy-start.6 = (bf16[3072]{0:T(1024)(128)(2,1)S(1)}, bf16[3072]{0:T(1024)(128)(2,1)}, u32[]{:S(2)}) copy-start(bf16[3072]{0:T(1024)(128)(2,1)} %param.23) | copy-start | bytes 18436
  12.5 6.2 %slice-start.1 = ((s8[4718592]{0:T(1024)(128)(4,1)}), s8[524288]{0:T(1024)(128)(4,1)S(1)}, s32[]{:S(2)}) async-start(s8[4718592]{0:T(1024)(128)(4,1)} %bitcast.14), calls=%async_computation.1 | async-start | bytes 1048576
  12.5 6.2 %slice-start.3 = ((s8[4718592]{0:T(1024)(128)(4,1)}), s8[524288]{0:T(1024)(128)(4,1)S(1)}, s32[]{:S(2)}) async-start(s8[4718592]{0:T(1024)(128)(4,1)} %bitcast.16), calls=%async_computation.3 | async-start | bytes 1048576
  12.5 6.2 %copy-start.2 = (bf16[768,768]{1,0:T(8,128)(2,1)S(1)}, bf16[768,768]{1,0:T(8,128)(2,1)}, u32[]{:S(2)}) copy-start(bf16[768,768]{1,0:T(8,128)(2,1)} %w_merge.1) | copy-start | bytes 3538948
  12.5 6.2 %copy-start.4 = (bf16[512,768]{1,0:T(8,128)(2,1)S(1)}, bf16[512,768]{1,0:T(8,128)(2,1)}, u32[]{:S(2)}) copy-start(bf16[512,768]{1,0:T(8,128)(2,1)} %refs_5_.1) | copy-start | bytes 2359300
  18.7 10.9 %copy-start.11 = (bf16[768]{0:T(1024)(128)(2,1)S(1)}, bf16[768]{0:T(1024)(128)(2,1)}, u32[]{:S(2)}) copy-start(bf16[768]{0:T(1024)(128)(2,1)} %param.26) | copy-start | bytes 4612
  18.7 10.9 %copy-start.12 = (bf16[768]{0:T(1024)(128)(2,1)S(1)}, bf16[768]{0:T(1024)(128)(2,1)}, u32[]{:S(2)}) copy-start(bf16[768]{0:T(1024)(128)(2,1)} %param.27) | copy-start | bytes 4612
  18.7 10.9 %copy-start.5 = (bf16[512,768]{1,0:T(8,128)(2,1)S(1)}, bf16[512,768]{1,0:T(8,128)(2,1)}, u32[]{:S(2)}) copy-start(bf16[512,768]{1,0:T(8,128)(2,1)} %cot.1) | copy-start | bytes 2359300
  29.1 9.4 %collective-permute-start.3 = (bf16[512,3072]{1,0:T(8,128)(2,1)S(1)}, bf16[512,3072]{1,0:T(8,128)(2,1)S(1)}, u32[]{:S(2)}, u32[]{:S(2)}) collective-permute-start(bf16[512,3072]{1,0:T(8,128)(2,1)S(1)} %get-tuple-element.146.a_own), channel_id=1, source_target_pairs={{0,2},{1,3},{2,0},{3,1},{4,6},{5,7},{6,4},{7,5},{8,10},{9,11},{10,... | collective-permute-start | bytes 9437192 | tf_op jit(solution)/shard_map/ppermute | solution.py:619
  29.1 9.3 %collective-permute-start.2 = (bf16[2,4,192,512]{3,2,1,0:T(8,128)(2,1)S(1)}, bf16[2,4,192,512]{3,2,1,0:T(8,128)(2,1)S(1)}, u32[]{:S(2)}, u32[]{:S(2)}) collective-permute-start(bf16[2,4,192,512]{3,2,1,0:T(8,128)(2,1)S(1)} %get-tuple-element.140.a_own.m_own), channel_id=1, source_target_pairs={{0,2},{1,3},{2,0},{3,1},{4,6},{5,7},{6,4},{7,5},{8,10},{9,11},{10,... | collective-permute-start | bytes 4718600 | tf_op jit(solution)/shard_map/ppermute | solution.py:619
  32.3 6.2 %collective-permute-start.4 = (bf16[512,384]{1,0:T(8,128)(2,1)S(1)}, bf16[512,384]{1,0:T(8,128)(2,1)S(1)}, u32[]{:S(2)}, u32[]{:S(2)}) collective-permute-start(bf16[512,384]{1,0:T(8,128)(2,1)S(1)} %get-tuple-element.148), channel_id=1, source_target_pairs={{0,2},{1,3},{2,0},{3,1},{4,6},{5,7},{6,4},{7,5},{8,10},{9,11},{10,... | collective-permute-start | bytes 1179656 | tf_op jit(solution)/shard_map/ppermute | solution.py:619
  37.9 18.1 %collective-permute-start.5 = (bf16[2,512,768]{2,1,0:T(8,128)(2,1)S(1)}, bf16[2,512,768]{2,1,0:T(8,128)(2,1)S(1)}, u32[]{:S(2)}, u32[]{:S(2)}) collective-permute-start(bf16[2,512,768]{2,1,0:T(8,128)(2,1)S(1)} %get-tuple-element.156), channel_id=1, source_target_pairs={{0,2},{1,3},{2,0},{3,1},{4,6},{5,7},{6,4},{7,5},{8,10},{9,11},{10,... | collective-permute-start | bytes 4718600 | tf_op jit(solution)/shard_map/ppermute | solution.py:619
  43.8 29.9 %collective-permute-start.8 = (bf16[2,2,2,2,96,384]{5,4,3,2,1,0:T(8,128)(2,1)S(1)}, bf16[2,2,2,2,96,384]{5,4,3,2,1,0:T(8,128)(2,1)S(1)}, u32[]{:S(2)}, u32[]{:S(2)}) collective-permute-start(bf16[2,2,2,2,96,384]{5,4,3,2,1,0:T(8,128)(2,1)S(1)} %get-tuple-element.149), channel_id=1, source_target_pairs={{0,8},{1,9},{2,10},{3,11},{4,12},{5,13},{6,14},{7,15},{8,0},{9,1},... | collective-permute-start | bytes 3538952 | tf_op jit(solution)/shard_map/ppermute | solution.py:619
  54.4 1.8 %collective-permute-start.6 = (bf16[512,384]{1,0:T(8,128)(2,1)S(1)}, bf16[512,384]{1,0:T(8,128)(2,1)S(1)}, u32[]{:S(2)}, u32[]{:S(2)}) collective-permute-start(bf16[512,384]{1,0:T(8,128)(2,1)S(1)} %get-tuple-element.158), channel_id=1, source_target_pairs={{0,2},{1,3},{2,0},{3,1},{4,6},{5,7},{6,4},{7,5},{8,10},{9,11},{10,... | collective-permute-start | bytes 1179656 | tf_op jit(solution)/shard_map/ppermute | solution.py:619
  54.5 8.0 %collective-permute-start.7 = (bf16[7,128,128]{2,1,0:T(8,128)(2,1)S(1)}, bf16[7,128,128]{2,1,0:T(8,128)(2,1)S(1)}, u32[]{:S(2)}, u32[]{:S(2)}) collective-permute-start(bf16[7,128,128]{2,1,0:T(8,128)(2,1)S(1)} %get-tuple-element.160), channel_id=1, source_target_pairs={{0,1},{1,0},{2,3},{3,2},{4,5},{5,4},{6,7},{7,6},{8,9},{9,8},{10,11... | collective-permute-start | bytes 688136 | tf_op jit(solution)/shard_map/ppermute | solution.py:619
  62.5 21.4 %collective-permute-start.9 = (bf16[2,4,120,384]{3,2,1,0:T(8,128)(2,1)S(1)}, bf16[2,4,120,384]{3,2,1,0:T(8,128)(2,1)S(1)}, u32[]{:S(2)}, u32[]{:S(2)}) collective-permute-start(bf16[2,4,120,384]{3,2,1,0:T(8,128)(2,1)S(1)} %get-tuple-element.174), channel_id=1, source_target_pairs={{0,1},{1,0},{2,3},{3,2},{4,5},{5,4},{6,7},{7,6},{8,9},{9,8},{10,11... | collective-permute-start | bytes 2211848 | tf_op jit(solution)/shard_map/ppermute | solution.py:619
  64.0 19.9 %collective-permute-start.10 = (bf16[2,4,120,384]{3,2,1,0:T(8,128)(2,1)S(1)}, bf16[2,4,120,384]{3,2,1,0:T(8,128)(2,1)S(1)}, u32[]{:S(2)}, u32[]{:S(2)}) collective-permute-start(bf16[2,4,120,384]{3,2,1,0:T(8,128)(2,1)S(1)} %get-tuple-element.177), channel_id=1, source_target_pairs={{0,4},{1,5},{2,6},{3,7},{4,0},{5,1},{6,2},{7,3},{8,12},{9,13},{10,... | collective-permute-start | bytes 2211848 | tf_op jit(solution)/shard_map/ppermute | solution.py:619
  73.1 13.0 %collective-permute-start.12 = (bf16[3,256,384]{2,1,0:T(8,128)(2,1)S(1)}, bf16[3,256,384]{2,1,0:T(8,128)(2,1)S(1)}, u32[]{:S(2)}, u32[]{:S(2)}) collective-permute-start(bf16[3,256,384]{2,1,0:T(8,128)(2,1)S(1)} %get-tuple-element.181.send_late), channel_id=1, source_target_pairs={{0,2},{1,3},{2,0},{3,1},{4,6},{5,7},{6,4},{7,5},{8,10},{9,11},{10,... | collective-permute-start | bytes 1769480 | tf_op jit(solution)/shard_map/ppermute | solution.py:619
  73.2 12.9 %collective-permute-start.11 = (bf16[3,256,384]{2,1,0:T(8,128)(2,1)S(1)}, bf16[3,256,384]{2,1,0:T(8,128)(2,1)S(1)}, u32[]{:S(2)}, u32[]{:S(2)}) collective-permute-start(bf16[3,256,384]{2,1,0:T(8,128)(2,1)S(1)} %get-tuple-element.164.send_early), channel_id=1, source_target_pairs={{0,2},{1,3},{2,0},{3,1},{4,6},{5,7},{6,4},{7,5},{8,10},{9,11},{10,... | collective-permute-start | bytes 1769480 | tf_op jit(solution)/shard_map/ppermute | solution.py:619
  74.5 28.8 %collective-permute-start.13 = (bf16[2,2,2,96,384]{4,3,2,1,0:T(8,128)(2,1)S(1)}, bf16[2,2,2,96,384]{4,3,2,1,0:T(8,128)(2,1)S(1)}, u32[]{:S(2)}, u32[]{:S(2)}) collective-permute-start(bf16[2,2,2,96,384]{4,3,2,1,0:T(8,128)(2,1)S(1)} %get-tuple-element.192), channel_id=1, source_target_pairs={{0,16},{1,17},{2,18},{3,19},{4,20},{5,21},{6,22},{7,23},{8,24},{9,... | collective-permute-start | bytes 1769480 | tf_op jit(solution)/shard_map/ppermute | solution.py:619
  84.7 19.3 %collective-permute-start.15 = (bf16[4,120,384]{2,1,0:T(8,128)(2,1)S(1)}, bf16[4,120,384]{2,1,0:T(8,128)(2,1)S(1)}, u32[]{:S(2)}, u32[]{:S(2)}) collective-permute-start(bf16[4,120,384]{2,1,0:T(8,128)(2,1)S(1)} %get-tuple-element.195), channel_id=1, source_target_pairs={{0,1},{1,0},{2,3},{3,2},{4,5},{5,4},{6,7},{7,6},{8,9},{9,8},{10,11... | collective-permute-start | bytes 1105928 | tf_op jit(solution)/shard_map/ppermute | solution.py:619
  85.3 18.8 %collective-permute-start.14 = (bf16[4,120,384]{2,1,0:T(8,128)(2,1)S(1)}, bf16[4,120,384]{2,1,0:T(8,128)(2,1)S(1)}, u32[]{:S(2)}, u32[]{:S(2)}) collective-permute-start(bf16[4,120,384]{2,1,0:T(8,128)(2,1)S(1)} %get-tuple-element.178), channel_id=1, source_target_pairs={{0,4},{1,5},{2,6},{3,7},{4,0},{5,1},{6,2},{7,3},{8,12},{9,13},{10,... | collective-permute-start | bytes 1105928 | tf_op jit(solution)/shard_map/ppermute | solution.py:619
  86.1 7.8 %copy-start.1 = (bf16[768,2304]{1,0:T(8,128)(2,1)S(1)}, bf16[768,2304]{1,0:T(8,128)(2,1)}, u32[]{:S(2)}) copy-start(bf16[768,2304]{1,0:T(8,128)(2,1)} %w_send.1) | copy-start | bytes 10616836
  91.2 14.6 %collective-permute-start.17 = (bf16[2,4,80,384]{3,2,1,0:T(8,128)(2,1)S(1)}, bf16[2,4,80,384]{3,2,1,0:T(8,128)(2,1)S(1)}, u32[]{:S(2)}, u32[]{:S(2)}) collective-permute-start(bf16[2,4,80,384]{3,2,1,0:T(8,128)(2,1)S(1)} %get-tuple-element.200), channel_id=1, source_target_pairs={{0,4},{1,5},{2,6},{3,7},{4,0},{5,1},{6,2},{7,3},{8,12},{9,13},{10,... | collective-permute-start | bytes 1474568 | tf_op jit(solution)/shard_map/ppermute | solution.py:619
  92.4 13.4 %collective-permute-start.16 = (bf16[2,4,80,384]{3,2,1,0:T(8,128)(2,1)S(1)}, bf16[2,4,80,384]{3,2,1,0:T(8,128)(2,1)S(1)}, u32[]{:S(2)}, u32[]{:S(2)}) collective-permute-start(bf16[2,4,80,384]{3,2,1,0:T(8,128)(2,1)S(1)} %get-tuple-element.188), channel_id=1, source_target_pairs={{0,1},{1,0},{2,3},{3,2},{4,5},{5,4},{6,7},{7,6},{8,9},{9,8},{10,11... | collective-permute-start | bytes 1474568 | tf_op jit(solution)/shard_map/ppermute | solution.py:619
  104.9 10.6 %collective-permute-start.18 = (bf16[2,2,120,384]{3,2,1,0:T(8,128)(2,1)S(1)}, bf16[2,2,120,384]{3,2,1,0:T(8,128)(2,1)S(1)}, u32[]{:S(2)}, u32[]{:S(2)}) collective-permute-start(bf16[2,2,120,384]{3,2,1,0:T(8,128)(2,1)S(1)} %get-tuple-element.203), channel_id=1, source_target_pairs={{0,8},{1,9},{2,10},{3,11},{4,12},{5,13},{6,14},{7,15},{8,0},{9,1},... | collective-permute-start | bytes 1105928 | tf_op jit(solution)/shard_map/ppermute | solution.py:619
  106.5 10.3 %collective-permute-start.20 = (bf16[4,80,384]{2,1,0:T(8,128)(2,1)S(1)}, bf16[4,80,384]{2,1,0:T(8,128)(2,1)S(1)}, u32[]{:S(2)}, u32[]{:S(2)}) collective-permute-start(bf16[4,80,384]{2,1,0:T(8,128)(2,1)S(1)} %get-tuple-element.206), channel_id=1, source_target_pairs={{0,1},{1,0},{2,3},{3,2},{4,5},{5,4},{6,7},{7,6},{8,9},{9,8},{10,11... | collective-permute-start | bytes 737288 | tf_op jit(solution)/shard_map/ppermute | solution.py:619
  108.0 8.8 %collective-permute-start.19 = (bf16[4,80,384]{2,1,0:T(8,128)(2,1)S(1)}, bf16[4,80,384]{2,1,0:T(8,128)(2,1)S(1)}, u32[]{:S(2)}, u32[]{:S(2)}) collective-permute-start(bf16[4,80,384]{2,1,0:T(8,128)(2,1)S(1)} %get-tuple-element.201), channel_id=1, source_target_pairs={{0,4},{1,5},{2,6},{3,7},{4,0},{5,1},{6,2},{7,3},{8,12},{9,13},{10,... | collective-permute-start | bytes 737288 | tf_op jit(solution)/shard_map/ppermute | solution.py:619
  108.5 9.0 %collective-permute-start.21 = (bf16[2,96,384]{2,1,0:T(8,128)(2,1)S(1)}, bf16[2,96,384]{2,1,0:T(8,128)(2,1)S(1)}, u32[]{:S(2)}, u32[]{:S(2)}) collective-permute-start(bf16[2,96,384]{2,1,0:T(8,128)(2,1)S(1)} %get-tuple-element.209), channel_id=1, source_target_pairs={{0,1},{1,0},{2,3},{3,2},{4,5},{5,4},{6,7},{7,6},{8,9},{9,8},{10,11... | collective-permute-start | bytes 442376 | tf_op jit(solution)/shard_map/ppermute | solution.py:619
  109.1 8.5 %collective-permute-start.22 = (bf16[2,96,384]{2,1,0:T(8,128)(2,1)S(1)}, bf16[2,96,384]{2,1,0:T(8,128)(2,1)S(1)}, u32[]{:S(2)}, u32[]{:S(2)}) collective-permute-start(bf16[2,96,384]{2,1,0:T(8,128)(2,1)S(1)} %get-tuple-element.211), channel_id=1, source_target_pairs={{0,4},{1,5},{2,6},{3,7},{4,0},{5,1},{6,2},{7,3},{8,12},{9,13},{10,... | collective-permute-start | bytes 442376 | tf_op jit(solution)/shard_map/ppermute | solution.py:619
  116.1 16.0 %collective-permute-start.23 = (bf16[2,120,384]{2,1,0:T(8,128)(2,1)S(1)}, bf16[2,120,384]{2,1,0:T(8,128)(2,1)S(1)}, u32[]{:S(2)}, u32[]{:S(2)}) collective-permute-start(bf16[2,120,384]{2,1,0:T(8,128)(2,1)S(1)} %get-tuple-element.214), channel_id=1, source_target_pairs={{0,16},{1,17},{2,18},{3,19},{4,20},{5,21},{6,22},{7,23},{8,24},{9,... | collective-permute-start | bytes 552968 | tf_op jit(solution)/shard_map/ppermute | solution.py:619
  118.1 15.1 %collective-permute-start.24 = (bf16[96,384]{1,0:T(8,128)(2,1)S(1)}, bf16[96,384]{1,0:T(8,128)(2,1)S(1)}, u32[]{:S(2)}, u32[]{:S(2)}) collective-permute-start(bf16[96,384]{1,0:T(8,128)(2,1)S(1)} %get-tuple-element.217), channel_id=1, source_target_pairs={{0,4},{1,5},{2,6},{3,7},{4,0},{5,1},{6,2},{7,3},{8,12},{9,13},{10,... | collective-permute-start | bytes 221192 | tf_op jit(solution)/shard_map/ppermute | solution.py:619
  118.6 18.6 %collective-permute-start.26 = (bf16[2,80,384]{2,1,0:T(8,128)(2,1)S(1)}, bf16[2,80,384]{2,1,0:T(8,128)(2,1)S(1)}, u32[]{:S(2)}, u32[]{:S(2)}) collective-permute-start(bf16[2,80,384]{2,1,0:T(8,128)(2,1)S(1)} %get-tuple-element.221), channel_id=1, source_target_pairs={{0,8},{1,9},{2,10},{3,11},{4,12},{5,13},{6,14},{7,15},{8,0},{9,1},... | collective-permute-start | bytes 368648 | tf_op jit(solution)/shard_map/ppermute | solution.py:619
  120.2 17.0 %collective-permute-start.27 = (bf16[2,80,384]{2,1,0:T(8,128)(2,1)S(1)}, bf16[2,80,384]{2,1,0:T(8,128)(2,1)S(1)}, u32[]{:S(2)}, u32[]{:S(2)}) collective-permute-start(bf16[2,80,384]{2,1,0:T(8,128)(2,1)S(1)} %get-tuple-element.222), channel_id=1, source_target_pairs={{0,16},{1,17},{2,18},{3,19},{4,20},{5,21},{6,22},{7,23},{8,24},{9,... | collective-permute-start | bytes 368648 | tf_op jit(solution)/shard_map/ppermute | solution.py:619
  121.4 15.8 %collective-permute-start.28 = (bf16[2,80,384]{2,1,0:T(8,128)(2,1)S(1)}, bf16[2,80,384]{2,1,0:T(8,128)(2,1)S(1)}, u32[]{:S(2)}, u32[]{:S(2)}) collective-permute-start(bf16[2,80,384]{2,1,0:T(8,128)(2,1)S(1)} %get-tuple-element.223), channel_id=1, source_target_pairs={{0,24},{1,25},{2,26},{3,27},{4,28},{5,29},{6,30},{7,31},{8,16},{9,... | collective-permute-start | bytes 368648 | tf_op jit(solution)/shard_map/ppermute | solution.py:619
  132.1 4.4 %collective-permute-start.25 = (bf16[96,384]{1,0:T(8,128)(2,1)S(1)}, bf16[96,384]{1,0:T(8,128)(2,1)S(1)}, u32[]{:S(2)}, u32[]{:S(2)}) collective-permute-start(bf16[96,384]{1,0:T(8,128)(2,1)S(1)} %get-tuple-element.218), channel_id=1, source_target_pairs={{0,1},{1,0},{2,3},{3,2},{4,5},{5,4},{6,7},{7,6},{8,9},{9,8},{10,11... | collective-permute-start | bytes 221192 | tf_op jit(solution)/shard_map/ppermute | solution.py:619
  133.3 6.0 %collective-permute-start.31 = (f32[120,384]{1,0:T(8,128)S(1)}, f32[120,384]{1,0:T(8,128)S(1)}, u32[]{:S(2)}, u32[]{:S(2)}) collective-permute-start(f32[120,384]{1,0:T(8,128)S(1)} %get-tuple-element.227), channel_id=1, source_target_pairs={{0,2},{1,3},{2,0},{3,1},{4,6},{5,7},{6,4},{7,5},{8,10},{9,11},{10,... | collective-permute-start | bytes 552968 | tf_op jit(solution)/shard_map/ppermute | solution.py:619
  137.1 2.2 %collective-permute-start.30 = (f32[96,384]{1,0:T(8,128)S(1)}, f32[96,384]{1,0:T(8,128)S(1)}, u32[]{:S(2)}, u32[]{:S(2)}) collective-permute-start(f32[96,384]{1,0:T(8,128)S(1)} %get-tuple-element.226), channel_id=1, source_target_pairs={{0,2},{1,3},{2,0},{3,1},{4,6},{5,7},{6,4},{7,5},{8,10},{9,11},{10,... | collective-permute-start | bytes 442376 | tf_op jit(solution)/shard_map/ppermute | solution.py:619
  137.8 1.5 %collective-permute-start.29 = (f32[80,384]{1,0:T(8,128)S(1)}, f32[80,384]{1,0:T(8,128)S(1)}, u32[]{:S(2)}, u32[]{:S(2)}) collective-permute-start(f32[80,384]{1,0:T(8,128)S(1)} %get-tuple-element.225), channel_id=1, source_target_pairs={{0,2},{1,3},{2,0},{3,1},{4,6},{5,7},{6,4},{7,5},{8,10},{9,11},{10,... | collective-permute-start | bytes 368648 | tf_op jit(solution)/shard_map/ppermute | solution.py:619
  (1 other events, 1.1 us)
